TPU v7x, 256 devices: a whole 4x4x8 slice. The times are simulated.
256 devices in a mesh: grp: 4 (over x), sub: 64 (over y, z, core).
Axes of the slice: x: 4, y: 4, z: 8, core: 2. Of those that a mesh axis runs over, the one named last changes fastest.
Arguments:
- blocks: bfloat16 [4, 64, 2048, 2048], P('grp', 'sub'), may hold values from -0.125 to 0.125
- own_vectors: bfloat16 [4, 64, 48, 2048], P('grp', 'sub'), may hold values from -0.890625 to 0.890625
- over_vectors: bfloat16 [4, 64, 8, 4, 48, 128], P('grp', 'sub'), may hold values from -0.890625 to 0.890625
- neighbours: int32 [4, 64, 8], P('grp', 'sub'), may hold values from -1 to 63, as said below
- counts: int32 [4, 64, 8], P('grp', 'sub'), may hold values from 0 to 4, as said below
- margin_rows: int32 [4, 64, 8, 4, 128], P('grp', 'sub'), may hold values from 0 to 2047, as said below
Outputs:
- coarse: float32 [4, 64, 48, 816], P(None, 'sub')
Inputs may be any that keep to these rules, and one draw needn't show every extreme that they name: `neighbours`: each entry is -1 or the number of a subdomain of the same group at distance 1 to 4 from the listing subdomain; no number twice in a list; the subdomains at distance 1 are always listed when they exist. `counts`: 0 exactly for empty slots, 1 or more for listed neighbours; a subdomain always sends 4 blocks to the subdomain after it. `margin_rows`: within one owner and offset, all 512 rows are distinct.
All inputs are finite; a program needn't handle non-finite values.
Results may differ from a plain program's by a relative error of at most 0.0029.
Values may be sent and summed in bfloat16 or wider, within the bound.
No kernel may reach another device: no remote copies, remote signals or barrier semaphores. Data moves between devices by JAX's collectives and lax.ppermute only.
A program may use at most 128 MiB of HBM per device.

v0:
```python
import jax
import jax.numpy as jnp
from jax import lax
from jax.sharding import PartitionSpec as P

H = 4


def from_behind(block, axis, distance):
    devices = range(lax.axis_size(axis))
    route = [(i - distance, i) for i in devices if i - distance in devices]
    return lax.ppermute(block, axis, route)


def place_rows(values, rows, width):
    vectors = values.shape[1]
    flat = jnp.transpose(values, (1, 0, 2)).reshape(vectors, -1)
    dense = jnp.zeros((vectors, width), jnp.bfloat16).at[:, rows.reshape(-1)].set(flat)
    return (dense, flat)


def on_device(blocks, own_vectors, over_vectors, neighbours, counts, margin_rows):
    device = lax.axis_index("sub")
    matrix = blocks[0, 0]
    width = matrix.shape[0]
    vectors = own_vectors.shape[2]
    span = 2 * H + 1
    tile_index = jnp.arange(over_vectors.shape[3], dtype=jnp.int32)
    live = (tile_index[None, :] < counts[0, 0][:, None]).astype(jnp.bfloat16)
    outgoing = over_vectors[0, 0] * live[:, :, None, None]
    listed = neighbours[0, 0]
    outward = {}
    for offset in range(-H, H + 1):
        if offset == 0:
            continue
        picked = (listed == device + offset).astype(jnp.float32)
        outward[offset] = jnp.einsum("n,ntkc->tkc", picked, outgoing.astype(jnp.float32)).astype(
            jnp.bfloat16
        )
    arriving = {}
    for offset in range(-H, H + 1):
        if offset == 0:
            continue
        arriving[-offset] = from_behind(outward[offset], "sub", offset)
    stacks = []
    sparse = {}
    for offset in range(-H, H + 1):
        if offset == 0:
            stacks.append(own_vectors[0, 0])
            continue
        slot = offset + H if offset < 0 else offset + H - 1
        rows = margin_rows[0, 0, slot]
        dense, flat = place_rows(arriving[offset], rows, width)
        stacks.append(dense)
        sparse[offset] = (flat, rows.reshape(-1))
    present = jnp.concatenate(stacks, axis=0)
    product = jnp.dot(present, matrix, preferred_element_type=jnp.float32).astype(jnp.bfloat16)
    gram = lax.dot_general(
        product, present, (((1,), (1,)), ((), ())), preferred_element_type=jnp.float32
    )
    row_blocks = gram.reshape(span, vectors, span * vectors)
    coarse = jnp.zeros((vectors, (4 * H + 1) * vectors), jnp.float32)
    for offset in range(-H, H + 1):
        if offset == 0:
            incoming = row_blocks[H]
        else:
            incoming = from_behind(row_blocks[offset + H], "sub", offset)
        start = (H - offset) * vectors
        coarse = coarse.at[:, start : start + span * vectors].add(incoming)
    return lax.all_gather(coarse[None, None], "grp", axis=0, tiled=True)


def solution(mesh):
    placed = (
        P("grp", "sub", None, None),
        P("grp", "sub", None, None),
        P("grp", "sub", None, None, None, None),
        P("grp", "sub", None),
        P("grp", "sub", None),
        P("grp", "sub", None, None, None),
    )
    return jax.shard_map(
        on_device, mesh=mesh, in_specs=placed, out_specs=P(None, "sub", None, None), check_vma=False
    )
```

profile of v0, /device:TPU:24, one launch (start us, length us, event | category | flops | bytes accessed | tf_op | source)
XLA Modules:
  0.0 131.1 jit_solution(4270144581982958765)
XLA Ops:
  0.0 0.7 fusion.41
  0.7 1.1 multiply_bitcast_fusion
  1.9 1.0 fusion.39
  3.0 5.2 %collective-permute-start = (bf16[4,48,128]{1,2,0:T(8,128)(2,1)S(1)}, bf16[4,48,128]{1,2,0:T(8,128)(2,1)S(1)}, u32[]{:S(2)}, u32[]{:S(2)}) collective-permute-start(bf16[4,48,128]{1,2,0:T(8,128)(2,1)S(1)} %bitcast.156), channel_id=1, source_target_pairs={{0,4},{1,5},{2,6},{3,7},{4,8},{5,9},{6,10},{7,11},{8,12},{9,13},{1... | collective-permute-start | bytes 147464 | tf_op jit(solution)/shard_map/ppermute | solution.py:12
  8.2 1.0 fusion.37
  9.3 3.0 %collective-permute-start.1 = (bf16[4,48,128]{1,2,0:T(8,128)(2,1)S(1)}, bf16[4,48,128]{1,2,0:T(8,128)(2,1)S(1)}, u32[]{:S(2)}, u32[]{:S(2)}) collective-permute-start(bf16[4,48,128]{1,2,0:T(8,128)(2,1)S(1)} %bitcast.157), channel_id=1, source_target_pairs={{0,3},{1,4},{2,5},{3,6},{4,7},{5,8},{6,9},{7,10},{8,11},{9,12},{10... | collective-permute-start | bytes 147464 | tf_op jit(solution)/shard_map/ppermute | solution.py:12
  12.8 5.0 %collective-permute-start.2 = (bf16[4,48,128]{1,2,0:T(8,128)(2,1)S(1)}, bf16[4,48,128]{1,2,0:T(8,128)(2,1)S(1)}, u32[]{:S(2)}, u32[]{:S(2)}) collective-permute-start(bf16[4,48,128]{1,2,0:T(8,128)(2,1)S(1)} %bitcast.158), channel_id=1, source_target_pairs={{0,2},{1,3},{2,4},{3,5},{4,6},{5,7},{6,8},{7,9},{8,10},{9,11},{10,... | collective-permute-start | bytes 147464 | tf_op jit(solution)/shard_map/ppermute | solution.py:12
  18.3 3.0 %collective-permute-start.3 = (bf16[4,48,128]{1,2,0:T(8,128)(2,1)S(1)}, bf16[4,48,128]{1,2,0:T(8,128)(2,1)S(1)}, u32[]{:S(2)}, u32[]{:S(2)}) collective-permute-start(bf16[4,48,128]{1,2,0:T(8,128)(2,1)S(1)} %bitcast.154), channel_id=1, source_target_pairs={{0,1},{1,2},{2,3},{3,4},{4,5},{5,6},{6,7},{7,8},{8,9},{9,10},{10,1... | collective-permute-start | bytes 147464 | tf_op jit(solution)/shard_map/ppermute | solution.py:12
  21.8 4.6 %collective-permute-start.4 = (bf16[4,48,128]{1,2,0:T(8,128)(2,1)S(1)}, bf16[4,48,128]{1,2,0:T(8,128)(2,1)S(1)}, u32[]{:S(2)}, u32[]{:S(2)}) collective-permute-start(bf16[4,48,128]{1,2,0:T(8,128)(2,1)S(1)} %bitcast.155), channel_id=1, source_target_pairs={{1,0},{2,1},{3,2},{4,3},{5,4},{6,5},{7,6},{8,7},{9,8},{10,9},{11,1... | collective-permute-start | bytes 147464 | tf_op jit(solution)/shard_map/ppermute | solution.py:12
  28.0 2.3 %collective-permute-start.5 = (bf16[4,48,128]{1,2,0:T(8,128)(2,1)S(1)}, bf16[4,48,128]{1,2,0:T(8,128)(2,1)S(1)}, u32[]{:S(2)}, u32[]{:S(2)}) collective-permute-start(bf16[4,48,128]{1,2,0:T(8,128)(2,1)S(1)} %bitcast.161), channel_id=1, source_target_pairs={{2,0},{3,1},{4,2},{5,3},{6,4},{7,5},{8,6},{9,7},{10,8},{11,9},{12,... | collective-permute-start | bytes 147464 | tf_op jit(solution)/shard_map/ppermute | solution.py:12
  30.4 1.9 %collective-permute-start.6 = (bf16[4,48,128]{1,2,0:T(8,128)(2,1)S(1)}, bf16[4,48,128]{1,2,0:T(8,128)(2,1)S(1)}, u32[]{:S(2)}, u32[]{:S(2)}) collective-permute-start(bf16[4,48,128]{1,2,0:T(8,128)(2,1)S(1)} %bitcast.160), channel_id=1, source_target_pairs={{3,0},{4,1},{5,2},{6,3},{7,4},{8,5},{9,6},{10,7},{11,8},{12,9},{13... | collective-permute-start | bytes 147464 | tf_op jit(solution)/shard_map/ppermute | solution.py:12
  32.3 3.3 %collective-permute-start.7 = (bf16[4,48,128]{1,2,0:T(8,128)(2,1)S(1)}, bf16[4,48,128]{1,2,0:T(8,128)(2,1)S(1)}, u32[]{:S(2)}, u32[]{:S(2)}) collective-permute-start(bf16[4,48,128]{1,2,0:T(8,128)(2,1)S(1)} %bitcast.159), channel_id=1, source_target_pairs={{4,0},{5,1},{6,2},{7,3},{8,4},{9,5},{10,6},{11,7},{12,8},{13,9},{1... | collective-permute-start | bytes 147464 | tf_op jit(solution)/shard_map/ppermute | solution.py:12
  35.9 1.9 %scatter_custom_fusion = bf16[48,2048]{0,1:T(8,128)(2,1)S(1)} fusion(s32[512]{0:T(512)S(1)} %bitcast.176, bf16[512,48]{1,0:T(8,128)(2,1)S(1)} %bitcast.179, bf16[]{:T(256)} %constant.243.clone.1), kind=kCustom, calls=%fused_computation.35 | custom fusion | bytes 196610 | tf_op jit(solution)/shard_map/scatter | solution.py:18
  37.8 2.6 %scatter_custom_fusion.1 = bf16[48,2048]{0,1:T(8,128)(2,1)} fusion(s32[512]{0:T(512)S(1)} %bitcast.175, bf16[512,48]{1,0:T(8,128)(2,1)S(1)} %bitcast.180, bf16[]{:T(256)} %constant.243.clone.1), kind=kCustom, calls=%fused_computation.33 | custom fusion | bytes 196610 | tf_op jit(solution)/shard_map/scatter | solution.py:18
  40.4 2.6 %scatter_custom_fusion.2 = bf16[48,2048]{0,1:T(8,128)(2,1)} fusion(s32[512]{0:T(512)S(1)} %bitcast.174, bf16[512,48]{1,0:T(8,128)(2,1)S(1)} %bitcast.181, bf16[]{:T(256)} %constant.243.clone.1), kind=kCustom, calls=%fused_computation.31 | custom fusion | bytes 196610 | tf_op jit(solution)/shard_map/scatter | solution.py:18
  43.0 2.6 %scatter_custom_fusion.3 = bf16[48,2048]{0,1:T(8,128)(2,1)} fusion(s32[512]{0:T(512)S(1)} %bitcast.172, bf16[512,48]{1,0:T(8,128)(2,1)S(1)} %bitcast.182, bf16[]{:T(256)} %constant.243.clone.1), kind=kCustom, calls=%fused_computation.29 | custom fusion | bytes 196610 | tf_op jit(solution)/shard_map/scatter | solution.py:18
  45.6 2.6 %scatter_custom_fusion.4 = bf16[48,2048]{0,1:T(8,128)(2,1)} fusion(s32[512]{0:T(512)S(1)} %bitcast.170, bf16[512,48]{1,0:T(8,128)(2,1)S(1)} %bitcast.183, bf16[]{:T(256)} %constant.243.clone.1), kind=kCustom, calls=%fused_computation.27 | custom fusion | bytes 196610 | tf_op jit(solution)/shard_map/scatter | solution.py:18
  48.2 2.6 %scatter_custom_fusion.5 = bf16[48,2048]{0,1:T(8,128)(2,1)} fusion(s32[512]{0:T(512)S(1)} %bitcast.171, bf16[512,48]{1,0:T(8,128)(2,1)S(1)} %bitcast.184, bf16[]{:T(256)} %constant.243.clone.1), kind=kCustom, calls=%fused_computation.25 | custom fusion | bytes 196610 | tf_op jit(solution)/shard_map/scatter | solution.py:18
  50.8 2.6 %scatter_custom_fusion.6 = bf16[48,2048]{0,1:T(8,128)(2,1)} fusion(s32[512]{0:T(512)S(1)} %bitcast.173, bf16[512,48]{1,0:T(8,128)(2,1)S(1)} %bitcast.185, bf16[]{:T(256)} %constant.243.clone.1), kind=kCustom, calls=%fused_computation.23 | custom fusion | bytes 196610 | tf_op jit(solution)/shard_map/scatter | solution.py:18
  53.4 2.6 %scatter_custom_fusion.7 = bf16[48,2048]{0,1:T(8,128)(2,1)} fusion(s32[512]{0:T(512)S(1)} %bitcast.177, bf16[512,48]{1,0:T(8,128)(2,1)S(1)} %bitcast.186, bf16[]{:T(256)} %constant.243.clone.1), kind=kCustom, calls=%fused_computation.21 | custom fusion | bytes 196610 | tf_op jit(solution)/shard_map/scatter | solution.py:18
  56.0 6.1 %concatenate.21 = bf16[432,2048]{0,1:T(8,128)(2,1)S(1)} concatenate(bf16[48,2048]{0,1:T(8,128)(2,1)S(1)} %scatter_custom_fusion, bf16[48,2048]{0,1:T(8,128)(2,1)} %scatter_custom_fusion.1, bf16[48,2048]{0,1:T(8,128)(2,1)} %scatter_custom_fusion.2, bf16[48,2048]{0,1:T(8,128)(2,1)} %scatter_custom_fusion.3, bf16[48,2048]{0,1:T(8,128)(2,1)S(1)} %bitcast.153, ...), dimensions={0} | concatenate | bytes 3538944 | tf_op jit(solution)/shard_map/concatenate | solution.py:56
  62.1 8.2 %fusion.6 = f32[432,432]{1,0:T(8,128)S(1)} fusion(bf16[432,2048]{0,1:T(8,128)(2,1)S(1)} %concatenate.21, bf16[1,1,2048,2048]{3,2,1,0:T(8,128)(2,1)} %param.24), kind=kOutput, calls=%fused_computation.11 | convolution fusion | flops 4389175296 | bytes 10904576 | tf_op jit(solution)/shard_map/dot_general | solution.py:58
  70.3 4.0 %collective-permute-start.8 = (f32[48,432]{1,0:T(8,128)S(1)}, f32[48,432]{1,0:T(8,128)S(1)}, u32[]{:S(2)}, u32[]{:S(2)}) collective-permute-start(f32[48,432]{1,0:T(8,128)S(1)} %get-tuple-element.121), channel_id=1, source_target_pairs={{4,0},{5,1},{6,2},{7,3},{8,4},{9,5},{10,6},{11,7},{12,8},{13,9},{1... | collective-permute-start | bytes 248840 | tf_op jit(solution)/shard_map/ppermute | solution.py:12
  74.4 5.0 %collective-permute-start.9 = (f32[48,432]{1,0:T(8,128)S(1)}, f32[48,432]{1,0:T(8,128)S(1)}, u32[]{:S(2)}, u32[]{:S(2)}) collective-permute-start(f32[48,432]{1,0:T(8,128)S(1)} %get-tuple-element.120), channel_id=1, source_target_pairs={{3,0},{4,1},{5,2},{6,3},{7,4},{8,5},{9,6},{10,7},{11,8},{12,9},{13... | collective-permute-start | bytes 248840 | tf_op jit(solution)/shard_map/ppermute | solution.py:12
  82.0 2.3 %collective-permute-start.10 = (f32[48,432]{1,0:T(8,128)S(1)}, f32[48,432]{1,0:T(8,128)S(1)}, u32[]{:S(2)}, u32[]{:S(2)}) collective-permute-start(f32[48,432]{1,0:T(8,128)S(1)} %get-tuple-element.119), channel_id=1, source_target_pairs={{2,0},{3,1},{4,2},{5,3},{6,4},{7,5},{8,6},{9,7},{10,8},{11,9},{12,... | collective-permute-start | bytes 248840 | tf_op jit(solution)/shard_map/ppermute | solution.py:12
  84.3 2.4 %collective-permute-start.11 = (f32[48,432]{1,0:T(8,128)S(1)}, f32[48,432]{1,0:T(8,128)S(1)}, u32[]{:S(2)}, u32[]{:S(2)}) collective-permute-start(f32[48,432]{1,0:T(8,128)S(1)} %get-tuple-element.118), channel_id=1, source_target_pairs={{1,0},{2,1},{3,2},{4,3},{5,4},{6,5},{7,6},{8,7},{9,8},{10,9},{11,1... | collective-permute-start | bytes 248840 | tf_op jit(solution)/shard_map/ppermute | solution.py:12
  86.7 0.7 add_select_fusion.7
  87.5 0.9 scatter-add.31
  88.5 0.8 add_select_fusion.6
  89.2 0.9 scatter-add.34
  90.9 1.0 scatter-add.35
  91.8 1.7 %fusion.66 = (f32[48,432]{1,0:T(8,128)S(1)}, f32[48,432]{1,0:T(8,128)S(1)}, f32[48,432]{1,0:T(8,128)S(1)}, f32[48,432]{1,0:T(8,128)S(1)}, f32[48,432]{1,0:T(8,128)S(1)}) fusion(f32[432,432]{1,0:T(8,128)} %copy-done, f32[48,816]{1,0:T(8,128)S(1)} %scatter-add.35, pred[]{:T(512)} %compare_reduce_fusion.4), kind=kLoop, calls=%fused_computation.105 | loop fusion | flops 41472 | bytes 912385 | tf_op jit(solution)/shard_map/slice | solution.py:67
  93.6 2.5 %collective-permute-start.12 = (f32[48,432]{1,0:T(8,128)S(1)}, f32[48,432]{1,0:T(8,128)S(1)}, u32[]{:S(2)}, u32[]{:S(2)}) collective-permute-start(f32[48,432]{1,0:T(8,128)S(1)} %get-tuple-element.116), channel_id=1, source_target_pairs={{0,1},{1,2},{2,3},{3,4},{4,5},{5,6},{6,7},{7,8},{8,9},{9,10},{10,1... | collective-permute-start | bytes 248840 | tf_op jit(solution)/shard_map/ppermute | solution.py:12
  96.0 0.7 compare_reduce_fusion
  98.7 2.9 %collective-permute-start.13 = (f32[48,432]{1,0:T(8,128)S(1)}, f32[48,432]{1,0:T(8,128)S(1)}, u32[]{:S(2)}, u32[]{:S(2)}) collective-permute-start(f32[48,432]{1,0:T(8,128)S(1)} %get-tuple-element.115), channel_id=1, source_target_pairs={{0,2},{1,3},{2,4},{3,5},{4,6},{5,7},{6,8},{7,9},{8,10},{9,11},{10,... | collective-permute-start | bytes 248840 | tf_op jit(solution)/shard_map/ppermute | solution.py:12
  101.6 1.9 %collective-permute-start.14 = (f32[48,432]{1,0:T(8,128)S(1)}, f32[48,432]{1,0:T(8,128)S(1)}, u32[]{:S(2)}, u32[]{:S(2)}) collective-permute-start(f32[48,432]{1,0:T(8,128)S(1)} %get-tuple-element.114), channel_id=1, source_target_pairs={{0,3},{1,4},{2,5},{3,6},{4,7},{5,8},{6,9},{7,10},{8,11},{9,12},{10... | collective-permute-start | bytes 248840 | tf_op jit(solution)/shard_map/ppermute | solution.py:12
  103.5 3.2 %collective-permute-start.15 = (f32[48,432]{1,0:T(8,128)S(1)}, f32[48,432]{1,0:T(8,128)S(1)}, u32[]{:S(2)}, u32[]{:S(2)}) collective-permute-start(f32[48,432]{1,0:T(8,128)S(1)} %get-tuple-element.113), channel_id=1, source_target_pairs={{0,4},{1,5},{2,6},{3,7},{4,8},{5,9},{6,10},{7,11},{8,12},{9,13},{1... | collective-permute-start | bytes 248840 | tf_op jit(solution)/shard_map/ppermute | solution.py:12
  106.8 1.0 scatter-add.36
  107.8 0.7 add_select_fusion.3
  108.5 1.0 scatter-add.39
  110.1 1.0 scatter-add.40
  111.6 0.7 add_select_fusion.1
  112.3 1.0 scatter-add.41
  113.4 1.9 %collective-permute-done.15 = f32[48,432]{1,0:T(8,128)S(1)} collective-permute-done((f32[48,432]{1,0:T(8,128)S(1)}, f32[48,432]{1,0:T(8,128)S(1)}, u32[]{:S(2)}, u32[]{:S(2)}) %collective-permute-start.15) | collective-permute-done | bytes 82976 | tf_op jit(solution)/shard_map/ppermute | solution.py:12
  115.2 0.7 fusion.24
  115.9 0.9 scatter-add.44
  116.8 13.5 %all_gather.3 = f32[4,1,48,816]{3,2,1,0:T(8,128)S(1)} all-gather(f32[1,1,48,816]{3,2,1,0:T(8,128)S(1)} %scatter-add.44), channel_id=1, replica_groups=mesh['grp'=4,'sub'=64] {'grp'}, dimensions={0}, use_global_device_ids=true | all-gather | bytes 783360 | tf_op jit(solution)/shard_map/all_gather | solution.py:70
  130.2 0.8 copy.51
  (58 shorter events, 9.9 us)
Async XLA Ops:
  0.0 12.3 %copy-start.2 = (s32[1,1,8]{2,1,0:T(1,128)S(1)}, s32[1,1,8]{2,1,0:T(1,128)}, u32[]{:S(2)}) copy-start(s32[1,1,8]{2,1,0:T(1,128)} %param.27) | copy-start | bytes 100
  0.7 25.7 %copy-start.3 = (s32[1,1,8,4,128]{4,3,2,1,0:T(4,128)S(1)}, s32[1,1,8,4,128]{4,3,2,1,0:T(4,128)}, u32[]{:S(2)}) copy-start(s32[1,1,8,4,128]{4,3,2,1,0:T(4,128)} %param.29) | copy-start | bytes 49156
  3.0 25.0 %collective-permute-start = (bf16[4,48,128]{1,2,0:T(8,128)(2,1)S(1)}, bf16[4,48,128]{1,2,0:T(8,128)(2,1)S(1)}, u32[]{:S(2)}, u32[]{:S(2)}) collective-permute-start(bf16[4,48,128]{1,2,0:T(8,128)(2,1)S(1)} %bitcast.156), channel_id=1, source_target_pairs={{0,4},{1,5},{2,6},{3,7},{4,8},{5,9},{6,10},{7,11},{8,12},{9,13},{1... | collective-permute-start | bytes 147464 | tf_op jit(solution)/shard_map/ppermute | solution.py:12
  9.3 21.0 %collective-permute-start.1 = (bf16[4,48,128]{1,2,0:T(8,128)(2,1)S(1)}, bf16[4,48,128]{1,2,0:T(8,128)(2,1)S(1)}, u32[]{:S(2)}, u32[]{:S(2)}) collective-permute-start(bf16[4,48,128]{1,2,0:T(8,128)(2,1)S(1)} %bitcast.157), channel_id=1, source_target_pairs={{0,3},{1,4},{2,5},{3,6},{4,7},{5,8},{6,9},{7,10},{8,11},{9,12},{10... | collective-permute-start | bytes 147464 | tf_op jit(solution)/shard_map/ppermute | solution.py:12
  12.6 23.0 %copy-start.1 = (bf16[1,1,48,2048]{3,2,1,0:T(8,128)(2,1)S(1)}, bf16[1,1,48,2048]{3,2,1,0:T(8,128)(2,1)}, u32[]{:S(2)}) copy-start(bf16[1,1,48,2048]{3,2,1,0:T(8,128)(2,1)} %param.25) | copy-start | bytes 589828
  12.8 19.5 %collective-permute-start.2 = (bf16[4,48,128]{1,2,0:T(8,128)(2,1)S(1)}, bf16[4,48,128]{1,2,0:T(8,128)(2,1)S(1)}, u32[]{:S(2)}, u32[]{:S(2)}) collective-permute-start(bf16[4,48,128]{1,2,0:T(8,128)(2,1)S(1)} %bitcast.158), channel_id=1, source_target_pairs={{0,2},{1,3},{2,4},{3,5},{4,6},{5,7},{6,8},{7,9},{8,10},{9,11},{10,... | collective-permute-start | bytes 147464 | tf_op jit(solution)/shard_map/ppermute | solution.py:12
  18.3 24.7 %collective-permute-start.3 = (bf16[4,48,128]{1,2,0:T(8,128)(2,1)S(1)}, bf16[4,48,128]{1,2,0:T(8,128)(2,1)S(1)}, u32[]{:S(2)}, u32[]{:S(2)}) collective-permute-start(bf16[4,48,128]{1,2,0:T(8,128)(2,1)S(1)} %bitcast.154), channel_id=1, source_target_pairs={{0,1},{1,2},{2,3},{3,4},{4,5},{5,6},{6,7},{7,8},{8,9},{9,10},{10,1... | collective-permute-start | bytes 147464 | tf_op jit(solution)/shard_map/ppermute | solution.py:12
  21.8 23.8 %collective-permute-start.4 = (bf16[4,48,128]{1,2,0:T(8,128)(2,1)S(1)}, bf16[4,48,128]{1,2,0:T(8,128)(2,1)S(1)}, u32[]{:S(2)}, u32[]{:S(2)}) collective-permute-start(bf16[4,48,128]{1,2,0:T(8,128)(2,1)S(1)} %bitcast.155), channel_id=1, source_target_pairs={{1,0},{2,1},{3,2},{4,3},{5,4},{6,5},{7,6},{8,7},{9,8},{10,9},{11,1... | collective-permute-start | bytes 147464 | tf_op jit(solution)/shard_map/ppermute | solution.py:12
  28.0 20.2 %collective-permute-start.5 = (bf16[4,48,128]{1,2,0:T(8,128)(2,1)S(1)}, bf16[4,48,128]{1,2,0:T(8,128)(2,1)S(1)}, u32[]{:S(2)}, u32[]{:S(2)}) collective-permute-start(bf16[4,48,128]{1,2,0:T(8,128)(2,1)S(1)} %bitcast.161), channel_id=1, source_target_pairs={{2,0},{3,1},{4,2},{5,3},{6,4},{7,5},{8,6},{9,7},{10,8},{11,9},{12,... | collective-permute-start | bytes 147464 | tf_op jit(solution)/shard_map/ppermute | solution.py:12
  30.4 20.5 %collective-permute-start.6 = (bf16[4,48,128]{1,2,0:T(8,128)(2,1)S(1)}, bf16[4,48,128]{1,2,0:T(8,128)(2,1)S(1)}, u32[]{:S(2)}, u32[]{:S(2)}) collective-permute-start(bf16[4,48,128]{1,2,0:T(8,128)(2,1)S(1)} %bitcast.160), channel_id=1, source_target_pairs={{3,0},{4,1},{5,2},{6,3},{7,4},{8,5},{9,6},{10,7},{11,8},{12,9},{13... | collective-permute-start | bytes 147464 | tf_op jit(solution)/shard_map/ppermute | solution.py:12
  32.3 21.1 %collective-permute-start.7 = (bf16[4,48,128]{1,2,0:T(8,128)(2,1)S(1)}, bf16[4,48,128]{1,2,0:T(8,128)(2,1)S(1)}, u32[]{:S(2)}, u32[]{:S(2)}) collective-permute-start(bf16[4,48,128]{1,2,0:T(8,128)(2,1)S(1)} %bitcast.159), channel_id=1, source_target_pairs={{4,0},{5,1},{6,2},{7,3},{8,4},{9,5},{10,6},{11,7},{12,8},{13,9},{1... | collective-permute-start | bytes 147464 | tf_op jit(solution)/shard_map/ppermute | solution.py:12
  70.3 16.4 %copy-start = (f32[432,432]{1,0:T(8,128)}, f32[432,432]{1,0:T(8,128)S(1)}, u32[]{:S(2)}) copy-start(f32[432,432]{1,0:T(8,128)S(1)} %fusion.6) | copy-start | bytes 2239492
  70.3 16.3 %collective-permute-start.8 = (f32[48,432]{1,0:T(8,128)S(1)}, f32[48,432]{1,0:T(8,128)S(1)}, u32[]{:S(2)}, u32[]{:S(2)}) collective-permute-start(f32[48,432]{1,0:T(8,128)S(1)} %get-tuple-element.121), channel_id=1, source_target_pairs={{4,0},{5,1},{6,2},{7,3},{8,4},{9,5},{10,6},{11,7},{12,8},{13,9},{1... | collective-permute-start | bytes 248840 | tf_op jit(solution)/shard_map/ppermute | solution.py:12
  74.4 12.3 %collective-permute-start.9 = (f32[48,432]{1,0:T(8,128)S(1)}, f32[48,432]{1,0:T(8,128)S(1)}, u32[]{:S(2)}, u32[]{:S(2)}) collective-permute-start(f32[48,432]{1,0:T(8,128)S(1)} %get-tuple-element.120), channel_id=1, source_target_pairs={{3,0},{4,1},{5,2},{6,3},{7,4},{8,5},{9,6},{10,7},{11,8},{12,9},{13... | collective-permute-start | bytes 248840 | tf_op jit(solution)/shard_map/ppermute | solution.py:12
  82.0 6.5 %collective-permute-start.10 = (f32[48,432]{1,0:T(8,128)S(1)}, f32[48,432]{1,0:T(8,128)S(1)}, u32[]{:S(2)}, u32[]{:S(2)}) collective-permute-start(f32[48,432]{1,0:T(8,128)S(1)} %get-tuple-element.119), channel_id=1, source_target_pairs={{2,0},{3,1},{4,2},{5,3},{6,4},{7,5},{8,6},{9,7},{10,8},{11,9},{12,... | collective-permute-start | bytes 248840 | tf_op jit(solution)/shard_map/ppermute | solution.py:12
  84.3 5.9 %collective-permute-start.11 = (f32[48,432]{1,0:T(8,128)S(1)}, f32[48,432]{1,0:T(8,128)S(1)}, u32[]{:S(2)}, u32[]{:S(2)}) collective-permute-start(f32[48,432]{1,0:T(8,128)S(1)} %get-tuple-element.118), channel_id=1, source_target_pairs={{1,0},{2,1},{3,2},{4,3},{5,4},{6,5},{7,6},{8,7},{9,8},{10,9},{11,1... | collective-permute-start | bytes 248840 | tf_op jit(solution)/shard_map/ppermute | solution.py:12
  93.6 14.2 %collective-permute-start.12 = (f32[48,432]{1,0:T(8,128)S(1)}, f32[48,432]{1,0:T(8,128)S(1)}, u32[]{:S(2)}, u32[]{:S(2)}) collective-permute-start(f32[48,432]{1,0:T(8,128)S(1)} %get-tuple-element.116), channel_id=1, source_target_pairs={{0,1},{1,2},{2,3},{3,4},{4,5},{5,6},{6,7},{7,8},{8,9},{9,10},{10,1... | collective-permute-start | bytes 248840 | tf_op jit(solution)/shard_map/ppermute | solution.py:12
  98.7 10.8 %collective-permute-start.13 = (f32[48,432]{1,0:T(8,128)S(1)}, f32[48,432]{1,0:T(8,128)S(1)}, u32[]{:S(2)}, u32[]{:S(2)}) collective-permute-start(f32[48,432]{1,0:T(8,128)S(1)} %get-tuple-element.115), channel_id=1, source_target_pairs={{0,2},{1,3},{2,4},{3,5},{4,6},{5,7},{6,8},{7,9},{8,10},{9,11},{10,... | collective-permute-start | bytes 248840 | tf_op jit(solution)/shard_map/ppermute | solution.py:12
  101.6 10.0 %collective-permute-start.14 = (f32[48,432]{1,0:T(8,128)S(1)}, f32[48,432]{1,0:T(8,128)S(1)}, u32[]{:S(2)}, u32[]{:S(2)}) collective-permute-start(f32[48,432]{1,0:T(8,128)S(1)} %get-tuple-element.114), channel_id=1, source_target_pairs={{0,3},{1,4},{2,5},{3,6},{4,7},{5,8},{6,9},{7,10},{8,11},{9,12},{10... | collective-permute-start | bytes 248840 | tf_op jit(solution)/shard_map/ppermute | solution.py:12
  103.5 11.7 %collective-permute-start.15 = (f32[48,432]{1,0:T(8,128)S(1)}, f32[48,432]{1,0:T(8,128)S(1)}, u32[]{:S(2)}, u32[]{:S(2)}) collective-permute-start(f32[48,432]{1,0:T(8,128)S(1)} %get-tuple-element.113), channel_id=1, source_target_pairs={{0,4},{1,5},{2,6},{3,7},{4,8},{5,9},{6,10},{7,11},{8,12},{9,13},{1... | collective-permute-start | bytes 248840 | tf_op jit(solution)/shard_map/ppermute | solution.py:12
where the time goes:
time: 133 us; the launch traced here: 131 us
  starting transfers between devices  52.6 us (40%)
  local copies, waits for them, and re-layouts  36 us (27%)
  other arithmetic  13.9 us (10%)
  blocking collectives  13.5 us (10%)
  matrix products  12.1 us (9%)
  waiting for transfers between devices  2.42 us (2%)
    ppermute x16, starting transfers between devices, from_behind(): return lax.ppermute(block, axis, route)  52.6 us
    scatter x8, local copies, waits for them, and re-layouts, place_rows(): jnp.zeros((vectors, width), jnp.bfloat16).at[:, rows.reshape(-1)].set(flat)  20.1 us
    all_gather x1, blocking collectives, on_device(): return lax.all_gather(coarse[None, None], 'grp', axis=0, tiled=True)  13.5 us
    another operation x14, other arithmetic  9.59 us
    dot_general x1, matrix products, on_device(): lax.dot_general(product, present, (((1,), (1,)), ((), ())), preferred_ele...  8.16 us
    scatter-add x9, local copies, waits for them, and re-layouts, on_device(): coarse = coarse.at[:, start:start + span * vectors].add(incoming)  7.58 us
    concatenate x1, local copies, waits for them, and re-layouts, on_device(): present = jnp.concatenate(stacks, axis=0)  6.11 us
    dot_general x8, matrix products, on_device(): jnp.einsum('n,ntkc->tkc', picked, outgoing.astype(jnp.float32))  3.93 us
  transfers between devices with their start and end apart: 16, of which 3 were waited for; matrix products, arithmetic and copies ran while one was open for 28% of the time, Pallas kernels for 0%

commit v1 on v0

v1 whole, which is shorter than its diff:
```python
import jax
import jax.numpy as jnp
from jax import lax
from jax.experimental import pallas as pl
from jax.experimental.pallas import tpu as pltpu
from jax.sharding import PartitionSpec as P

H = 4
SPAN = 2 * H + 1
WIDE = SPAN + 1
FULL = 4 * H + 1
STACK = (0, 1, 2, 3, 4, -1, -2, -3, -4)
VMEM = pl.BlockSpec(memory_space=pltpu.VMEM)
SMEM = pl.BlockSpec(memory_space=pltpu.SMEM)


def partner_swap(block):
    return lax.ppermute(block, "sub", [(i, i ^ 1) for i in range(lax.axis_size("sub"))])


def stream(block, chips):
    count = lax.axis_size("sub")
    route = []
    for i in range(count):
        target = i + 2 * chips if i % 2 == 0 else i - 2 * chips
        route.append((i, target if 0 <= target < count else i ^ 1))
    return lax.ppermute(block, "sub", route)


def pick_kernel(place_ref, listed_ref, counts_ref, over_ref, swap_ref, keep_ref):
    me = place_ref[0]
    sign = place_ref[2]
    slots, tiles = over_ref.shape[0], over_ref.shape[1]

    def pick(k, out_ref, at):
        target = me + sign * k
        slot = jnp.int32(0)
        amount = jnp.int32(0)
        for n in range(slots):
            hit = listed_ref[n] == target
            slot = jnp.where(hit, n, slot)
            amount = jnp.where(hit, counts_ref[n], amount)
        for t in range(tiles):
            live = (t < amount).astype(jnp.bfloat16)
            out_ref[at, t] = over_ref[slot, t] * live

    for at, k in enumerate((1, -1, -2, -3, -4)):
        pick(k, swap_ref, at)
    for at, k in enumerate((2, 3, 4)):
        pick(k, keep_ref, at)


def gram_kernel(
    place_ref, rows_ref, own_ref, swap_ref, one_ref, two_ref, post_ref, matrix_ref,
    home_ref, ahead_ref, back_ref, left, right, acc,
):
    step = pl.program_id(0)
    vectors, width = own_ref.shape
    tiles, lanes = rows_ref.shape[1], rows_ref.shape[2]
    part = 256
    core, sign = place_ref[1], place_ref[2]

    def position(k):
        return jnp.where(core == 0, H + k, H + 1 - k)

    def right_rows(k):
        return pl.ds(pl.multiple_of(position(k) * vectors, vectors), vectors)

    @pl.when(step == 0)
    def _():
        left[0:vectors] = own_ref[...]
        right[right_rows(0)] = own_ref[...]
        right[right_rows(H + 1)] = jnp.zeros((vectors, width), jnp.bfloat16)
        sources = {
            1: (swap_ref, 0), 2: (post_ref, 1), 3: (post_ref, 0), 4: (post_ref, 2),
            -1: (one_ref, 1), -2: (one_ref, 0), -3: (two_ref, 1), -4: (two_ref, 0),
        }
        for at, k in enumerate(STACK):
            if k == 0:
                continue
            offset = sign * k
            slot = jnp.where(offset < 0, offset + H, offset + H - 1)
            source, which = sources[k]
            chosen = rows_ref[slot]
            low = chosen % part
            high = chosen // part
            index = lax.broadcasted_iota(jnp.int32, (part, lanes), 0)
            hot = jnp.concatenate(
                [
                    jnp.where(index == low[t : t + 1], 1.0, 0.0).astype(jnp.bfloat16)
                    for t in range(tiles)
                ],
                axis=1,
            )
            values = [source[which, t] for t in range(tiles)]
            spread = jnp.concatenate(
                [
                    jnp.concatenate(
                        [
                            values[t] * jnp.where(high[t : t + 1] == h, 1.0, 0.0).astype(jnp.bfloat16)
                            for t in range(tiles)
                        ],
                        axis=1,
                    )
                    for h in range(width // part)
                ],
                axis=0,
            )
            dense = lax.dot_general(
                spread, hot, (((1,), (1,)), ((), ())), preferred_element_type=jnp.float32
            ).astype(jnp.bfloat16)
            for h in range(width // part):
                block = dense[h * vectors : (h + 1) * vectors]
                left[at * vectors : (at + 1) * vectors, h * part : (h + 1) * part] = block
                right[right_rows(k), h * part : (h + 1) * part] = block

    product = jnp.dot(left[...], matrix_ref[...], preferred_element_type=jnp.float32).astype(
        jnp.bfloat16
    )
    columns = matrix_ref.shape[1]
    across = right[:, pl.ds(pl.multiple_of(step * columns, columns), columns)]
    term = lax.dot_general(
        product, across, (((1,), (1,)), ((), ())), preferred_element_type=jnp.float32
    )

    @pl.when(step == 0)
    def _():
        acc[...] = term

    @pl.when(step > 0)
    def _():
        acc[...] += term

    @pl.when(step == pl.num_programs(0) - 1)
    def _():
        for at in range(2):
            home_ref[at] = acc[at * vectors : (at + 1) * vectors]
        for at in range(3):
            ahead_ref[at] = acc[(2 + at) * vectors : (3 + at) * vectors]
        for at in range(4):
            back_ref[at] = acc[(5 + at) * vectors : (6 + at) * vectors].astype(jnp.bfloat16)


def window_kernel(place_ref, home_ref, one_ref, two_ref, near_ref, far_ref):
    core = place_ref[1]
    vectors = home_ref.shape[1]
    blocks = FULL

    def window(terms):
        total = None
        for value, start in terms:
            value = value.astype(jnp.float32)
            if start < 0:
                value = value[:, -start * vectors :]
                start = 0
            if start + value.shape[1] // vectors > blocks:
                value = value[:, : (blocks - start) * vectors]
            after = blocks * vectors - start * vectors - value.shape[1]
            value = jnp.pad(value, ((0, 0), (start * vectors, after)))
            total = value if total is None else total + value
        return total

    for c in range(2):
        way = 1 - 2 * c

        @pl.when(core == c)
        def _():
            for ref, at, row in ((near_ref, 0, c), (far_ref, 1, 1 - c)):
                ref[...] = window(
                    [
                        (home_ref[at], H - row),
                        (one_ref[at], H - 2 * way - row),
                        (two_ref[at], H - 4 * way - row),
                    ]
                )


def spread_kernel(place_ref, own_ref, up_ref, down_ref, far_ref, out_ref):
    x = place_ref[3]
    count = out_ref.shape[0]
    out_ref[x] = own_ref[...].astype(jnp.float32)
    out_ref[lax.rem(x + count - 1, count)] = up_ref[...].astype(jnp.float32)
    out_ref[lax.rem(x + 1, count)] = down_ref[...].astype(jnp.float32)
    out_ref[lax.rem(x + 2, count)] = far_ref[...].astype(jnp.float32)


def ring(block, distance):
    count = lax.axis_size("grp")
    return lax.ppermute(block, "grp", [(i, (i + distance) % count) for i in range(count)])


def on_device(blocks, own_vectors, over_vectors, neighbours, counts, margin_rows):
    device = lax.axis_index("sub")
    core = device % 2
    place = jnp.stack([device, core, 1 - 2 * core, lax.axis_index("grp")]).astype(jnp.int32)
    matrix = blocks[0, 0]
    width = matrix.shape[0]
    vectors = own_vectors.shape[2]
    over = over_vectors[0, 0]
    message = over.shape[1:]
    shape = jax.ShapeDtypeStruct

    give, keep = pl.pallas_call(
        pick_kernel,
        out_shape=(shape((5,) + message, jnp.bfloat16), shape((3,) + message, jnp.bfloat16)),
        in_specs=[SMEM, SMEM, SMEM, VMEM],
        out_specs=(VMEM, VMEM),
        name="pick",
    )(place, neighbours[0, 0], counts[0, 0], over)
    swap = partner_swap(give)
    two = stream(jnp.stack([keep[2], swap[3], swap[4]]), 2)
    one = stream(jnp.stack([keep[0], swap[1], keep[1], swap[2]]), 1)
    post = partner_swap(jnp.concatenate([one[2:4], two[2:3]]))

    columns = 256
    steps = width // columns
    whole = lambda *dims: pl.BlockSpec(dims, lambda i: (0,) * len(dims))
    home, ahead, back = pl.pallas_call(
        gram_kernel,
        grid=(steps,),
        out_shape=(
            shape((2, vectors, WIDE * vectors), jnp.float32),
            shape((3, vectors, WIDE * vectors), jnp.float32),
            shape((4, vectors, WIDE * vectors), jnp.bfloat16),
        ),
        in_specs=[
            SMEM,
            whole(*margin_rows.shape[2:]),
            whole(vectors, width),
            whole(*swap.shape),
            whole(*one.shape),
            whole(*two.shape),
            whole(*post.shape),
            pl.BlockSpec((width, columns), lambda i: (0, i)),
        ],
        out_specs=(
            whole(2, vectors, WIDE * vectors),
            whole(3, vectors, WIDE * vectors),
            whole(4, vectors, WIDE * vectors),
        ),
        scratch_shapes=[
            pltpu.VMEM((SPAN * vectors, width), jnp.bfloat16),
            pltpu.VMEM((WIDE * vectors, width), jnp.bfloat16),
            pltpu.VMEM((SPAN * vectors, WIDE * vectors), jnp.float32),
        ],
        compiler_params=pltpu.CompilerParams(vmem_limit_bytes=32 * 1024 * 1024),
        cost_estimate=pl.CostEstimate(flops=6 * 10**9, bytes_accessed=12 * 2**20, transcendentals=0),
        name="gram",
    )(place, margin_rows[0, 0], own_vectors[0, 0], swap, one, two, post, matrix)

    reverse = partner_swap(back).astype(jnp.float32)
    far_rows = stream(
        jnp.stack([ahead[2] + reverse[2], reverse[3]]).astype(jnp.bfloat16), 2
    )
    near_rows = stream((ahead[0:2] + reverse[0:2]).astype(jnp.bfloat16), 1)
    row = shape((vectors, FULL * vectors), jnp.float32)
    mine, other = pl.pallas_call(
        window_kernel,
        out_shape=(row, row),
        in_specs=[SMEM, VMEM, VMEM, VMEM],
        out_specs=(VMEM, VMEM),
        name="window",
    )(place, home, near_rows, far_rows)
    coarse = (mine + partner_swap(other)).astype(jnp.bfloat16)

    opposite = ring(coarse, 2)
    up = ring(coarse, 1)
    down = ring(coarse, -1)
    count = lax.axis_size("grp")
    spread = pl.pallas_call(
        spread_kernel,
        out_shape=shape((count, vectors, FULL * vectors), jnp.float32),
        in_specs=[SMEM, VMEM, VMEM, VMEM, VMEM],
        out_specs=VMEM,
        name="spread",
    )(place, coarse, up, down, opposite)
    return spread[:, None]


def solution(mesh):
    placed = (
        P("grp", "sub", None, None),
        P("grp", "sub", None, None),
        P("grp", "sub", None, None, None, None),
        P("grp", "sub", None),
        P("grp", "sub", None),
        P("grp", "sub", None, None, None),
    )
    return jax.shard_map(
        on_device, mesh=mesh, in_specs=placed, out_specs=P(None, "sub", None, None), check_vma=False
    )
```

time: 133 us -> 64.2 us (0.48); the launches traced: 131 us -> 63.8 us
  starting transfers between devices: 52.6 us -> 12.2 us
  local copies, waits for them, and re-layouts: 36 us -> 7.78 us
  waiting for transfers between devices: 2.42 us -> 24.9 us
  Pallas kernels: 0 us -> 17.2 us
  blocking collectives: 13.5 us -> 0 us
  other arithmetic: 13.9 us -> 1.65 us
  matrix products: 12.1 us -> 0 us
    ppermute x16 -> x11, starting transfers between devices: 52.6 us -> 12.2 us  [the longest x4 6.7 us: stream(): return lax.ppermute(block, 'sub', route)]
    ppermute x16 -> x11, waiting for transfers between devices: 2.42 us -> 24.9 us  [the longest x4 15 us: stream(): return lax.ppermute(block, 'sub', route)]
    scatter x8 -> x0, local copies, waits for them, and re-layouts: 20.1 us -> none  [place_rows(): jnp.zeros((vectors, width), jnp.bfloat16).at[:, rows.reshape(-1)].set(flat)]
    pallas_call x0 -> x4, Pallas kernels: none -> 17.2 us  [the longest x1 11.4 us: on_device(): pl.pallas_call(gram_kernel, grid=(steps,), out_shape=(shape((2, vectors,...]
    all_gather x1 -> x0, blocking collectives: 13.5 us -> none  [on_device(): return lax.all_gather(coarse[None, None], 'grp', axis=0, tiled=True)]
    dot_general x9 -> x0, matrix products: 12.1 us -> none  [the longest x1 8.16 us: on_device(): lax.dot_general(product, present, (((1,), (1,)), ((), ())), preferred_ele...]
    another operation x14 -> x5, other arithmetic: 9.59 us -> 0.64 us  [the longest x1 0.56 us: on_device(): jnp.stack([device, core, 1 - 2 * core, lax.axis_index('grp')])]
    scatter-add x9 -> x0, local copies, waits for them, and re-layouts: 7.58 us -> none  [on_device(): coarse = coarse.at[:, start:start + span * vectors].add(incoming)]
  transfers between devices with their start and end apart: 16 -> 11, of which waited for: 3 -> 10; matrix products, arithmetic and copies ran while one was open for 28% -> 1% of each run, Pallas kernels for 0% -> 0%
where the time goes in v1:
time: 64.2 us; the launch traced here: 63.8 us
  waiting for transfers between devices  24.9 us (39%)
  Pallas kernels  17.2 us (27%)
  starting transfers between devices  12.2 us (19%)
  local copies, waits for them, and re-layouts  7.78 us (12%)
  other arithmetic  1.65 us (3%)
    ppermute x4, waiting for transfers between devices, stream(): return lax.ppermute(block, 'sub', route)  15 us
    pallas_call x1, Pallas kernels, on_device(): pl.pallas_call(gram_kernel, grid=(steps,), out_shape=(shape((2, vectors,...  11.4 us
    unnamed x22, local copies, waits for them, and re-layouts  6.89 us
    ppermute x4, starting transfers between devices, stream(): return lax.ppermute(block, 'sub', route)  6.7 us
    ppermute x3, starting transfers between devices, ring(): lax.ppermute(block, 'grp', [(i, (i + distance) % count) for i in range(co...  5.14 us
    ppermute x4, waiting for transfers between devices, partner_swap(): lax.ppermute(block, 'sub', [(i, i ^ 1) for i in range(lax.axis_size('sub'...  5.13 us
    ppermute x3, waiting for transfers between devices, ring(): lax.ppermute(block, 'grp', [(i, (i + distance) % count) for i in range(co...  4.8 us
    pallas_call x1, Pallas kernels, on_device(): pl.pallas_call(pick_kernel, out_shape=(shape((5,) + message, jnp.bfloat16...  1.96 us
  transfers between devices with their start and end apart: 11, of which 10 were waited for; matrix products, arithmetic and copies ran while one was open for 1% of the time, Pallas kernels for 0%

profile of v1, /device:TPU:24, one launch (start us, length us, event | category | flops | bytes accessed | tf_op | source)
XLA Modules:
  0.0 63.8 jit_solution(7325407287828635981)
XLA Ops:
  0.0 0.6 pad_add_fusion.place_ref
  0.6 2.0 %pick.1 = (bf16[5,4,48,128]{3,2,1,0:T(8,128)(2,1)}, bf16[3,4,48,128]{3,2,1,0:T(8,128)(2,1)}) custom-call(s32[4]{0:T(128)} %pad_add_fusion.place_ref, s32[8]{0:T(128)} %bitcast.17, s32[8]{0:T(128)} %bitcast.18, bf16[8,4,48,128]{3,2,1,0:T(8,128)(2,1)} %bitcast.16), custom_call_target="tpu_custom_call" | custom-call | tf_op jit(solution)/shard_map/pick/pallas_call | solution.py:203
  2.5 0.0 collective-permute-start
  2.5 0.9 %fusion.3 = (bf16[1,4,48,128]{3,2,1,0:T(8,128)(2,1)S(1)}, bf16[1,4,48,128]{3,2,1,0:T(8,128)(2,1)S(1)}, bf16[1,4,48,128]{3,2,1,0:T(8,128)(2,1)S(1)}) fusion(bf16[3,4,48,128]{3,2,1,0:T(8,128)(2,1)} %get-tuple-element.13), kind=kLoop, calls=%fused_computation.11 | loop fusion | bytes 294912 | tf_op jit(solution)/shard_map/slice | solution.py:211
  3.4 0.9 %collective-permute-done.swap_ref = bf16[5,4,48,128]{3,2,1,0:T(8,128)(2,1)S(1)} collective-permute-done((bf16[5,4,48,128]{3,2,1,0:T(8,128)(2,1)}, bf16[5,4,48,128]{3,2,1,0:T(8,128)(2,1)S(1)}, u32[]{:S(2)}, u32[]{:S(2)}) %collective-permute-start) | collective-permute-done | bytes 245792 | tf_op jit(solution)/shard_map/ppermute | solution.py:18
  4.3 2.0 %collective-permute-start.1 = (bf16[4,4,48,128]{3,2,1,0:T(8,128)(2,1)S(1)}, bf16[4,4,48,128]{3,2,1,0:T(8,128)(2,1)S(1)}, u32[]{:S(2)}, u32[]{:S(2)}) collective-permute-start(bf16[4,4,48,128]{3,2,1,0:T(8,128)(2,1)S(1)} %pad_maximum_fusion), channel_id=1, source_target_pairs={{0,2},{1,0},{2,4},{3,1},{4,6},{5,3},{6,8},{7,5},{8,10},{9,7},{10,1... | collective-permute-start | bytes 589832 | tf_op jit(solution)/shard_map/ppermute | solution.py:27
  6.3 3.3 %collective-permute-start.2 = (bf16[3,4,48,128]{3,2,1,0:T(8,128)(2,1)S(1)}, bf16[3,4,48,128]{3,2,1,0:T(8,128)(2,1)S(1)}, u32[]{:S(2)}, u32[]{:S(2)}) collective-permute-start(bf16[3,4,48,128]{3,2,1,0:T(8,128)(2,1)S(1)} %pad_maximum_fusion.1), channel_id=1, source_target_pairs={{0,4},{1,0},{2,6},{3,2},{4,8},{5,1},{6,10},{7,3},{8,12},{9,5},{10,... | collective-permute-start | bytes 442376 | tf_op jit(solution)/shard_map/ppermute | solution.py:27
  9.7 8.0 %collective-permute-done.2.two_ref = bf16[3,4,48,128]{3,2,1,0:T(8,128)(2,1)S(1)} collective-permute-done((bf16[3,4,48,128]{3,2,1,0:T(8,128)(2,1)S(1)}, bf16[3,4,48,128]{3,2,1,0:T(8,128)(2,1)S(1)}, u32[]{:S(2)}, u32[]{:S(2)}) %collective-permute-start.2) | collective-permute-done | bytes 147488 | tf_op jit(solution)/shard_map/ppermute | solution.py:27
  17.6 0.0 collective-permute-done.1.one_ref
  17.7 0.1 collective-permute-start.3
  17.8 1.4 %collective-permute-done.3.post_ref = bf16[3,4,48,128]{3,2,1,0:T(8,128)(2,1)S(1)} collective-permute-done((bf16[3,4,48,128]{3,2,1,0:T(8,128)(2,1)S(1)}, bf16[3,4,48,128]{3,2,1,0:T(8,128)(2,1)S(1)}, u32[]{:S(2)}, u32[]{:S(2)}) %collective-permute-start.3) | collective-permute-done | bytes 147488 | tf_op jit(solution)/shard_map/ppermute | solution.py:18
  19.1 0.0 copy-start.1
  19.2 0.6 copy-done.1
  19.7 0.0 copy-start.2
  19.7 3.4 %copy-done.2 = bf16[1,1,2048,2048]{3,2,1,0:T(8,128)(2,1)S(1)} copy-done((bf16[1,1,2048,2048]{3,2,1,0:T(8,128)(2,1)S(1)}, bf16[1,1,2048,2048]{3,2,1,0:T(8,128)(2,1)}, u32[]{:S(2)}) %copy-start.2) | copy-done | bytes 8388632
  23.1 0.0 copy-start.3
  23.1 0.9 %copy-done.3 = bf16[1,1,48,2048]{3,2,1,0:T(8,128)(2,1)S(1)} copy-done((bf16[1,1,48,2048]{3,2,1,0:T(8,128)(2,1)S(1)}, bf16[1,1,48,2048]{3,2,1,0:T(8,128)(2,1)}, u32[]{:S(2)}) %copy-start.3) | copy-done | bytes 196632
  24.0 0.0 copy-start.4
  24.0 0.7 %copy-done.4 = s32[1,1,8,4,128]{4,3,2,1,0:T(4,128)S(1)} copy-done((s32[1,1,8,4,128]{4,3,2,1,0:T(4,128)S(1)}, s32[1,1,8,4,128]{4,3,2,1,0:T(4,128)}, u32[]{:S(2)}) %copy-start.4) | copy-done | bytes 16408
  24.8 11.4 %gram.1 = (f32[2,48,480]{2,1,0:T(8,128)S(1)}, f32[3,48,480]{2,1,0:T(8,128)S(1)}, bf16[4,48,480]{2,1,0:T(8,128)(2,1)S(1)}) custom-call(s32[4]{0:T(128)S(1)} %copy-done.1, s32[8,4,128]{2,1,0:T(4,128)S(1)} %bitcast.15, bf16[48,2048]{1,0:T(8,128)(2,1)S(1)} %bitcast.14, bf16[5,4,48,128]{3,2,1,0:T(8,128)(2,1)S(1)} %collective-permute-done.swap_ref, ...), custom_call_target="tpu_custom_call" | custom-call | flops 6000000000 | bytes 12582912 | tf_op jit(solution)/shard_map/gram/pallas_call | solution.py:218
  36.1 0.0 copy-start
  36.1 0.2 collective-permute-start.4
  36.4 1.3 %collective-permute-done.4 = bf16[4,48,480]{2,1,0:T(8,128)(2,1)S(1)} collective-permute-done((bf16[4,48,480]{2,1,0:T(8,128)(2,1)S(1)}, bf16[4,48,480]{2,1,0:T(8,128)(2,1)S(1)}, u32[]{:S(2)}, u32[]{:S(2)}) %collective-permute-start.4) | collective-permute-done | bytes 184352 | tf_op jit(solution)/shard_map/ppermute | solution.py:18
  37.8 0.0 copy-done
  37.8 0.1 collective-permute-start.6
  37.9 1.3 %collective-permute-start.5 = (bf16[2,48,480]{2,1,0:T(8,128)(2,1)S(1)}, bf16[2,48,480]{2,1,0:T(8,128)(2,1)S(1)}, u32[]{:S(2)}, u32[]{:S(2)}) collective-permute-start(bf16[2,48,480]{2,1,0:T(8,128)(2,1)S(1)} %fusion), channel_id=1, source_target_pairs={{0,2},{1,0},{2,4},{3,1},{4,6},{5,3},{6,8},{7,5},{8,10},{9,7},{10,1... | collective-permute-start | bytes 276488 | tf_op jit(solution)/shard_map/ppermute | solution.py:27
  39.2 6.9 %collective-permute-done.6.two_ref = bf16[2,48,480]{2,1,0:T(8,128)(2,1)S(1)} collective-permute-done((bf16[2,48,480]{2,1,0:T(8,128)(2,1)S(1)}, bf16[2,48,480]{2,1,0:T(8,128)(2,1)S(1)}, u32[]{:S(2)}, u32[]{:S(2)}) %collective-permute-start.6) | collective-permute-done | bytes 92192 | tf_op jit(solution)/shard_map/ppermute | solution.py:27
  46.1 0.0 copy-start.6
  46.1 0.1 collective-permute-done.5.one_ref
  46.2 0.5 copy-done.6
  46.7 0.1 copy-done.7
  46.8 1.9 %window.1 = (f32[48,816]{1,0:T(8,128)}, f32[48,816]{1,0:T(8,128)}) custom-call(s32[4]{0:T(128)} %pad_add_fusion.place_ref, f32[2,48,480]{2,1,0:T(8,128)} %copy-done, bf16[2,48,480]{2,1,0:T(8,128)(2,1)} %copy-done.7, bf16[2,48,480]{2,1,0:T(8,128)(2,1)} %copy-done.6), custom_call_target="tpu_custom_call" | custom-call | tf_op jit(solution)/shard_map/window/pallas_call | solution.py:257
  48.7 0.0 collective-permute-start.7
  48.7 1.6 %collective-permute-done.7 = f32[48,816]{1,0:T(8,128)S(1)} collective-permute-done((f32[48,816]{1,0:T(8,128)}, f32[48,816]{1,0:T(8,128)S(1)}, u32[]{:S(2)}, u32[]{:S(2)}) %collective-permute-start.7) | collective-permute-done | bytes 156704 | tf_op jit(solution)/shard_map/ppermute | solution.py:18
  50.4 0.9 %add_convert_fusion.own_ref = bf16[48,816]{1,0:T(8,128)(2,1)S(1)} fusion(f32[48,816]{1,0:T(8,128)} %get-tuple-element.17, f32[48,816]{1,0:T(8,128)S(1)} %collective-permute-done.7), kind=kLoop, calls=%fused_computation.3 | loop fusion | flops 78336 | bytes 391680 | tf_op jit(solution)/shard_map/convert_element_type | solution.py:264
  51.3 0.0 copy-start.5
  51.3 3.1 %collective-permute-start.10 = (bf16[48,816]{1,0:T(8,128)(2,1)S(1)}, bf16[48,816]{1,0:T(8,128)(2,1)S(1)}, u32[]{:S(2)}, u32[]{:S(2)}) collective-permute-start(bf16[48,816]{1,0:T(8,128)(2,1)S(1)} %add_convert_fusion.own_ref), channel_id=1, source_target_pairs={{0,128},{64,192},{128,0},{192,64},{1,129},{65,193},{129,1},{193,65... | collective-permute-start | bytes 235016 | tf_op jit(solution)/shard_map/ppermute | solution.py:189
  54.4 1.1 %collective-permute-start.9 = (bf16[48,816]{1,0:T(8,128)(2,1)S(1)}, bf16[48,816]{1,0:T(8,128)(2,1)S(1)}, u32[]{:S(2)}, u32[]{:S(2)}) collective-permute-start(bf16[48,816]{1,0:T(8,128)(2,1)S(1)} %add_convert_fusion.own_ref), channel_id=1, source_target_pairs={{0,192},{64,0},{128,64},{192,128},{1,193},{65,1},{129,65},{193,129... | collective-permute-start | bytes 235016 | tf_op jit(solution)/shard_map/ppermute | solution.py:189
  55.6 0.9 %collective-permute-start.8 = (bf16[48,816]{1,0:T(8,128)(2,1)S(1)}, bf16[48,816]{1,0:T(8,128)(2,1)S(1)}, u32[]{:S(2)}, u32[]{:S(2)}) collective-permute-start(bf16[48,816]{1,0:T(8,128)(2,1)S(1)} %add_convert_fusion.own_ref), channel_id=1, source_target_pairs={{0,64},{64,128},{128,192},{192,0},{1,65},{65,129},{129,193},{193,1... | collective-permute-start | bytes 235016 | tf_op jit(solution)/shard_map/ppermute | solution.py:189
  56.4 1.0 %collective-permute-done.10.far_ref = bf16[48,816]{1,0:T(8,128)(2,1)S(1)} collective-permute-done((bf16[48,816]{1,0:T(8,128)(2,1)S(1)}, bf16[48,816]{1,0:T(8,128)(2,1)S(1)}, u32[]{:S(2)}, u32[]{:S(2)}) %collective-permute-start.10) | collective-permute-done | bytes 78368 | tf_op jit(solution)/shard_map/ppermute | solution.py:189
  57.5 1.9 %collective-permute-done.9.down_ref = bf16[48,816]{1,0:T(8,128)(2,1)S(1)} collective-permute-done((bf16[48,816]{1,0:T(8,128)(2,1)S(1)}, bf16[48,816]{1,0:T(8,128)(2,1)S(1)}, u32[]{:S(2)}, u32[]{:S(2)}) %collective-permute-start.9) | collective-permute-done | bytes 78368 | tf_op jit(solution)/shard_map/ppermute | solution.py:189
  59.4 1.8 %collective-permute-done.8.up_ref = bf16[48,816]{1,0:T(8,128)(2,1)S(1)} collective-permute-done((bf16[48,816]{1,0:T(8,128)(2,1)S(1)}, bf16[48,816]{1,0:T(8,128)(2,1)S(1)}, u32[]{:S(2)}, u32[]{:S(2)}) %collective-permute-start.8) | collective-permute-done | bytes 78368 | tf_op jit(solution)/shard_map/ppermute | solution.py:189
  61.3 0.0 copy-done.5
  61.3 0.0 copy-done.8
  61.3 0.0 copy-done.9
  61.3 0.0 copy-start.10
  61.3 0.6 copy-done.10
  61.9 1.9 %spread.1 = f32[4,48,816]{2,1,0:T(8,128)} custom-call(s32[4]{0:T(128)} %pad_add_fusion.place_ref, bf16[48,816]{1,0:T(8,128)(2,1)} %copy-done.5, bf16[48,816]{1,0:T(8,128)(2,1)} %copy-done.10, bf16[48,816]{1,0:T(8,128)(2,1)} %copy-done.9, bf16[48,816]{1,0:T(8,128)(2,1)} %copy-done.8), custom_call_target="tpu_custom_call" | custom-call | tf_op jit(solution)/shard_map/spread/pallas_call | solution.py:270
  (15 shorter events, 0.2 us)
Async XLA Ops:
  2.5 1.7 %collective-permute-start = (bf16[5,4,48,128]{3,2,1,0:T(8,128)(2,1)}, bf16[5,4,48,128]{3,2,1,0:T(8,128)(2,1)S(1)}, u32[]{:S(2)}, u32[]{:S(2)}) collective-permute-start(bf16[5,4,48,128]{3,2,1,0:T(8,128)(2,1)} %get-tuple-element.12), channel_id=1, source_target_pairs={{0,1},{1,0},{2,3},{3,2},{4,5},{5,4},{6,7},{7,6},{8,9},{9,8},{10,11... | collective-permute-start | bytes 737288 | tf_op jit(solution)/shard_map/ppermute | solution.py:18
  4.3 13.4 %collective-permute-start.1 = (bf16[4,4,48,128]{3,2,1,0:T(8,128)(2,1)S(1)}, bf16[4,4,48,128]{3,2,1,0:T(8,128)(2,1)S(1)}, u32[]{:S(2)}, u32[]{:S(2)}) collective-permute-start(bf16[4,4,48,128]{3,2,1,0:T(8,128)(2,1)S(1)} %pad_maximum_fusion), channel_id=1, source_target_pairs={{0,2},{1,0},{2,4},{3,1},{4,6},{5,3},{6,8},{7,5},{8,10},{9,7},{10,1... | collective-permute-start | bytes 589832 | tf_op jit(solution)/shard_map/ppermute | solution.py:27
  6.3 11.3 %collective-permute-start.2 = (bf16[3,4,48,128]{3,2,1,0:T(8,128)(2,1)S(1)}, bf16[3,4,48,128]{3,2,1,0:T(8,128)(2,1)S(1)}, u32[]{:S(2)}, u32[]{:S(2)}) collective-permute-start(bf16[3,4,48,128]{3,2,1,0:T(8,128)(2,1)S(1)} %pad_maximum_fusion.1), channel_id=1, source_target_pairs={{0,4},{1,0},{2,6},{3,2},{4,8},{5,1},{6,10},{7,3},{8,12},{9,5},{10,... | collective-permute-start | bytes 442376 | tf_op jit(solution)/shard_map/ppermute | solution.py:27
  17.7 1.5 %collective-permute-start.3 = (bf16[3,4,48,128]{3,2,1,0:T(8,128)(2,1)S(1)}, bf16[3,4,48,128]{3,2,1,0:T(8,128)(2,1)S(1)}, u32[]{:S(2)}, u32[]{:S(2)}) collective-permute-start(bf16[3,4,48,128]{3,2,1,0:T(8,128)(2,1)S(1)} %pad_maximum_fusion.2), channel_id=1, source_target_pairs={{0,1},{1,0},{2,3},{3,2},{4,5},{5,4},{6,7},{7,6},{8,9},{9,8},{10,11... | collective-permute-start | bytes 442376 | tf_op jit(solution)/shard_map/ppermute | solution.py:18
  19.1 0.6 copy-start.1
  19.7 3.4 %copy-start.2 = (bf16[1,1,2048,2048]{3,2,1,0:T(8,128)(2,1)S(1)}, bf16[1,1,2048,2048]{3,2,1,0:T(8,128)(2,1)}, u32[]{:S(2)}) copy-start(bf16[1,1,2048,2048]{3,2,1,0:T(8,128)(2,1)} %param.6) | copy-start | bytes 25165828
  23.1 0.9 %copy-start.3 = (bf16[1,1,48,2048]{3,2,1,0:T(8,128)(2,1)S(1)}, bf16[1,1,48,2048]{3,2,1,0:T(8,128)(2,1)}, u32[]{:S(2)}) copy-start(bf16[1,1,48,2048]{3,2,1,0:T(8,128)(2,1)} %param.7) | copy-start | bytes 589828
  24.0 0.7 %copy-start.4 = (s32[1,1,8,4,128]{4,3,2,1,0:T(4,128)S(1)}, s32[1,1,8,4,128]{4,3,2,1,0:T(4,128)}, u32[]{:S(2)}) copy-start(s32[1,1,8,4,128]{4,3,2,1,0:T(4,128)} %param.11) | copy-start | bytes 49156
  36.1 1.6 %copy-start = (f32[2,48,480]{2,1,0:T(8,128)}, f32[2,48,480]{2,1,0:T(8,128)S(1)}, u32[]{:S(2)}) copy-start(f32[2,48,480]{2,1,0:T(8,128)S(1)} %get-tuple-element.14.home_ref) | copy-start | bytes 552964
  36.1 1.5 %collective-permute-start.4 = (bf16[4,48,480]{2,1,0:T(8,128)(2,1)S(1)}, bf16[4,48,480]{2,1,0:T(8,128)(2,1)S(1)}, u32[]{:S(2)}, u32[]{:S(2)}) collective-permute-start(bf16[4,48,480]{2,1,0:T(8,128)(2,1)S(1)} %get-tuple-element.16), channel_id=1, source_target_pairs={{0,1},{1,0},{2,3},{3,2},{4,5},{5,4},{6,7},{7,6},{8,9},{9,8},{10,11... | collective-permute-start | bytes 552968 | tf_op jit(solution)/shard_map/ppermute | solution.py:18
  37.8 8.2 %collective-permute-start.6 = (bf16[2,48,480]{2,1,0:T(8,128)(2,1)S(1)}, bf16[2,48,480]{2,1,0:T(8,128)(2,1)S(1)}, u32[]{:S(2)}, u32[]{:S(2)}) collective-permute-start(bf16[2,48,480]{2,1,0:T(8,128)(2,1)S(1)} %pad_maximum_fusion.3), channel_id=1, source_target_pairs={{0,4},{1,0},{2,6},{3,2},{4,8},{5,1},{6,10},{7,3},{8,12},{9,5},{10,... | collective-permute-start | bytes 276488 | tf_op jit(solution)/shard_map/ppermute | solution.py:27
  37.9 8.3 %collective-permute-start.5 = (bf16[2,48,480]{2,1,0:T(8,128)(2,1)S(1)}, bf16[2,48,480]{2,1,0:T(8,128)(2,1)S(1)}, u32[]{:S(2)}, u32[]{:S(2)}) collective-permute-start(bf16[2,48,480]{2,1,0:T(8,128)(2,1)S(1)} %fusion), channel_id=1, source_target_pairs={{0,2},{1,0},{2,4},{3,1},{4,6},{5,3},{6,8},{7,5},{8,10},{9,7},{10,1... | collective-permute-start | bytes 276488 | tf_op jit(solution)/shard_map/ppermute | solution.py:27
  46.1 0.6 %copy-start.6 = (bf16[2,48,480]{2,1,0:T(8,128)(2,1)}, bf16[2,48,480]{2,1,0:T(8,128)(2,1)S(1)}, u32[]{:S(2)}) copy-start(bf16[2,48,480]{2,1,0:T(8,128)(2,1)S(1)} %collective-permute-done.6.two_ref) | copy-start | bytes 276484
  46.2 0.6 %copy-start.7 = (bf16[2,48,480]{2,1,0:T(8,128)(2,1)}, bf16[2,48,480]{2,1,0:T(8,128)(2,1)S(1)}, u32[]{:S(2)}) copy-start(bf16[2,48,480]{2,1,0:T(8,128)(2,1)S(1)} %collective-permute-done.5.one_ref) | copy-start | bytes 276484
  48.7 1.6 %collective-permute-start.7 = (f32[48,816]{1,0:T(8,128)}, f32[48,816]{1,0:T(8,128)S(1)}, u32[]{:S(2)}, u32[]{:S(2)}) collective-permute-start(f32[48,816]{1,0:T(8,128)} %get-tuple-element.18), channel_id=1, source_target_pairs={{0,1},{1,0},{2,3},{3,2},{4,5},{5,4},{6,7},{7,6},{8,9},{9,8},{10,11... | collective-permute-start | bytes 470024 | tf_op jit(solution)/shard_map/ppermute | solution.py:18
  51.3 10.0 %copy-start.5 = (bf16[48,816]{1,0:T(8,128)(2,1)}, bf16[48,816]{1,0:T(8,128)(2,1)S(1)}, u32[]{:S(2)}) copy-start(bf16[48,816]{1,0:T(8,128)(2,1)S(1)} %add_convert_fusion.own_ref) | copy-start | bytes 235012
  51.3 6.2 %collective-permute-start.10 = (bf16[48,816]{1,0:T(8,128)(2,1)S(1)}, bf16[48,816]{1,0:T(8,128)(2,1)S(1)}, u32[]{:S(2)}, u32[]{:S(2)}) collective-permute-start(bf16[48,816]{1,0:T(8,128)(2,1)S(1)} %add_convert_fusion.own_ref), channel_id=1, source_target_pairs={{0,128},{64,192},{128,0},{192,64},{1,129},{65,193},{129,1},{193,65... | collective-permute-start | bytes 235016 | tf_op jit(solution)/shard_map/ppermute | solution.py:189
  54.4 5.0 %collective-permute-start.9 = (bf16[48,816]{1,0:T(8,128)(2,1)S(1)}, bf16[48,816]{1,0:T(8,128)(2,1)S(1)}, u32[]{:S(2)}, u32[]{:S(2)}) collective-permute-start(bf16[48,816]{1,0:T(8,128)(2,1)S(1)} %add_convert_fusion.own_ref), channel_id=1, source_target_pairs={{0,192},{64,0},{128,64},{192,128},{1,193},{65,1},{129,65},{193,129... | collective-permute-start | bytes 235016 | tf_op jit(solution)/shard_map/ppermute | solution.py:189
  55.6 5.7 %collective-permute-start.8 = (bf16[48,816]{1,0:T(8,128)(2,1)S(1)}, bf16[48,816]{1,0:T(8,128)(2,1)S(1)}, u32[]{:S(2)}, u32[]{:S(2)}) collective-permute-start(bf16[48,816]{1,0:T(8,128)(2,1)S(1)} %add_convert_fusion.own_ref), channel_id=1, source_target_pairs={{0,64},{64,128},{128,192},{192,0},{1,65},{65,129},{129,193},{193,1... | collective-permute-start | bytes 235016 | tf_op jit(solution)/shard_map/ppermute | solution.py:189
  57.5 3.8 %copy-start.8 = (bf16[48,816]{1,0:T(8,128)(2,1)}, bf16[48,816]{1,0:T(8,128)(2,1)S(1)}, u32[]{:S(2)}) copy-start(bf16[48,816]{1,0:T(8,128)(2,1)S(1)} %collective-permute-done.10.far_ref) | copy-start | bytes 235012
  59.4 1.9 %copy-start.9 = (bf16[48,816]{1,0:T(8,128)(2,1)}, bf16[48,816]{1,0:T(8,128)(2,1)S(1)}, u32[]{:S(2)}) copy-start(bf16[48,816]{1,0:T(8,128)(2,1)S(1)} %collective-permute-done.9.down_ref) | copy-start | bytes 235012
  61.3 0.6 %copy-start.10 = (bf16[48,816]{1,0:T(8,128)(2,1)}, bf16[48,816]{1,0:T(8,128)(2,1)S(1)}, u32[]{:S(2)}) copy-start(bf16[48,816]{1,0:T(8,128)(2,1)S(1)} %collective-permute-done.8.up_ref) | copy-start | bytes 235012

commit v2 on v0

v2 whole, which is shorter than its diff:
```python
import jax
import jax.numpy as jnp
from jax import lax
from jax.experimental import pallas as pl
from jax.experimental.pallas import tpu as pltpu
from jax.sharding import PartitionSpec as P

H = 4
SPAN = 2 * H + 1
WIDE = SPAN + 1
FULL = 4 * H + 1
PART = 256
CHUNKS = 8
STACK = (0, 1, 2, 3, 4, -1, -2, -3, -4)
VMEM = pl.BlockSpec(memory_space=pltpu.VMEM)
HBM = pl.BlockSpec(memory_space=pltpu.HBM)


def partner_swap(block):
    return lax.ppermute(block, "sub", [(i, i ^ 1) for i in range(lax.axis_size("sub"))])


def stream(block, chips):
    count = lax.axis_size("sub")
    route = []
    for i in range(count):
        target = i + 2 * chips if i % 2 == 0 else i - 2 * chips
        route.append((i, target if 0 <= target < count else i ^ 1))
    return lax.ppermute(block, "sub", route)


def signs():
    me = lax.axis_index("sub")
    core = lax.rem(me, 2)
    return me, core, 1 - 2 * core


def pick_kernel(
    listed_hbm, counts_hbm, over_hbm, swap_ref, keep_ref, listed_ref, counts_ref, over_ref, sems
):
    pairs = [(listed_hbm, listed_ref), (counts_hbm, counts_ref)]
    pairs += [(over_hbm.at[n], over_ref.at[n]) for n in range(over_ref.shape[0])]
    copies = [
        pltpu.make_async_copy(source, target, sems.at[n])
        for n, (source, target) in enumerate(pairs)
    ]
    for copy in copies:
        copy.start()
    for copy in copies:
        copy.wait()
    me, core, sign = signs()
    slots, tiles = over_ref.shape[0], over_ref.shape[1]

    def pick(k, out_ref, at):
        target = me + sign * k
        slot = jnp.int32(0)
        amount = jnp.int32(0)
        for n in range(slots):
            hit = listed_ref[n] == target
            slot = jnp.where(hit, n, slot)
            amount = jnp.where(hit, counts_ref[n], amount)
        for t in range(tiles):
            live = (t < amount).astype(jnp.bfloat16)
            out_ref[at, t] = over_ref[slot, t] * live

    for at, k in enumerate((1, -1, -2, -3, -4)):
        pick(k, swap_ref, at)
    for at, k in enumerate((2, 3, 4)):
        pick(k, keep_ref, at)


def slot_of(sign, k):
    offset = sign * k
    return jnp.where(offset < 0, offset + H, offset + H - 1)


def expand(message, hot, mask):
    tiles, vectors, lanes = message.shape
    flat = jnp.concatenate([message[t] for t in range(tiles)], axis=1)
    parts = mask.shape[0]
    spread = jnp.concatenate([flat * mask[h : h + 1] for h in range(parts)], axis=0)
    dense = lax.dot_general(
        spread, hot, (((1,), (1,)), ((), ())), preferred_element_type=jnp.float32
    ).astype(jnp.bfloat16)
    return [dense[h * vectors : (h + 1) * vectors] for h in range(parts)]


def own_kernel(
    rows_hbm, own_hbm, matrix_hbm, swap_ref,
    matrix_ref, product_ref, present_ref, hot_ref, mask_ref, rows_ref, acc, sems, chunk_sems,
):
    width = matrix_ref.shape[0]
    vectors = own_hbm.shape[0]
    chunks = chunk_sems.shape[0]
    depth = width // chunks
    rows_copy = pltpu.make_async_copy(rows_hbm, rows_ref, sems.at[0])
    own_copy = pltpu.make_async_copy(own_hbm, present_ref.at[pl.ds(0, vectors)], sems.at[1])
    rows_copy.start()
    own_copy.start()
    copies = []
    for c in range(chunks):
        part = pl.ds(c * depth, depth)
        copy = pltpu.make_async_copy(matrix_hbm.at[part], matrix_ref.at[part], chunk_sems.at[c])
        copy.start()
        copies.append(copy)
    me, core, sign = signs()

    rows_copy.wait()
    lanes = rows_ref.shape[2]
    index = lax.broadcasted_iota(jnp.int32, (PART, lanes), 0)
    parts = lax.broadcasted_iota(jnp.int32, (width // PART, lanes), 0)
    for slot in range(rows_ref.shape[0]):
        low = rows_ref[slot] & (PART - 1)
        high = rows_ref[slot] // PART
        for t in range(rows_ref.shape[1]):
            place = slice(t * lanes, (t + 1) * lanes)
            hot_ref[slot, :, place] = jnp.where(index == low[t : t + 1], 1.0, 0.0).astype(jnp.bfloat16)
            mask_ref[slot, :, place] = jnp.where(parts == high[t : t + 1], 1.0, 0.0).astype(jnp.bfloat16)
    slot = slot_of(sign, 1)
    for h, block in enumerate(expand(swap_ref[0], hot_ref[slot], mask_ref[slot])):
        present_ref[vectors:, h * PART : (h + 1) * PART] = block

    own_copy.wait()
    for half in range(2):
        for copy in copies[half * chunks // 2 : (half + 1) * chunks // 2]:
            copy.wait()
        part = slice(half * width // 2, (half + 1) * width // 2)
        term = jnp.dot(
            present_ref[:, part], matrix_ref[part], preferred_element_type=jnp.float32
        )
        if half == 0:
            acc[...] = term
        else:
            product_ref[...] = (acc[...] + term).astype(jnp.bfloat16)


def near_kernel(matrix_ref, hot_ref, mask_ref, two_ref, one_ref, present_ref, product_ref):
    vectors = one_ref.shape[2]
    me, core, sign = signs()
    sources = (one_ref.at[1], one_ref.at[0], two_ref.at[1], two_ref.at[0])
    for at, source in enumerate(sources):
        slot = slot_of(sign, -1 - at)
        for h, block in enumerate(expand(source[...], hot_ref[slot], mask_ref[slot])):
            present_ref[at * vectors : (at + 1) * vectors, h * PART : (h + 1) * PART] = block
    product_ref[...] = jnp.dot(
        present_ref[...], matrix_ref[...], preferred_element_type=jnp.float32
    ).astype(jnp.bfloat16)


def times_all(product, right):
    return lax.dot_general(
        product, right, (((1,), (1,)), ((), ())), preferred_element_type=jnp.float32
    )


def back_kernel(
    own_present_ref, near_present_ref, near_product_ref, hot_ref, mask_ref, post_ref,
    far_present_ref, right_ref, back_ref,
):
    vectors = post_ref.shape[2]
    width = right_ref.shape[1]
    me, core, sign = signs()

    def right_rows(k):
        position = jnp.where(core == 0, H + k, H + 1 - k)
        return pl.ds(pl.multiple_of(position * vectors, vectors), vectors)

    right_ref[right_rows(H + 1)] = jnp.zeros((vectors, width), jnp.bfloat16)
    for at in range(2):
        right_ref[right_rows(at)] = own_present_ref[at * vectors : (at + 1) * vectors]
    for at in range(4):
        right_ref[right_rows(-1 - at)] = near_present_ref[at * vectors : (at + 1) * vectors]
    for at, source in enumerate((post_ref.at[2], post_ref.at[1], post_ref.at[0])):
        slot = slot_of(sign, 2 + at)
        for h, block in enumerate(expand(source[...], hot_ref[slot], mask_ref[slot])):
            place = slice(h * PART, (h + 1) * PART)
            far_present_ref[at * vectors : (at + 1) * vectors, place] = block
            right_ref[right_rows(2 + at), place] = block
    gram = times_all(near_product_ref[...], right_ref[...]).astype(jnp.bfloat16)
    for at in range(4):
        back_ref[at] = gram[at * vectors : (at + 1) * vectors]


def ahead_kernel(
    matrix_ref, own_product_ref, far_present_ref, right_ref, home_ref, ahead_ref, product
):
    vectors = home_ref.shape[1]
    product[0 : 2 * vectors] = own_product_ref[...]
    product[2 * vectors :] = jnp.dot(
        far_present_ref[...], matrix_ref[...], preferred_element_type=jnp.float32
    ).astype(jnp.bfloat16)
    gram = times_all(product[...], right_ref[...])
    for at in range(2):
        home_ref[at] = gram[at * vectors : (at + 1) * vectors]
    for at in range(3):
        ahead_ref[at] = gram[(2 + at) * vectors : (3 + at) * vectors]


def window_kernel(home_ref, one_ref, two_ref, near_ref, far_ref):
    me, core, sign = signs()
    vectors = home_ref.shape[1]
    blocks = FULL

    def window(terms):
        total = None
        for value, start in terms:
            value = value.astype(jnp.float32)
            if start < 0:
                value = value[:, -start * vectors :]
                start = 0
            if start + value.shape[1] // vectors > blocks:
                value = value[:, : (blocks - start) * vectors]
            after = blocks * vectors - start * vectors - value.shape[1]
            value = jnp.pad(value, ((0, 0), (start * vectors, after)))
            total = value if total is None else total + value
        return total

    for c in range(2):
        way = 1 - 2 * c

        @pl.when(core == c)
        def _():
            for ref, at, row in ((near_ref, 0, c), (far_ref, 1, 1 - c)):
                ref[...] = window(
                    [
                        (home_ref[at], H - row),
                        (one_ref[at], H - 2 * way - row),
                        (two_ref[at], H - 4 * way - row),
                    ]
                )


def spread_kernel(own_ref, one_ref, three_ref, two_ref, out_hbm, wide, sems):
    x = lax.axis_index("grp")
    copies = []
    for d, ref in enumerate((own_ref, one_ref, two_ref, three_ref)):
        wide[d] = ref[...].astype(jnp.float32)
        copy = pltpu.make_async_copy(wide.at[d], out_hbm.at[x ^ d], sems.at[d])
        copy.start()
        copies.append(copy)
    for copy in copies:
        copy.wait()


def across(block, bits):
    return lax.ppermute(block, "grp", [(i, i ^ bits) for i in range(lax.axis_size("grp"))])


def limit(mib):
    return pltpu.CompilerParams(vmem_limit_bytes=mib * 2**20)


def in_hbm(array):
    return pltpu.with_memory_space_constraint(array, pltpu.HBM)


def on_device(blocks, own_vectors, over_vectors, neighbours, counts, margin_rows):
    matrix = blocks[0, 0]
    width = matrix.shape[0]
    vectors = own_vectors.shape[2]
    over, rows = over_vectors[0, 0], margin_rows[0, 0]
    message = over.shape[1:]
    f32, bf16 = jnp.float32, jnp.bfloat16

    give, keep = pl.pallas_call(
        pick_kernel,
        out_shape=(pltpu.VMEM((5,) + message, bf16), pltpu.VMEM((3,) + message, bf16)),
        in_specs=[HBM] * 3,
        out_specs=(VMEM, VMEM),
        scratch_shapes=[
            pltpu.SMEM(neighbours.shape[2:], jnp.int32),
            pltpu.SMEM(counts.shape[2:], jnp.int32),
            pltpu.VMEM(over.shape, bf16),
            pltpu.SemaphoreType.DMA((2 + over.shape[0],)),
        ],
        compiler_params=limit(6),
        name="pick",
    )(in_hbm(neighbours[0, 0]), in_hbm(counts[0, 0]), in_hbm(over))
    swap = partner_swap(give)
    two = stream(jnp.stack([keep[2], swap[3], swap[4]]), 2)
    one = stream(jnp.stack([keep[0], swap[1], keep[1], swap[2]]), 1)

    loaded, own_product, own_present, hot, mask = pl.pallas_call(
        own_kernel,
        out_shape=(
            pltpu.VMEM((width, width), bf16),
            pltpu.VMEM((2 * vectors, width), bf16),
            pltpu.VMEM((2 * vectors, width), bf16),
            pltpu.VMEM((rows.shape[0], PART, rows.shape[1] * rows.shape[2]), bf16),
            pltpu.VMEM((rows.shape[0], width // PART, rows.shape[1] * rows.shape[2]), bf16),
        ),
        in_specs=[HBM, HBM, HBM, VMEM],
        out_specs=(VMEM,) * 5,
        scratch_shapes=[
            pltpu.VMEM(rows.shape, jnp.int32),
            pltpu.VMEM((2 * vectors, width), f32),
            pltpu.SemaphoreType.DMA((2,)),
            pltpu.SemaphoreType.DMA((CHUNKS,)),
        ],
        compiler_params=limit(16),
        cost_estimate=pl.CostEstimate(flops=10**9, bytes_accessed=10 * 2**20, transcendentals=0),
        name="own",
    )(in_hbm(rows), in_hbm(own_vectors[0, 0]), in_hbm(matrix), swap)

    two, one, mask = lax.optimization_barrier((two, one, mask))
    post = partner_swap(jnp.concatenate([two[2:3], one[2:4]]))

    near_present, near_product = pl.pallas_call(
        near_kernel,
        out_shape=(pltpu.VMEM((4 * vectors, width), bf16),) * 2,
        in_specs=[VMEM] * 5,
        out_specs=(VMEM,) * 2,
        compiler_params=limit(12),
        cost_estimate=pl.CostEstimate(flops=2 * 10**9, bytes_accessed=2**20, transcendentals=0),
        name="near",
    )(loaded, hot, mask, two, one)
    post, near_product = lax.optimization_barrier((post, near_product))
    far_present, right, back = pl.pallas_call(
        back_kernel,
        out_shape=(
            pltpu.VMEM((3 * vectors, width), bf16),
            pltpu.VMEM((WIDE * vectors, width), bf16),
            pltpu.VMEM((4, vectors, WIDE * vectors), bf16),
        ),
        in_specs=[VMEM] * 6,
        out_specs=(VMEM,) * 3,
        compiler_params=limit(12),
        cost_estimate=pl.CostEstimate(flops=10**9, bytes_accessed=2**20, transcendentals=0),
        name="back",
    )(own_present, near_present, near_product, hot, mask, post)
    reverse = partner_swap(back)
    home, ahead = pl.pallas_call(
        ahead_kernel,
        out_shape=(
            pltpu.VMEM((2, vectors, WIDE * vectors), f32),
            pltpu.VMEM((3, vectors, WIDE * vectors), f32),
        ),
        in_specs=[VMEM] * 4,
        out_specs=(VMEM,) * 2,
        scratch_shapes=[pltpu.VMEM((5 * vectors, width), bf16)],
        compiler_params=limit(12),
        cost_estimate=pl.CostEstimate(flops=2 * 10**9, bytes_accessed=2**20, transcendentals=0),
        name="ahead",
    )(loaded, own_product, far_present, right)
    reverse, ahead = lax.optimization_barrier((reverse, ahead))
    reverse = reverse.astype(f32)

    far_rows = stream(
        jnp.stack([ahead[2] + reverse[2], reverse[3]]).astype(jnp.bfloat16), 2
    )
    near_rows = stream((ahead[0:2] + reverse[0:2]).astype(jnp.bfloat16), 1)
    row = pltpu.VMEM((vectors, FULL * vectors), f32)
    mine, other = pl.pallas_call(
        window_kernel,
        out_shape=(row, row),
        in_specs=[VMEM, VMEM, VMEM],
        out_specs=(VMEM, VMEM),
        compiler_params=limit(6),
        name="window",
    )(home, near_rows, far_rows)
    coarse = (mine + partner_swap(other)).astype(jnp.bfloat16)

    across_two = across(coarse, 2)
    across_three = across(coarse, 3)
    across_one = across(coarse, 1)
    count = lax.axis_size("grp")
    gathered = pl.pallas_call(
        spread_kernel,
        out_shape=pltpu.HBM((count,) + row.shape, f32),
        in_specs=[VMEM] * 4,
        out_specs=HBM,
        scratch_shapes=[
            pltpu.VMEM((count,) + row.shape, f32),
            pltpu.SemaphoreType.DMA((count,)),
        ],
        compiler_params=limit(6),
        name="spread",
    )(coarse, across_one, across_three, across_two)
    return gathered[:, None]


def solution(mesh):
    placed = (
        P("grp", "sub", None, None),
        P("grp", "sub", None, None),
        P("grp", "sub", None, None, None, None),
        P("grp", "sub", None),
        P("grp", "sub", None),
        P("grp", "sub", None, None, None),
    )
    return jax.shard_map(
        on_device, mesh=mesh, in_specs=placed, out_specs=P(None, "sub", None, None), check_vma=False
    )
```

time: 133 us -> 43.1 us (0.32); the launches traced: 131 us -> 43 us
  starting transfers between devices: 52.6 us -> 12.3 us
  local copies, waits for them, and re-layouts: 36 us -> 0.04 us
  waiting for transfers between devices: 2.42 us -> 17.1 us
  other arithmetic: 13.9 us -> 0.18 us
  blocking collectives: 13.5 us -> 0 us
  Pallas kernels: 0 us -> 13 us
  matrix products: 12.1 us -> 0 us
    ppermute x16 -> x11, starting transfers between devices: 52.6 us -> 12.3 us  [the longest x4 7.21 us: stream(): return lax.ppermute(block, 'sub', route)]
    scatter x8 -> x0, local copies, waits for them, and re-layouts: 20.1 us -> none  [place_rows(): jnp.zeros((vectors, width), jnp.bfloat16).at[:, rows.reshape(-1)].set(flat)]
    ppermute x16 -> x11, waiting for transfers between devices: 2.42 us -> 17.1 us  [the longest x4 9.63 us: stream(): return lax.ppermute(block, 'sub', route)]
    all_gather x1 -> x0, blocking collectives: 13.5 us -> none  [on_device(): return lax.all_gather(coarse[None, None], 'grp', axis=0, tiled=True)]
    pallas_call x0 -> x7, Pallas kernels: none -> 13 us  [the longest x1 5.14 us: on_device(): pl.pallas_call(own_kernel, out_shape=(pltpu.VMEM((width, width), bf16), p...]
    dot_general x9 -> x0, matrix products: 12.1 us -> none  [the longest x1 8.16 us: on_device(): lax.dot_general(product, present, (((1,), (1,)), ((), ())), preferred_ele...]
    another operation x14 -> x4, other arithmetic: 9.59 us -> 0.08 us  [the longest x1 0.03 us: on_device(): one = stream(jnp.stack([keep[0], swap[1], keep[1], swap[2]]), 1)]
    scatter-add x9 -> x0, local copies, waits for them, and re-layouts: 7.58 us -> none  [on_device(): coarse = coarse.at[:, start:start + span * vectors].add(incoming)]
  transfers between devices with their start and end apart: 16 -> 11, of which waited for: 3 -> 7; matrix products, arithmetic and copies ran while one was open for 28% -> 0% of each run, Pallas kernels for 0% -> 22%
where the time goes in v2:
time: 43.1 us; the launch traced here: 43 us
  waiting for transfers between devices  17.1 us (40%)
  Pallas kernels  13 us (30%)
  starting transfers between devices  12.3 us (29%)
    ppermute x4, waiting for transfers between devices, stream(): return lax.ppermute(block, 'sub', route)  9.63 us
    ppermute x4, starting transfers between devices, stream(): return lax.ppermute(block, 'sub', route)  7.21 us
    pallas_call x1, Pallas kernels, on_device(): pl.pallas_call(own_kernel, out_shape=(pltpu.VMEM((width, width), bf16), p...  5.14 us
    ppermute x3, waiting for transfers between devices, across(): lax.ppermute(block, 'grp', [(i, i ^ bits) for i in range(lax.axis_size('g...  4.56 us
    ppermute x3, starting transfers between devices, across(): lax.ppermute(block, 'grp', [(i, i ^ bits) for i in range(lax.axis_size('g...  4.25 us
    ppermute x4, waiting for transfers between devices, partner_swap(): lax.ppermute(block, 'sub', [(i, i ^ 1) for i in range(lax.axis_size('sub'...  2.88 us
    pallas_call x1, Pallas kernels, on_device(): pl.pallas_call(near_kernel, out_shape=(pltpu.VMEM((4 * vectors, width), b...  2.24 us
    pallas_call x1, Pallas kernels, on_device(): pl.pallas_call(ahead_kernel, out_shape=(pltpu.VMEM((2, vectors, WIDE * ve...  1.94 us
  transfers between devices with their start and end apart: 11, of which 7 were waited for; matrix products, arithmetic and copies ran while one was open for 0% of the time, Pallas kernels for 22%

profile of v2, /device:TPU:24, one launch (start us, length us, event | category | flops | bytes accessed | tf_op | source)
XLA Modules:
  0.0 43.0 jit_solution(7591911263193814029)
XLA Ops:
  0.0 1.3 %pick.1 = (bf16[5,4,48,128]{3,2,1,0:T(8,128)(2,1)S(1)}, bf16[3,4,48,128]{3,2,1,0:T(8,128)(2,1)S(1)}) custom-call(s32[8]{0:T(128)} %bitcast.13, s32[8]{0:T(128)} %bitcast.14, bf16[8,4,48,128]{3,2,1,0:T(8,128)(2,1)} %bitcast.10), custom_call_target="tpu_custom_call" | custom-call | tf_op jit(solution)/shard_map/pick/pallas_call | solution.py:265
  1.3 0.1 collective-permute-start
  1.4 1.5 %collective-permute-done.swap_ref = bf16[5,4,48,128]{3,2,1,0:T(8,128)(2,1)S(1)} collective-permute-done((bf16[5,4,48,128]{3,2,1,0:T(8,128)(2,1)S(1)}, bf16[5,4,48,128]{3,2,1,0:T(8,128)(2,1)S(1)}, u32[]{:S(2)}, u32[]{:S(2)}) %collective-permute-start) | collective-permute-done | bytes 245792 | tf_op jit(solution)/shard_map/ppermute | solution.py:20
  2.9 2.0 %collective-permute-start.2 = (bf16[4,4,48,128]{3,2,1,0:T(8,128)(2,1)S(1)}, bf16[4,4,48,128]{3,2,1,0:T(8,128)(2,1)S(1)}, u32[]{:S(2)}, u32[]{:S(2)}) collective-permute-start(bf16[4,4,48,128]{3,2,1,0:T(8,128)(2,1)S(1)} %pad_maximum_fusion), channel_id=1, source_target_pairs={{0,2},{1,0},{2,4},{3,1},{4,6},{5,3},{6,8},{7,5},{8,10},{9,7},{10,1... | collective-permute-start | bytes 589832 | tf_op jit(solution)/shard_map/ppermute | solution.py:29
  4.9 3.3 %collective-permute-start.1 = (bf16[3,4,48,128]{3,2,1,0:T(8,128)(2,1)S(1)}, bf16[3,4,48,128]{3,2,1,0:T(8,128)(2,1)S(1)}, u32[]{:S(2)}, u32[]{:S(2)}) collective-permute-start(bf16[3,4,48,128]{3,2,1,0:T(8,128)(2,1)S(1)} %pad_maximum_fusion.1), channel_id=1, source_target_pairs={{0,4},{1,0},{2,6},{3,2},{4,8},{5,1},{6,10},{7,3},{8,12},{9,5},{10,... | collective-permute-start | bytes 442376 | tf_op jit(solution)/shard_map/ppermute | solution.py:29
  8.3 5.1 %own.1 = (bf16[2048,2048]{1,0:T(8,128)(2,1)S(1)}, bf16[96,2048]{1,0:T(8,128)(2,1)S(1)}, bf16[96,2048]{1,0:T(8,128)(2,1)S(1)}, bf16[8,256,512]{2,1,0:T(8,128)(2,1)S(1)}, bf16[8,8,512]{2,1,0:T(8,128)(2,1)S(1)}) custom-call(s32[8,4,128]{2,1,0:T(4,128)} %bitcast.12, bf16[48,2048]{1,0:T(8,128)(2,1)} %bitcast.11, bf16[2048,2048]{1,0:T(8,128)(2,1)} %bitcast.9, ...), custom_call_target="tpu_custom_call" | custom-call | flops 1000000000 | bytes 10485760 | tf_op jit(solution)/shard_map/own/pallas_call | solution.py:283
  13.4 2.8 %collective-permute-done.1.two_ref = bf16[3,4,48,128]{3,2,1,0:T(8,128)(2,1)S(1)} collective-permute-done((bf16[3,4,48,128]{3,2,1,0:T(8,128)(2,1)S(1)}, bf16[3,4,48,128]{3,2,1,0:T(8,128)(2,1)S(1)}, u32[]{:S(2)}, u32[]{:S(2)}) %collective-permute-start.1) | collective-permute-done | bytes 147488 | tf_op jit(solution)/shard_map/ppermute | solution.py:29
  16.3 0.0 collective-permute-done.2.one_ref
  16.3 0.1 collective-permute-start.3
  16.4 2.2 %near.1 = (bf16[192,2048]{1,0:T(8,128)(2,1)S(1)}, bf16[192,2048]{1,0:T(8,128)(2,1)S(1)}) custom-call(bf16[2048,2048]{1,0:T(8,128)(2,1)S(1)} %get-tuple-element.29.matrix_ref, bf16[8,256,512]{2,1,0:T(8,128)(2,1)S(1)} %get-tuple-element.32.hot_ref, bf16[8,8,512]{2,1,0:T(8,128)(2,1)S(1)} %get-tuple-element.35.mask_ref, ...), custom_call_target="tpu_custom_call" | custom-call | flops 2000000000 | bytes 1048576 | tf_op jit(solution)/shard_map/near/pallas_call | solution.py:308
  18.7 0.0 collective-permute-done.3.post_ref
  18.7 1.4 %back.1 = (bf16[144,2048]{1,0:T(8,128)(2,1)S(1)}, bf16[480,2048]{1,0:T(8,128)(2,1)S(1)}, bf16[4,48,480]{2,1,0:T(8,128)(2,1)S(1)}) custom-call(bf16[96,2048]{1,0:T(8,128)(2,1)S(1)} %get-tuple-element.31.own_present_ref, bf16[192,2048]{1,0:T(8,128)(2,1)S(1)} %get-tuple-element.38.near_present_ref, bf16[192,2048]{1,0:T(8,128)(2,1)S(1)} %get-tuple-element.40.near_product_ref, ...), custom_call_target="tpu_custom_call" | custom-call | flops 1000000000 | bytes 1048576 | tf_op jit(solution)/shard_map/back/pallas_call | solution.py:318
  20.1 0.6 %collective-permute-start.4 = (bf16[4,48,480]{2,1,0:T(8,128)(2,1)S(1)}, bf16[4,48,480]{2,1,0:T(8,128)(2,1)S(1)}, u32[]{:S(2)}, u32[]{:S(2)}) collective-permute-start(bf16[4,48,480]{2,1,0:T(8,128)(2,1)S(1)} %get-tuple-element.45), channel_id=1, source_target_pairs={{0,1},{1,0},{2,3},{3,2},{4,5},{5,4},{6,7},{7,6},{8,9},{9,8},{10,11... | collective-permute-start | bytes 552968 | tf_op jit(solution)/shard_map/ppermute | solution.py:20
  20.6 1.9 %ahead.1 = (f32[2,48,480]{2,1,0:T(8,128)S(1)}, f32[3,48,480]{2,1,0:T(8,128)S(1)}) custom-call(bf16[2048,2048]{1,0:T(8,128)(2,1)S(1)} %get-tuple-element.29.matrix_ref, bf16[96,2048]{1,0:T(8,128)(2,1)S(1)} %get-tuple-element.30.own_product_ref, bf16[144,2048]{1,0:T(8,128)(2,1)S(1)} %get-tuple-element.42.far_present_ref, ...), custom_call_target="tpu_custom_call" | custom-call | flops 2000000000 | bytes 1048576 | tf_op jit(solution)/shard_map/ahead/pallas_call | solution.py:332
  22.6 0.0 collective-permute-done.4
  22.7 0.9 %collective-permute-start.6 = (bf16[2,48,480]{2,1,0:T(8,128)(2,1)S(1)}, bf16[2,48,480]{2,1,0:T(8,128)(2,1)S(1)}, u32[]{:S(2)}, u32[]{:S(2)}) collective-permute-start(bf16[2,48,480]{2,1,0:T(8,128)(2,1)S(1)} %pad_maximum_fusion.3), channel_id=1, source_target_pairs={{0,4},{1,0},{2,6},{3,2},{4,8},{5,1},{6,10},{7,3},{8,12},{9,5},{10,... | collective-permute-start | bytes 276488 | tf_op jit(solution)/shard_map/ppermute | solution.py:29
  23.6 1.0 %collective-permute-start.5 = (bf16[2,48,480]{2,1,0:T(8,128)(2,1)S(1)}, bf16[2,48,480]{2,1,0:T(8,128)(2,1)S(1)}, u32[]{:S(2)}, u32[]{:S(2)}) collective-permute-start(bf16[2,48,480]{2,1,0:T(8,128)(2,1)S(1)} %fusion), channel_id=1, source_target_pairs={{0,2},{1,0},{2,4},{3,1},{4,6},{5,3},{6,8},{7,5},{8,10},{9,7},{10,1... | collective-permute-start | bytes 276488 | tf_op jit(solution)/shard_map/ppermute | solution.py:29
  24.6 6.4 %collective-permute-done.6.two_ref = bf16[2,48,480]{2,1,0:T(8,128)(2,1)S(1)} collective-permute-done((bf16[2,48,480]{2,1,0:T(8,128)(2,1)S(1)}, bf16[2,48,480]{2,1,0:T(8,128)(2,1)S(1)}, u32[]{:S(2)}, u32[]{:S(2)}) %collective-permute-start.6) | collective-permute-done | bytes 92192 | tf_op jit(solution)/shard_map/ppermute | solution.py:29
  31.0 0.4 %collective-permute-done.5.one_ref = bf16[2,48,480]{2,1,0:T(8,128)(2,1)S(1)} collective-permute-done((bf16[2,48,480]{2,1,0:T(8,128)(2,1)S(1)}, bf16[2,48,480]{2,1,0:T(8,128)(2,1)S(1)}, u32[]{:S(2)}, u32[]{:S(2)}) %collective-permute-start.5) | collective-permute-done | bytes 92192 | tf_op jit(solution)/shard_map/ppermute | solution.py:29
  31.4 0.2 window.1
  31.6 0.1 collective-permute-start.7
  31.7 1.4 %collective-permute-done.7 = f32[48,816]{1,0:T(8,128)S(1)} collective-permute-done((f32[48,816]{1,0:T(8,128)S(1)}, f32[48,816]{1,0:T(8,128)S(1)}, u32[]{:S(2)}, u32[]{:S(2)}) %collective-permute-start.7) | collective-permute-done | bytes 156704 | tf_op jit(solution)/shard_map/ppermute | solution.py:20
  33.1 3.1 %collective-permute-start.10 = (bf16[48,816]{1,0:T(8,128)(2,1)S(1)}, bf16[48,816]{1,0:T(8,128)(2,1)S(1)}, u32[]{:S(2)}, u32[]{:S(2)}) collective-permute-start(bf16[48,816]{1,0:T(8,128)(2,1)S(1)} %add_convert_fusion.own_ref), channel_id=1, source_target_pairs={{0,128},{64,192},{128,0},{192,64},{1,129},{65,193},{129,1},{193,65... | collective-permute-start | bytes 235016 | tf_op jit(solution)/shard_map/ppermute | solution.py:246
  36.2 1.1 %collective-permute-start.9 = (bf16[48,816]{1,0:T(8,128)(2,1)S(1)}, bf16[48,816]{1,0:T(8,128)(2,1)S(1)}, u32[]{:S(2)}, u32[]{:S(2)}) collective-permute-start(bf16[48,816]{1,0:T(8,128)(2,1)S(1)} %add_convert_fusion.own_ref), channel_id=1, source_target_pairs={{0,192},{64,128},{128,64},{192,0},{1,193},{65,129},{129,65},{193,1... | collective-permute-start | bytes 235016 | tf_op jit(solution)/shard_map/ppermute | solution.py:246
  37.4 0.0 collective-permute-start.8
  37.4 1.9 %collective-permute-done.10.two_ref = bf16[48,816]{1,0:T(8,128)(2,1)S(1)} collective-permute-done((bf16[48,816]{1,0:T(8,128)(2,1)S(1)}, bf16[48,816]{1,0:T(8,128)(2,1)S(1)}, u32[]{:S(2)}, u32[]{:S(2)}) %collective-permute-start.10) | collective-permute-done | bytes 78368 | tf_op jit(solution)/shard_map/ppermute | solution.py:246
  39.3 2.6 %collective-permute-done.9.three_ref = bf16[48,816]{1,0:T(8,128)(2,1)S(1)} collective-permute-done((bf16[48,816]{1,0:T(8,128)(2,1)S(1)}, bf16[48,816]{1,0:T(8,128)(2,1)S(1)}, u32[]{:S(2)}, u32[]{:S(2)}) %collective-permute-start.9) | collective-permute-done | bytes 78368 | tf_op jit(solution)/shard_map/ppermute | solution.py:246
  41.9 0.0 collective-permute-done.8.one_ref
  41.9 0.9 %spread.1 = f32[4,48,816]{2,1,0:T(8,128)} custom-call(bf16[48,816]{1,0:T(8,128)(2,1)S(1)} %add_convert_fusion.own_ref, bf16[48,816]{1,0:T(8,128)(2,1)S(1)} %collective-permute-done.8.one_ref, bf16[48,816]{1,0:T(8,128)(2,1)S(1)} %collective-permute-done.9.three_ref, bf16[48,816]{1,0:T(8,128)(2,1)S(1)} %collective-permute-done.10.two_ref), custom_call_target="tpu_custom_call" | custom-call | tf_op jit(solution)/shard_map/spread/pallas_call | solution.py:367
  (14 shorter events, 0.2 us)
Async XLA Ops:
  1.3 1.6 %collective-permute-start = (bf16[5,4,48,128]{3,2,1,0:T(8,128)(2,1)S(1)}, bf16[5,4,48,128]{3,2,1,0:T(8,128)(2,1)S(1)}, u32[]{:S(2)}, u32[]{:S(2)}) collective-permute-start(bf16[5,4,48,128]{3,2,1,0:T(8,128)(2,1)S(1)} %get-tuple-element.28), channel_id=1, source_target_pairs={{0,1},{1,0},{2,3},{3,2},{4,5},{5,4},{6,7},{7,6},{8,9},{9,8},{10,11... | collective-permute-start | bytes 737288 | tf_op jit(solution)/shard_map/ppermute | solution.py:20
  2.9 13.4 %collective-permute-start.2 = (bf16[4,4,48,128]{3,2,1,0:T(8,128)(2,1)S(1)}, bf16[4,4,48,128]{3,2,1,0:T(8,128)(2,1)S(1)}, u32[]{:S(2)}, u32[]{:S(2)}) collective-permute-start(bf16[4,4,48,128]{3,2,1,0:T(8,128)(2,1)S(1)} %pad_maximum_fusion), channel_id=1, source_target_pairs={{0,2},{1,0},{2,4},{3,1},{4,6},{5,3},{6,8},{7,5},{8,10},{9,7},{10,1... | collective-permute-start | bytes 589832 | tf_op jit(solution)/shard_map/ppermute | solution.py:29
  4.9 11.3 %collective-permute-start.1 = (bf16[3,4,48,128]{3,2,1,0:T(8,128)(2,1)S(1)}, bf16[3,4,48,128]{3,2,1,0:T(8,128)(2,1)S(1)}, u32[]{:S(2)}, u32[]{:S(2)}) collective-permute-start(bf16[3,4,48,128]{3,2,1,0:T(8,128)(2,1)S(1)} %pad_maximum_fusion.1), channel_id=1, source_target_pairs={{0,4},{1,0},{2,6},{3,2},{4,8},{5,1},{6,10},{7,3},{8,12},{9,5},{10,... | collective-permute-start | bytes 442376 | tf_op jit(solution)/shard_map/ppermute | solution.py:29
  16.3 2.4 %collective-permute-start.3 = (bf16[3,4,48,128]{3,2,1,0:T(8,128)(2,1)S(1)}, bf16[3,4,48,128]{3,2,1,0:T(8,128)(2,1)S(1)}, u32[]{:S(2)}, u32[]{:S(2)}) collective-permute-start(bf16[3,4,48,128]{3,2,1,0:T(8,128)(2,1)S(1)} %pad_maximum_fusion.2), channel_id=1, source_target_pairs={{0,1},{1,0},{2,3},{3,2},{4,5},{5,4},{6,7},{7,6},{8,9},{9,8},{10,11... | collective-permute-start | bytes 442376 | tf_op jit(solution)/shard_map/ppermute | solution.py:20
  20.1 2.5 %collective-permute-start.4 = (bf16[4,48,480]{2,1,0:T(8,128)(2,1)S(1)}, bf16[4,48,480]{2,1,0:T(8,128)(2,1)S(1)}, u32[]{:S(2)}, u32[]{:S(2)}) collective-permute-start(bf16[4,48,480]{2,1,0:T(8,128)(2,1)S(1)} %get-tuple-element.45), channel_id=1, source_target_pairs={{0,1},{1,0},{2,3},{3,2},{4,5},{5,4},{6,7},{7,6},{8,9},{9,8},{10,11... | collective-permute-start | bytes 552968 | tf_op jit(solution)/shard_map/ppermute | solution.py:20
  22.7 8.2 %collective-permute-start.6 = (bf16[2,48,480]{2,1,0:T(8,128)(2,1)S(1)}, bf16[2,48,480]{2,1,0:T(8,128)(2,1)S(1)}, u32[]{:S(2)}, u32[]{:S(2)}) collective-permute-start(bf16[2,48,480]{2,1,0:T(8,128)(2,1)S(1)} %pad_maximum_fusion.3), channel_id=1, source_target_pairs={{0,4},{1,0},{2,6},{3,2},{4,8},{5,1},{6,10},{7,3},{8,12},{9,5},{10,... | collective-permute-start | bytes 276488 | tf_op jit(solution)/shard_map/ppermute | solution.py:29
  23.6 7.8 %collective-permute-start.5 = (bf16[2,48,480]{2,1,0:T(8,128)(2,1)S(1)}, bf16[2,48,480]{2,1,0:T(8,128)(2,1)S(1)}, u32[]{:S(2)}, u32[]{:S(2)}) collective-permute-start(bf16[2,48,480]{2,1,0:T(8,128)(2,1)S(1)} %fusion), channel_id=1, source_target_pairs={{0,2},{1,0},{2,4},{3,1},{4,6},{5,3},{6,8},{7,5},{8,10},{9,7},{10,1... | collective-permute-start | bytes 276488 | tf_op jit(solution)/shard_map/ppermute | solution.py:29
  31.6 1.5 %collective-permute-start.7 = (f32[48,816]{1,0:T(8,128)S(1)}, f32[48,816]{1,0:T(8,128)S(1)}, u32[]{:S(2)}, u32[]{:S(2)}) collective-permute-start(f32[48,816]{1,0:T(8,128)S(1)} %get-tuple-element.50), channel_id=1, source_target_pairs={{0,1},{1,0},{2,3},{3,2},{4,5},{5,4},{6,7},{7,6},{8,9},{9,8},{10,11... | collective-permute-start | bytes 470024 | tf_op jit(solution)/shard_map/ppermute | solution.py:20
  33.1 6.2 %collective-permute-start.10 = (bf16[48,816]{1,0:T(8,128)(2,1)S(1)}, bf16[48,816]{1,0:T(8,128)(2,1)S(1)}, u32[]{:S(2)}, u32[]{:S(2)}) collective-permute-start(bf16[48,816]{1,0:T(8,128)(2,1)S(1)} %add_convert_fusion.own_ref), channel_id=1, source_target_pairs={{0,128},{64,192},{128,0},{192,64},{1,129},{65,193},{129,1},{193,65... | collective-permute-start | bytes 235016 | tf_op jit(solution)/shard_map/ppermute | solution.py:246
  36.2 5.7 %collective-permute-start.9 = (bf16[48,816]{1,0:T(8,128)(2,1)S(1)}, bf16[48,816]{1,0:T(8,128)(2,1)S(1)}, u32[]{:S(2)}, u32[]{:S(2)}) collective-permute-start(bf16[48,816]{1,0:T(8,128)(2,1)S(1)} %add_convert_fusion.own_ref), channel_id=1, source_target_pairs={{0,192},{64,128},{128,64},{192,0},{1,193},{65,129},{129,65},{193,1... | collective-permute-start | bytes 235016 | tf_op jit(solution)/shard_map/ppermute | solution.py:246
  37.4 4.6 %collective-permute-start.8 = (bf16[48,816]{1,0:T(8,128)(2,1)S(1)}, bf16[48,816]{1,0:T(8,128)(2,1)S(1)}, u32[]{:S(2)}, u32[]{:S(2)}) collective-permute-start(bf16[48,816]{1,0:T(8,128)(2,1)S(1)} %add_convert_fusion.own_ref), channel_id=1, source_target_pairs={{0,64},{64,0},{128,192},{192,128},{1,65},{65,1},{129,193},{193,129... | collective-permute-start | bytes 235016 | tf_op jit(solution)/shard_map/ppermute | solution.py:246

commit v3 on v2

--- a/solution.py
+++ b/solution.py
@@ -10,7 +10,6 @@
 WIDE = SPAN + 1
 FULL = 4 * H + 1
 PART = 256
-CHUNKS = 8
 STACK = (0, 1, 2, 3, 4, -1, -2, -3, -4)
 VMEM = pl.BlockSpec(memory_space=pltpu.VMEM)
 HBM = pl.BlockSpec(memory_space=pltpu.HBM)
@@ -85,30 +84,13 @@
     return [dense[h * vectors : (h + 1) * vectors] for h in range(parts)]
 
 
-def own_kernel(
-    rows_hbm, own_hbm, matrix_hbm, swap_ref,
-    matrix_ref, product_ref, present_ref, hot_ref, mask_ref, rows_ref, acc, sems, chunk_sems,
-):
-    width = matrix_ref.shape[0]
-    vectors = own_hbm.shape[0]
-    chunks = chunk_sems.shape[0]
-    depth = width // chunks
-    rows_copy = pltpu.make_async_copy(rows_hbm, rows_ref, sems.at[0])
-    own_copy = pltpu.make_async_copy(own_hbm, present_ref.at[pl.ds(0, vectors)], sems.at[1])
-    rows_copy.start()
-    own_copy.start()
-    copies = []
-    for c in range(chunks):
-        part = pl.ds(c * depth, depth)
-        copy = pltpu.make_async_copy(matrix_hbm.at[part], matrix_ref.at[part], chunk_sems.at[c])
-        copy.start()
-        copies.append(copy)
-    me, core, sign = signs()
-
-    rows_copy.wait()
+def hot_kernel(rows_hbm, hot_ref, mask_ref, rows_ref, sem):
+    copy = pltpu.make_async_copy(rows_hbm, rows_ref, sem)
+    copy.start()
+    copy.wait()
     lanes = rows_ref.shape[2]
     index = lax.broadcasted_iota(jnp.int32, (PART, lanes), 0)
-    parts = lax.broadcasted_iota(jnp.int32, (width // PART, lanes), 0)
+    parts = lax.broadcasted_iota(jnp.int32, (mask_ref.shape[1], lanes), 0)
     for slot in range(rows_ref.shape[0]):
         low = rows_ref[slot] & (PART - 1)
         high = rows_ref[slot] // PART
@@ -116,29 +98,39 @@
             place = slice(t * lanes, (t + 1) * lanes)
             hot_ref[slot, :, place] = jnp.where(index == low[t : t + 1], 1.0, 0.0).astype(jnp.bfloat16)
             mask_ref[slot, :, place] = jnp.where(parts == high[t : t + 1], 1.0, 0.0).astype(jnp.bfloat16)
+
+
+def own_kernel(own_hbm, swap_ref, hot_ref, mask_ref, present_ref, sem):
+    vectors = own_hbm.shape[0]
+    own_copy = pltpu.make_async_copy(own_hbm, present_ref.at[pl.ds(0, vectors)], sem)
+    own_copy.start()
+    me, core, sign = signs()
     slot = slot_of(sign, 1)
     for h, block in enumerate(expand(swap_ref[0], hot_ref[slot], mask_ref[slot])):
         present_ref[vectors:, h * PART : (h + 1) * PART] = block
-
     own_copy.wait()
-    for half in range(2):
-        for copy in copies[half * chunks // 2 : (half + 1) * chunks // 2]:
-            copy.wait()
-        part = slice(half * width // 2, (half + 1) * width // 2)
-        term = jnp.dot(
-            present_ref[:, part], matrix_ref[part], preferred_element_type=jnp.float32
-        )
-        if half == 0:
-            acc[...] = term
-        else:
-            product_ref[...] = (acc[...] + term).astype(jnp.bfloat16)
-
-
-def near_kernel(matrix_ref, hot_ref, mask_ref, two_ref, one_ref, present_ref, product_ref):
+
+
+def times_kernel(present_ref, matrix_ref, product_ref):
+    product_ref[...] = jnp.dot(
+        present_ref[...], matrix_ref[...], preferred_element_type=jnp.float32
+    ).astype(jnp.bfloat16)
+
+
+def pair_kernel(hot_ref, mask_ref, two_ref, present_ref):
+    vectors = two_ref.shape[2]
+    me, core, sign = signs()
+    for at, source in enumerate((two_ref.at[1], two_ref.at[0])):
+        slot = slot_of(sign, -3 - at)
+        for h, block in enumerate(expand(source[...], hot_ref[slot], mask_ref[slot])):
+            present_ref[at * vectors : (at + 1) * vectors, h * PART : (h + 1) * PART] = block
+
+
+def near_kernel(matrix_ref, hot_ref, mask_ref, pair_ref, one_ref, present_ref, product_ref):
     vectors = one_ref.shape[2]
     me, core, sign = signs()
-    sources = (one_ref.at[1], one_ref.at[0], two_ref.at[1], two_ref.at[0])
-    for at, source in enumerate(sources):
+    present_ref[2 * vectors :] = pair_ref[...]
+    for at, source in enumerate((one_ref.at[1], one_ref.at[0])):
         slot = slot_of(sign, -1 - at)
         for h, block in enumerate(expand(source[...], hot_ref[slot], mask_ref[slot])):
             present_ref[at * vectors : (at + 1) * vectors, h * PART : (h + 1) * PART] = block
@@ -277,32 +269,55 @@
         name="pick",
     )(in_hbm(neighbours[0, 0]), in_hbm(counts[0, 0]), in_hbm(over))
     swap = partner_swap(give)
+    size = rows.shape[1] * rows.shape[2]
+    hot, mask = pl.pallas_call(
+        hot_kernel,
+        out_shape=(
+            pltpu.VMEM((rows.shape[0], PART, size), bf16),
+            pltpu.VMEM((rows.shape[0], width // PART, size), bf16),
+        ),
+        in_specs=[HBM],
+        out_specs=(VMEM,) * 2,
+        scratch_shapes=[pltpu.VMEM(rows.shape, jnp.int32), pltpu.SemaphoreType.DMA],
+        compiler_params=limit(4),
+        cost_estimate=pl.CostEstimate(flops=10**9, bytes_accessed=2**24, transcendentals=0),
+        name="hot",
+    )(in_hbm(rows))
+    swap, mask = lax.optimization_barrier((swap, mask))
     two = stream(jnp.stack([keep[2], swap[3], swap[4]]), 2)
     one = stream(jnp.stack([keep[0], swap[1], keep[1], swap[2]]), 1)
 
-    loaded, own_product, own_present, hot, mask = pl.pallas_call(
+    own_present = pl.pallas_call(
         own_kernel,
-        out_shape=(
-            pltpu.VMEM((width, width), bf16),
-            pltpu.VMEM((2 * vectors, width), bf16),
-            pltpu.VMEM((2 * vectors, width), bf16),
-            pltpu.VMEM((rows.shape[0], PART, rows.shape[1] * rows.shape[2]), bf16),
-            pltpu.VMEM((rows.shape[0], width // PART, rows.shape[1] * rows.shape[2]), bf16),
-        ),
-        in_specs=[HBM, HBM, HBM, VMEM],
-        out_specs=(VMEM,) * 5,
-        scratch_shapes=[
-            pltpu.VMEM(rows.shape, jnp.int32),
-            pltpu.VMEM((2 * vectors, width), f32),
-            pltpu.SemaphoreType.DMA((2,)),
-            pltpu.SemaphoreType.DMA((CHUNKS,)),
-        ],
-        compiler_params=limit(16),
-        cost_estimate=pl.CostEstimate(flops=10**9, bytes_accessed=10 * 2**20, transcendentals=0),
+        out_shape=pltpu.VMEM((2 * vectors, width), bf16),
+        in_specs=[HBM, VMEM, VMEM, VMEM],
+        out_specs=VMEM,
+        scratch_shapes=[pltpu.SemaphoreType.DMA],
+        compiler_params=limit(8),
+        cost_estimate=pl.CostEstimate(flops=10**9, bytes_accessed=2**24, transcendentals=0),
         name="own",
-    )(in_hbm(rows), in_hbm(own_vectors[0, 0]), in_hbm(matrix), swap)
-
-    two, one, mask = lax.optimization_barrier((two, one, mask))
+    )(in_hbm(own_vectors[0, 0]), swap, hot, mask)
+    loaded = pltpu.with_memory_space_constraint(matrix, pltpu.VMEM)
+    own_product = pl.pallas_call(
+        times_kernel,
+        out_shape=pltpu.VMEM((2 * vectors, width), bf16),
+        in_specs=[VMEM, VMEM],
+        out_specs=VMEM,
+        compiler_params=limit(8),
+        cost_estimate=pl.CostEstimate(flops=10**9, bytes_accessed=2**23, transcendentals=0),
+        name="times",
+    )(own_present, loaded)
+    two, own_product = lax.optimization_barrier((two, own_product))
+    pair = pl.pallas_call(
+        pair_kernel,
+        out_shape=pltpu.VMEM((2 * vectors, width), bf16),
+        in_specs=[VMEM] * 3,
+        out_specs=VMEM,
+        compiler_params=limit(8),
+        cost_estimate=pl.CostEstimate(flops=10**9, bytes_accessed=2**23, transcendentals=0),
+        name="pair",
+    )(hot, mask, two)
+    one, pair = lax.optimization_barrier((one, pair))
     post = partner_swap(jnp.concatenate([two[2:3], one[2:4]]))
 
     near_present, near_product = pl.pallas_call(
@@ -313,7 +328,7 @@
         compiler_params=limit(12),
         cost_estimate=pl.CostEstimate(flops=2 * 10**9, bytes_accessed=2**20, transcendentals=0),
         name="near",
-    )(loaded, hot, mask, two, one)
+    )(loaded, hot, mask, pair, one)
     post, near_product = lax.optimization_barrier((post, near_product))
     far_present, right, back = pl.pallas_call(
         back_kernel,

time: 43.1 us -> 42.3 us (0.981)
  starting transfers between devices: 12.3 us -> 13.7 us
  Pallas kernels: 13 us -> 11.9 us
  waiting for transfers between devices: 17.1 us -> 16.1 us
    ppermute x4, starting transfers between devices: 7.21 us -> 8.65 us  [stream(): return lax.ppermute(block, 'sub', route)]
    ppermute x4, waiting for transfers between devices: 2.88 us -> 1.52 us  [partner_swap(): lax.ppermute(block, 'sub', [(i, i ^ 1) for i in range(lax.axis_size('sub'...]
    pallas_call x1 -> x4, Pallas kernels: 5.14 us -> 4.13 us  [the longest x1 1.46 us: on_device(): pl.pallas_call(times_kernel, out_shape=pltpu.VMEM((2 * vectors, width), b...]
  transfers between devices with their start and end apart: 11 -> 11, of which waited for: 7 -> 8; matrix products, arithmetic and copies ran while one was open for 0% -> 0% of each run, Pallas kernels for 22% -> 19%
where the time goes in v3:
time: 42.3 us; the launch traced here: 42.1 us
  waiting for transfers between devices  16.1 us (38%)
  starting transfers between devices  13.7 us (32%)
  Pallas kernels  11.9 us (28%)
    ppermute x4, waiting for transfers between devices, stream(): return lax.ppermute(block, 'sub', route)  10 us
    ppermute x4, starting transfers between devices, stream(): return lax.ppermute(block, 'sub', route)  8.65 us
    ppermute x3, waiting for transfers between devices, across(): lax.ppermute(block, 'grp', [(i, i ^ bits) for i in range(lax.axis_size('g...  4.55 us
    ppermute x3, starting transfers between devices, across(): lax.ppermute(block, 'grp', [(i, i ^ bits) for i in range(lax.axis_size('g...  4.25 us
    pallas_call x1, Pallas kernels, on_device(): pl.pallas_call(near_kernel, out_shape=(pltpu.VMEM((4 * vectors, width), b...  2.08 us
    pallas_call x1, Pallas kernels, on_device(): pl.pallas_call(ahead_kernel, out_shape=(pltpu.VMEM((2, vectors, WIDE * ve...  1.94 us
    ppermute x4, waiting for transfers between devices, partner_swap(): lax.ppermute(block, 'sub', [(i, i ^ 1) for i in range(lax.axis_size('sub'...  1.52 us
    pallas_call x1, Pallas kernels, on_device(): pl.pallas_call(times_kernel, out_shape=pltpu.VMEM((2 * vectors, width), b...  1.46 us
  transfers between devices with their start and end apart: 11, of which 8 were waited for; matrix products, arithmetic and copies ran while one was open for 0% of the time, Pallas kernels for 19%

profile of v3, /device:TPU:24, one launch (start us, length us, event | category | flops | bytes accessed | tf_op | source)
XLA Modules:
  0.0 42.1 jit_solution(4048553987438079374)
XLA Ops:
  0.0 1.3 %pick.1 = (bf16[5,4,48,128]{3,2,1,0:T(8,128)(2,1)S(1)}, bf16[3,4,48,128]{3,2,1,0:T(8,128)(2,1)S(1)}) custom-call(s32[8]{0:T(128)} %bitcast.13, s32[8]{0:T(128)} %bitcast.14, bf16[8,4,48,128]{3,2,1,0:T(8,128)(2,1)} %bitcast.12), custom_call_target="tpu_custom_call" | custom-call | tf_op jit(solution)/shard_map/pick/pallas_call | solution.py:257
  1.3 0.1 collective-permute-start
  1.4 0.0 copy-start
  1.4 1.3 %hot.1 = (bf16[8,256,512]{2,1,0:T(8,128)(2,1)S(1)}, bf16[8,8,512]{2,1,0:T(8,128)(2,1)S(1)}) custom-call(s32[8,4,128]{2,1,0:T(4,128)} %bitcast.16), custom_call_target="tpu_custom_call" | custom-call | flops 1000000000 | bytes 16777216 | tf_op jit(solution)/shard_map/hot/pallas_call | solution.py:273
  2.7 0.1 collective-permute-done.swap_ref
  2.9 3.3 %collective-permute-start.1 = (bf16[3,4,48,128]{3,2,1,0:T(8,128)(2,1)S(1)}, bf16[3,4,48,128]{3,2,1,0:T(8,128)(2,1)S(1)}, u32[]{:S(2)}, u32[]{:S(2)}) collective-permute-start(bf16[3,4,48,128]{3,2,1,0:T(8,128)(2,1)S(1)} %pad_maximum_fusion.1), channel_id=1, source_target_pairs={{0,4},{1,0},{2,6},{3,2},{4,8},{5,1},{6,10},{7,3},{8,12},{9,5},{10,... | collective-permute-start | bytes 442376 | tf_op jit(solution)/shard_map/ppermute | solution.py:28
  6.3 2.0 %collective-permute-start.2 = (bf16[4,4,48,128]{3,2,1,0:T(8,128)(2,1)S(1)}, bf16[4,4,48,128]{3,2,1,0:T(8,128)(2,1)S(1)}, u32[]{:S(2)}, u32[]{:S(2)}) collective-permute-start(bf16[4,4,48,128]{3,2,1,0:T(8,128)(2,1)S(1)} %pad_maximum_fusion), channel_id=1, source_target_pairs={{0,2},{1,0},{2,4},{3,1},{4,6},{5,3},{6,8},{7,5},{8,10},{9,7},{10,1... | collective-permute-start | bytes 589832 | tf_op jit(solution)/shard_map/ppermute | solution.py:28
  8.3 0.9 %own.1.present_ref.own_present_ref = bf16[96,2048]{1,0:T(8,128)(2,1)S(1)} custom-call(bf16[48,2048]{1,0:T(8,128)(2,1)} %bitcast.15, bf16[5,4,48,128]{3,2,1,0:T(8,128)(2,1)S(1)} %collective-permute-done.swap_ref, bf16[8,256,512]{2,1,0:T(8,128)(2,1)S(1)} %get-tuple-element.32.hot_ref, bf16[8,8,512]{2,1,0:T(8,128)(2,1)S(1)} %get-tuple-element.33.mask_ref), custom_call_target="tpu_custom_call" | custom-call | flops 1000000000 | bytes 16777216 | tf_op jit(solution)/shard_map/own/pallas_call | solution.py:290
  9.2 0.0 copy-done
  9.2 1.5 %times.1.own_product_ref = bf16[96,2048]{1,0:T(8,128)(2,1)S(1)} custom-call(bf16[96,2048]{1,0:T(8,128)(2,1)S(1)} %own.1.present_ref.own_present_ref, bf16[2048,2048]{1,0:T(8,128)(2,1)S(1)} %bitcast.9), custom_call_target="tpu_custom_call" | custom-call | flops 1000000000 | bytes 8388608 | tf_op jit(solution)/shard_map/times/pallas_call | solution.py:301
  10.7 2.0 %collective-permute-done.1.two_ref = bf16[3,4,48,128]{3,2,1,0:T(8,128)(2,1)S(1)} collective-permute-done((bf16[3,4,48,128]{3,2,1,0:T(8,128)(2,1)S(1)}, bf16[3,4,48,128]{3,2,1,0:T(8,128)(2,1)S(1)}, u32[]{:S(2)}, u32[]{:S(2)}) %collective-permute-start.1) | collective-permute-done | bytes 147488 | tf_op jit(solution)/shard_map/ppermute | solution.py:28
  12.7 0.4 pair.1.pair_ref
  13.1 2.7 %collective-permute-done.2.one_ref = bf16[4,4,48,128]{3,2,1,0:T(8,128)(2,1)S(1)} collective-permute-done((bf16[4,4,48,128]{3,2,1,0:T(8,128)(2,1)S(1)}, bf16[4,4,48,128]{3,2,1,0:T(8,128)(2,1)S(1)}, u32[]{:S(2)}, u32[]{:S(2)}) %collective-permute-start.2) | collective-permute-done | bytes 196640 | tf_op jit(solution)/shard_map/ppermute | solution.py:28
  15.9 0.1 collective-permute-start.3
  16.0 2.1 %near.1 = (bf16[192,2048]{1,0:T(8,128)(2,1)S(1)}, bf16[192,2048]{1,0:T(8,128)(2,1)S(1)}) custom-call(bf16[2048,2048]{1,0:T(8,128)(2,1)S(1)} %bitcast.10, bf16[8,256,512]{2,1,0:T(8,128)(2,1)S(1)} %get-tuple-element.32.hot_ref, bf16[8,8,512]{2,1,0:T(8,128)(2,1)S(1)} %get-tuple-element.33.mask_ref, bf16[96,2048]{1,0:T(8,128)(2,1)S(1)} %pair.1.pair_ref, ...), custom_call_target="tpu_custom_call" | custom-call | flops 2000000000 | bytes 1048576 | tf_op jit(solution)/shard_map/near/pallas_call | solution.py:323
  18.1 0.0 collective-permute-done.3.post_ref
  18.1 1.4 %back.1 = (bf16[144,2048]{1,0:T(8,128)(2,1)S(1)}, bf16[480,2048]{1,0:T(8,128)(2,1)S(1)}, bf16[4,48,480]{2,1,0:T(8,128)(2,1)S(1)}) custom-call(bf16[96,2048]{1,0:T(8,128)(2,1)S(1)} %own.1.present_ref.own_present_ref, bf16[192,2048]{1,0:T(8,128)(2,1)S(1)} %get-tuple-element.38.near_present_ref, bf16[192,2048]{1,0:T(8,128)(2,1)S(1)} %get-tuple-element.40.near_product_ref, ...), custom_call_target="tpu_custom_call" | custom-call | flops 1000000000 | bytes 1048576 | tf_op jit(solution)/shard_map/back/pallas_call | solution.py:333
  19.5 0.6 %collective-permute-start.4 = (bf16[4,48,480]{2,1,0:T(8,128)(2,1)S(1)}, bf16[4,48,480]{2,1,0:T(8,128)(2,1)S(1)}, u32[]{:S(2)}, u32[]{:S(2)}) collective-permute-start(bf16[4,48,480]{2,1,0:T(8,128)(2,1)S(1)} %get-tuple-element.45), channel_id=1, source_target_pairs={{0,1},{1,0},{2,3},{3,2},{4,5},{5,4},{6,7},{7,6},{8,9},{9,8},{10,11... | collective-permute-start | bytes 552968 | tf_op jit(solution)/shard_map/ppermute | solution.py:19
  20.1 1.9 %ahead.1 = (f32[2,48,480]{2,1,0:T(8,128)S(1)}, f32[3,48,480]{2,1,0:T(8,128)S(1)}) custom-call(bf16[2048,2048]{1,0:T(8,128)(2,1)S(1)} %bitcast.11, bf16[96,2048]{1,0:T(8,128)(2,1)S(1)} %times.1.own_product_ref, bf16[144,2048]{1,0:T(8,128)(2,1)S(1)} %get-tuple-element.42.far_present_ref, bf16[480,2048]{1,0:T(8,128)(2,1)S(1)} %get-tuple-element.43.right_ref), custom_call_target="tpu_custom_call" | custom-call | flops 2000000000 | bytes 1048576 | tf_op jit(solution)/shard_map/ahead/pallas_call | solution.py:347
  22.0 0.0 collective-permute-done.4
  22.1 0.8 %collective-permute-start.6 = (bf16[2,48,480]{2,1,0:T(8,128)(2,1)S(1)}, bf16[2,48,480]{2,1,0:T(8,128)(2,1)S(1)}, u32[]{:S(2)}, u32[]{:S(2)}) collective-permute-start(bf16[2,48,480]{2,1,0:T(8,128)(2,1)S(1)} %pad_maximum_fusion.3), channel_id=1, source_target_pairs={{0,4},{1,0},{2,6},{3,2},{4,8},{5,1},{6,10},{7,3},{8,12},{9,5},{10,... | collective-permute-start | bytes 276488 | tf_op jit(solution)/shard_map/ppermute | solution.py:28
  23.0 2.5 %collective-permute-start.5 = (bf16[2,48,480]{2,1,0:T(8,128)(2,1)S(1)}, bf16[2,48,480]{2,1,0:T(8,128)(2,1)S(1)}, u32[]{:S(2)}, u32[]{:S(2)}) collective-permute-start(bf16[2,48,480]{2,1,0:T(8,128)(2,1)S(1)} %fusion), channel_id=1, source_target_pairs={{0,2},{1,0},{2,4},{3,1},{4,6},{5,3},{6,8},{7,5},{8,10},{9,7},{10,1... | collective-permute-start | bytes 276488 | tf_op jit(solution)/shard_map/ppermute | solution.py:28
  25.5 4.5 %collective-permute-done.6.two_ref = bf16[2,48,480]{2,1,0:T(8,128)(2,1)S(1)} collective-permute-done((bf16[2,48,480]{2,1,0:T(8,128)(2,1)S(1)}, bf16[2,48,480]{2,1,0:T(8,128)(2,1)S(1)}, u32[]{:S(2)}, u32[]{:S(2)}) %collective-permute-start.6) | collective-permute-done | bytes 92192 | tf_op jit(solution)/shard_map/ppermute | solution.py:28
  30.0 0.8 %collective-permute-done.5.one_ref = bf16[2,48,480]{2,1,0:T(8,128)(2,1)S(1)} collective-permute-done((bf16[2,48,480]{2,1,0:T(8,128)(2,1)S(1)}, bf16[2,48,480]{2,1,0:T(8,128)(2,1)S(1)}, u32[]{:S(2)}, u32[]{:S(2)}) %collective-permute-start.5) | collective-permute-done | bytes 92192 | tf_op jit(solution)/shard_map/ppermute | solution.py:28
  30.8 0.2 window.1
  30.9 0.1 collective-permute-start.7
  31.0 1.4 %collective-permute-done.7 = f32[48,816]{1,0:T(8,128)S(1)} collective-permute-done((f32[48,816]{1,0:T(8,128)S(1)}, f32[48,816]{1,0:T(8,128)S(1)}, u32[]{:S(2)}, u32[]{:S(2)}) %collective-permute-start.7) | collective-permute-done | bytes 156704 | tf_op jit(solution)/shard_map/ppermute | solution.py:19
  32.4 3.1 %collective-permute-start.10 = (bf16[48,816]{1,0:T(8,128)(2,1)S(1)}, bf16[48,816]{1,0:T(8,128)(2,1)S(1)}, u32[]{:S(2)}, u32[]{:S(2)}) collective-permute-start(bf16[48,816]{1,0:T(8,128)(2,1)S(1)} %add_convert_fusion.own_ref), channel_id=1, source_target_pairs={{0,128},{64,192},{128,0},{192,64},{1,129},{65,193},{129,1},{193,65... | collective-permute-start | bytes 235016 | tf_op jit(solution)/shard_map/ppermute | solution.py:238
  35.6 1.1 %collective-permute-start.9 = (bf16[48,816]{1,0:T(8,128)(2,1)S(1)}, bf16[48,816]{1,0:T(8,128)(2,1)S(1)}, u32[]{:S(2)}, u32[]{:S(2)}) collective-permute-start(bf16[48,816]{1,0:T(8,128)(2,1)S(1)} %add_convert_fusion.own_ref), channel_id=1, source_target_pairs={{0,192},{64,128},{128,64},{192,0},{1,193},{65,129},{129,65},{193,1... | collective-permute-start | bytes 235016 | tf_op jit(solution)/shard_map/ppermute | solution.py:238
  36.7 0.0 collective-permute-start.8
  36.7 1.9 %collective-permute-done.10.two_ref = bf16[48,816]{1,0:T(8,128)(2,1)S(1)} collective-permute-done((bf16[48,816]{1,0:T(8,128)(2,1)S(1)}, bf16[48,816]{1,0:T(8,128)(2,1)S(1)}, u32[]{:S(2)}, u32[]{:S(2)}) %collective-permute-start.10) | collective-permute-done | bytes 78368 | tf_op jit(solution)/shard_map/ppermute | solution.py:238
  38.6 2.6 %collective-permute-done.9.three_ref = bf16[48,816]{1,0:T(8,128)(2,1)S(1)} collective-permute-done((bf16[48,816]{1,0:T(8,128)(2,1)S(1)}, bf16[48,816]{1,0:T(8,128)(2,1)S(1)}, u32[]{:S(2)}, u32[]{:S(2)}) %collective-permute-start.9) | collective-permute-done | bytes 78368 | tf_op jit(solution)/shard_map/ppermute | solution.py:238
  41.2 0.0 collective-permute-done.8.one_ref
  41.3 0.9 %spread.1 = f32[4,48,816]{2,1,0:T(8,128)} custom-call(bf16[48,816]{1,0:T(8,128)(2,1)S(1)} %add_convert_fusion.own_ref, bf16[48,816]{1,0:T(8,128)(2,1)S(1)} %collective-permute-done.8.one_ref, bf16[48,816]{1,0:T(8,128)(2,1)S(1)} %collective-permute-done.9.three_ref, bf16[48,816]{1,0:T(8,128)(2,1)S(1)} %collective-permute-done.10.two_ref), custom_call_target="tpu_custom_call" | custom-call | tf_op jit(solution)/shard_map/spread/pallas_call | solution.py:382
  (14 shorter events, 0.2 us)
Async XLA Ops:
  1.3 1.6 %collective-permute-start = (bf16[5,4,48,128]{3,2,1,0:T(8,128)(2,1)S(1)}, bf16[5,4,48,128]{3,2,1,0:T(8,128)(2,1)S(1)}, u32[]{:S(2)}, u32[]{:S(2)}) collective-permute-start(bf16[5,4,48,128]{3,2,1,0:T(8,128)(2,1)S(1)} %get-tuple-element.29), channel_id=1, source_target_pairs={{0,1},{1,0},{2,3},{3,2},{4,5},{5,4},{6,7},{7,6},{8,9},{9,8},{10,11... | collective-permute-start | bytes 737288 | tf_op jit(solution)/shard_map/ppermute | solution.py:19
  1.4 7.9 %copy-start = (bf16[1,1,2048,2048]{3,2,1,0:T(8,128)(2,1)S(1)}, bf16[1,1,2048,2048]{3,2,1,0:T(8,128)(2,1)}, u32[]{:S(2)}) copy-start(bf16[1,1,2048,2048]{3,2,1,0:T(8,128)(2,1)} %param.6) | copy-start | bytes 25165828
  2.9 9.8 %collective-permute-start.1 = (bf16[3,4,48,128]{3,2,1,0:T(8,128)(2,1)S(1)}, bf16[3,4,48,128]{3,2,1,0:T(8,128)(2,1)S(1)}, u32[]{:S(2)}, u32[]{:S(2)}) collective-permute-start(bf16[3,4,48,128]{3,2,1,0:T(8,128)(2,1)S(1)} %pad_maximum_fusion.1), channel_id=1, source_target_pairs={{0,4},{1,0},{2,6},{3,2},{4,8},{5,1},{6,10},{7,3},{8,12},{9,5},{10,... | collective-permute-start | bytes 442376 | tf_op jit(solution)/shard_map/ppermute | solution.py:28
  6.3 9.5 %collective-permute-start.2 = (bf16[4,4,48,128]{3,2,1,0:T(8,128)(2,1)S(1)}, bf16[4,4,48,128]{3,2,1,0:T(8,128)(2,1)S(1)}, u32[]{:S(2)}, u32[]{:S(2)}) collective-permute-start(bf16[4,4,48,128]{3,2,1,0:T(8,128)(2,1)S(1)} %pad_maximum_fusion), channel_id=1, source_target_pairs={{0,2},{1,0},{2,4},{3,1},{4,6},{5,3},{6,8},{7,5},{8,10},{9,7},{10,1... | collective-permute-start | bytes 589832 | tf_op jit(solution)/shard_map/ppermute | solution.py:28
  15.9 2.2 %collective-permute-start.3 = (bf16[3,4,48,128]{3,2,1,0:T(8,128)(2,1)S(1)}, bf16[3,4,48,128]{3,2,1,0:T(8,128)(2,1)S(1)}, u32[]{:S(2)}, u32[]{:S(2)}) collective-permute-start(bf16[3,4,48,128]{3,2,1,0:T(8,128)(2,1)S(1)} %pad_maximum_fusion.2), channel_id=1, source_target_pairs={{0,1},{1,0},{2,3},{3,2},{4,5},{5,4},{6,7},{7,6},{8,9},{9,8},{10,11... | collective-permute-start | bytes 442376 | tf_op jit(solution)/shard_map/ppermute | solution.py:19
  19.5 2.5 %collective-permute-start.4 = (bf16[4,48,480]{2,1,0:T(8,128)(2,1)S(1)}, bf16[4,48,480]{2,1,0:T(8,128)(2,1)S(1)}, u32[]{:S(2)}, u32[]{:S(2)}) collective-permute-start(bf16[4,48,480]{2,1,0:T(8,128)(2,1)S(1)} %get-tuple-element.45), channel_id=1, source_target_pairs={{0,1},{1,0},{2,3},{3,2},{4,5},{5,4},{6,7},{7,6},{8,9},{9,8},{10,11... | collective-permute-start | bytes 552968 | tf_op jit(solution)/shard_map/ppermute | solution.py:19
  22.1 7.8 %collective-permute-start.6 = (bf16[2,48,480]{2,1,0:T(8,128)(2,1)S(1)}, bf16[2,48,480]{2,1,0:T(8,128)(2,1)S(1)}, u32[]{:S(2)}, u32[]{:S(2)}) collective-permute-start(bf16[2,48,480]{2,1,0:T(8,128)(2,1)S(1)} %pad_maximum_fusion.3), channel_id=1, source_target_pairs={{0,4},{1,0},{2,6},{3,2},{4,8},{5,1},{6,10},{7,3},{8,12},{9,5},{10,... | collective-permute-start | bytes 276488 | tf_op jit(solution)/shard_map/ppermute | solution.py:28
  23.0 7.8 %collective-permute-start.5 = (bf16[2,48,480]{2,1,0:T(8,128)(2,1)S(1)}, bf16[2,48,480]{2,1,0:T(8,128)(2,1)S(1)}, u32[]{:S(2)}, u32[]{:S(2)}) collective-permute-start(bf16[2,48,480]{2,1,0:T(8,128)(2,1)S(1)} %fusion), channel_id=1, source_target_pairs={{0,2},{1,0},{2,4},{3,1},{4,6},{5,3},{6,8},{7,5},{8,10},{9,7},{10,1... | collective-permute-start | bytes 276488 | tf_op jit(solution)/shard_map/ppermute | solution.py:28
  30.9 1.5 %collective-permute-start.7 = (f32[48,816]{1,0:T(8,128)S(1)}, f32[48,816]{1,0:T(8,128)S(1)}, u32[]{:S(2)}, u32[]{:S(2)}) collective-permute-start(f32[48,816]{1,0:T(8,128)S(1)} %get-tuple-element.50), channel_id=1, source_target_pairs={{0,1},{1,0},{2,3},{3,2},{4,5},{5,4},{6,7},{7,6},{8,9},{9,8},{10,11... | collective-permute-start | bytes 470024 | tf_op jit(solution)/shard_map/ppermute | solution.py:19
  32.4 6.2 %collective-permute-start.10 = (bf16[48,816]{1,0:T(8,128)(2,1)S(1)}, bf16[48,816]{1,0:T(8,128)(2,1)S(1)}, u32[]{:S(2)}, u32[]{:S(2)}) collective-permute-start(bf16[48,816]{1,0:T(8,128)(2,1)S(1)} %add_convert_fusion.own_ref), channel_id=1, source_target_pairs={{0,128},{64,192},{128,0},{192,64},{1,129},{65,193},{129,1},{193,65... | collective-permute-start | bytes 235016 | tf_op jit(solution)/shard_map/ppermute | solution.py:238
  35.6 5.7 %collective-permute-start.9 = (bf16[48,816]{1,0:T(8,128)(2,1)S(1)}, bf16[48,816]{1,0:T(8,128)(2,1)S(1)}, u32[]{:S(2)}, u32[]{:S(2)}) collective-permute-start(bf16[48,816]{1,0:T(8,128)(2,1)S(1)} %add_convert_fusion.own_ref), channel_id=1, source_target_pairs={{0,192},{64,128},{128,64},{192,0},{1,193},{65,129},{129,65},{193,1... | collective-permute-start | bytes 235016 | tf_op jit(solution)/shard_map/ppermute | solution.py:238
  36.7 4.6 %collective-permute-start.8 = (bf16[48,816]{1,0:T(8,128)(2,1)S(1)}, bf16[48,816]{1,0:T(8,128)(2,1)S(1)}, u32[]{:S(2)}, u32[]{:S(2)}) collective-permute-start(bf16[48,816]{1,0:T(8,128)(2,1)S(1)} %add_convert_fusion.own_ref), channel_id=1, source_target_pairs={{0,64},{64,0},{128,192},{192,128},{1,65},{65,1},{129,193},{193,129... | collective-permute-start | bytes 235016 | tf_op jit(solution)/shard_map/ppermute | solution.py:238

commit v4 on v3

--- a/solution.py
+++ b/solution.py
@@ -77,7 +77,9 @@
     tiles, vectors, lanes = message.shape
     flat = jnp.concatenate([message[t] for t in range(tiles)], axis=1)
     parts = mask.shape[0]
-    spread = jnp.concatenate([flat * mask[h : h + 1] for h in range(parts)], axis=0)
+    spread = jnp.concatenate(
+        [flat * mask[h : h + 1].astype(jnp.bfloat16) for h in range(parts)], axis=0
+    )
     dense = lax.dot_general(
         spread, hot, (((1,), (1,)), ((), ())), preferred_element_type=jnp.float32
     ).astype(jnp.bfloat16)
@@ -97,7 +99,7 @@
         for t in range(rows_ref.shape[1]):
             place = slice(t * lanes, (t + 1) * lanes)
             hot_ref[slot, :, place] = jnp.where(index == low[t : t + 1], 1.0, 0.0).astype(jnp.bfloat16)
-            mask_ref[slot, :, place] = jnp.where(parts == high[t : t + 1], 1.0, 0.0).astype(jnp.bfloat16)
+            mask_ref[slot, :, place] = jnp.where(parts == high[t : t + 1], 1.0, 0.0)
 
 
 def own_kernel(own_hbm, swap_ref, hot_ref, mask_ref, present_ref, sem):
@@ -274,7 +276,7 @@
         hot_kernel,
         out_shape=(
             pltpu.VMEM((rows.shape[0], PART, size), bf16),
-            pltpu.VMEM((rows.shape[0], width // PART, size), bf16),
+            pltpu.VMEM((rows.shape[0], width // PART, size), f32),
         ),
         in_specs=[HBM],
         out_specs=(VMEM,) * 2,

time: 42.3 us -> 42.3 us (level)
  no operation moved by 1% of the time
where the time goes in v4:
time: 42.3 us; the launch traced here: 42.1 us
  waiting for transfers between devices  16.1 us (38%)
  starting transfers between devices  13.8 us (33%)
  Pallas kernels  11.8 us (28%)
    ppermute x4, waiting for transfers between devices, stream(): return lax.ppermute(block, 'sub', route)  10 us
    ppermute x4, starting transfers between devices, stream(): return lax.ppermute(block, 'sub', route)  8.66 us
    ppermute x3, waiting for transfers between devices, across(): lax.ppermute(block, 'grp', [(i, i ^ bits) for i in range(lax.axis_size('g...  4.55 us
    ppermute x3, starting transfers between devices, across(): lax.ppermute(block, 'grp', [(i, i ^ bits) for i in range(lax.axis_size('g...  4.25 us
    pallas_call x1, Pallas kernels, on_device(): pl.pallas_call(near_kernel, out_shape=(pltpu.VMEM((4 * vectors, width), b...  2.08 us
    pallas_call x1, Pallas kernels, on_device(): pl.pallas_call(ahead_kernel, out_shape=(pltpu.VMEM((2, vectors, WIDE * ve...  1.94 us
    ppermute x4, waiting for transfers between devices, partner_swap(): lax.ppermute(block, 'sub', [(i, i ^ 1) for i in range(lax.axis_size('sub'...  1.52 us
    pallas_call x1, Pallas kernels, on_device(): pl.pallas_call(times_kernel, out_shape=pltpu.VMEM((2 * vectors, width), b...  1.46 us
  transfers between devices with their start and end apart: 11, of which 8 were waited for; matrix products, arithmetic and copies ran while one was open for 0% of the time, Pallas kernels for 19%

profile of v4, /device:TPU:24, one launch (start us, length us, event | category | flops | bytes accessed | tf_op | source)
XLA Modules:
  0.0 42.1 jit_solution(12048377148326265145)
XLA Ops:
  0.0 1.3 %pick.1 = (bf16[5,4,48,128]{3,2,1,0:T(8,128)(2,1)S(1)}, bf16[3,4,48,128]{3,2,1,0:T(8,128)(2,1)S(1)}) custom-call(s32[8]{0:T(128)} %bitcast.13, s32[8]{0:T(128)} %bitcast.14, bf16[8,4,48,128]{3,2,1,0:T(8,128)(2,1)} %bitcast.12), custom_call_target="tpu_custom_call" | custom-call | tf_op jit(solution)/shard_map/pick/pallas_call | solution.py:259
  1.3 0.1 collective-permute-start
  1.4 0.0 copy-start
  1.4 1.3 %hot.1 = (bf16[8,256,512]{2,1,0:T(8,128)(2,1)S(1)}, f32[8,8,512]{2,1,0:T(8,128)S(1)}) custom-call(s32[8,4,128]{2,1,0:T(4,128)} %bitcast.16), custom_call_target="tpu_custom_call" | custom-call | flops 1000000000 | bytes 16777216 | tf_op jit(solution)/shard_map/hot/pallas_call | solution.py:275
  2.7 0.1 collective-permute-done.swap_ref
  2.9 3.3 %collective-permute-start.1 = (bf16[3,4,48,128]{3,2,1,0:T(8,128)(2,1)S(1)}, bf16[3,4,48,128]{3,2,1,0:T(8,128)(2,1)S(1)}, u32[]{:S(2)}, u32[]{:S(2)}) collective-permute-start(bf16[3,4,48,128]{3,2,1,0:T(8,128)(2,1)S(1)} %pad_maximum_fusion.1), channel_id=1, source_target_pairs={{0,4},{1,0},{2,6},{3,2},{4,8},{5,1},{6,10},{7,3},{8,12},{9,5},{10,... | collective-permute-start | bytes 442376 | tf_op jit(solution)/shard_map/ppermute | solution.py:28
  6.3 2.0 %collective-permute-start.2 = (bf16[4,4,48,128]{3,2,1,0:T(8,128)(2,1)S(1)}, bf16[4,4,48,128]{3,2,1,0:T(8,128)(2,1)S(1)}, u32[]{:S(2)}, u32[]{:S(2)}) collective-permute-start(bf16[4,4,48,128]{3,2,1,0:T(8,128)(2,1)S(1)} %pad_maximum_fusion), channel_id=1, source_target_pairs={{0,2},{1,0},{2,4},{3,1},{4,6},{5,3},{6,8},{7,5},{8,10},{9,7},{10,1... | collective-permute-start | bytes 589832 | tf_op jit(solution)/shard_map/ppermute | solution.py:28
  8.3 0.9 %own.1.present_ref.own_present_ref = bf16[96,2048]{1,0:T(8,128)(2,1)S(1)} custom-call(bf16[48,2048]{1,0:T(8,128)(2,1)} %bitcast.15, bf16[5,4,48,128]{3,2,1,0:T(8,128)(2,1)S(1)} %collective-permute-done.swap_ref, bf16[8,256,512]{2,1,0:T(8,128)(2,1)S(1)} %get-tuple-element.32.hot_ref, f32[8,8,512]{2,1,0:T(8,128)S(1)} %get-tuple-element.33.mask_ref), custom_call_target="tpu_custom_call" | custom-call | flops 1000000000 | bytes 16777216 | tf_op jit(solution)/shard_map/own/pallas_call | solution.py:292
  9.2 0.0 copy-done
  9.2 1.5 %times.1.own_product_ref = bf16[96,2048]{1,0:T(8,128)(2,1)S(1)} custom-call(bf16[96,2048]{1,0:T(8,128)(2,1)S(1)} %own.1.present_ref.own_present_ref, bf16[2048,2048]{1,0:T(8,128)(2,1)S(1)} %bitcast.9), custom_call_target="tpu_custom_call" | custom-call | flops 1000000000 | bytes 8388608 | tf_op jit(solution)/shard_map/times/pallas_call | solution.py:303
  10.7 2.0 %collective-permute-done.1.two_ref = bf16[3,4,48,128]{3,2,1,0:T(8,128)(2,1)S(1)} collective-permute-done((bf16[3,4,48,128]{3,2,1,0:T(8,128)(2,1)S(1)}, bf16[3,4,48,128]{3,2,1,0:T(8,128)(2,1)S(1)}, u32[]{:S(2)}, u32[]{:S(2)}) %collective-permute-start.1) | collective-permute-done | bytes 147488 | tf_op jit(solution)/shard_map/ppermute | solution.py:28
  12.7 0.4 pair.1.pair_ref
  13.1 2.7 %collective-permute-done.2.one_ref = bf16[4,4,48,128]{3,2,1,0:T(8,128)(2,1)S(1)} collective-permute-done((bf16[4,4,48,128]{3,2,1,0:T(8,128)(2,1)S(1)}, bf16[4,4,48,128]{3,2,1,0:T(8,128)(2,1)S(1)}, u32[]{:S(2)}, u32[]{:S(2)}) %collective-permute-start.2) | collective-permute-done | bytes 196640 | tf_op jit(solution)/shard_map/ppermute | solution.py:28
  15.9 0.1 collective-permute-start.3
  16.0 2.1 %near.1 = (bf16[192,2048]{1,0:T(8,128)(2,1)S(1)}, bf16[192,2048]{1,0:T(8,128)(2,1)S(1)}) custom-call(bf16[2048,2048]{1,0:T(8,128)(2,1)S(1)} %bitcast.10, bf16[8,256,512]{2,1,0:T(8,128)(2,1)S(1)} %get-tuple-element.32.hot_ref, f32[8,8,512]{2,1,0:T(8,128)S(1)} %get-tuple-element.33.mask_ref, bf16[96,2048]{1,0:T(8,128)(2,1)S(1)} %pair.1.pair_ref, ...), custom_call_target="tpu_custom_call" | custom-call | flops 2000000000 | bytes 1048576 | tf_op jit(solution)/shard_map/near/pallas_call | solution.py:325
  18.1 0.0 collective-permute-done.3.post_ref
  18.1 1.4 %back.1 = (bf16[144,2048]{1,0:T(8,128)(2,1)S(1)}, bf16[480,2048]{1,0:T(8,128)(2,1)S(1)}, bf16[4,48,480]{2,1,0:T(8,128)(2,1)S(1)}) custom-call(bf16[96,2048]{1,0:T(8,128)(2,1)S(1)} %own.1.present_ref.own_present_ref, bf16[192,2048]{1,0:T(8,128)(2,1)S(1)} %get-tuple-element.38.near_present_ref, bf16[192,2048]{1,0:T(8,128)(2,1)S(1)} %get-tuple-element.40.near_product_ref, ...), custom_call_target="tpu_custom_call" | custom-call | flops 1000000000 | bytes 1048576 | tf_op jit(solution)/shard_map/back/pallas_call | solution.py:335
  19.5 0.6 %collective-permute-start.4 = (bf16[4,48,480]{2,1,0:T(8,128)(2,1)S(1)}, bf16[4,48,480]{2,1,0:T(8,128)(2,1)S(1)}, u32[]{:S(2)}, u32[]{:S(2)}) collective-permute-start(bf16[4,48,480]{2,1,0:T(8,128)(2,1)S(1)} %get-tuple-element.45), channel_id=1, source_target_pairs={{0,1},{1,0},{2,3},{3,2},{4,5},{5,4},{6,7},{7,6},{8,9},{9,8},{10,11... | collective-permute-start | bytes 552968 | tf_op jit(solution)/shard_map/ppermute | solution.py:19
  20.0 1.9 %ahead.1 = (f32[2,48,480]{2,1,0:T(8,128)S(1)}, f32[3,48,480]{2,1,0:T(8,128)S(1)}) custom-call(bf16[2048,2048]{1,0:T(8,128)(2,1)S(1)} %bitcast.11, bf16[96,2048]{1,0:T(8,128)(2,1)S(1)} %times.1.own_product_ref, bf16[144,2048]{1,0:T(8,128)(2,1)S(1)} %get-tuple-element.42.far_present_ref, bf16[480,2048]{1,0:T(8,128)(2,1)S(1)} %get-tuple-element.43.right_ref), custom_call_target="tpu_custom_call" | custom-call | flops 2000000000 | bytes 1048576 | tf_op jit(solution)/shard_map/ahead/pallas_call | solution.py:349
  22.0 0.0 collective-permute-done.4
  22.1 0.8 %collective-permute-start.6 = (bf16[2,48,480]{2,1,0:T(8,128)(2,1)S(1)}, bf16[2,48,480]{2,1,0:T(8,128)(2,1)S(1)}, u32[]{:S(2)}, u32[]{:S(2)}) collective-permute-start(bf16[2,48,480]{2,1,0:T(8,128)(2,1)S(1)} %pad_maximum_fusion.3), channel_id=1, source_target_pairs={{0,4},{1,0},{2,6},{3,2},{4,8},{5,1},{6,10},{7,3},{8,12},{9,5},{10,... | collective-permute-start | bytes 276488 | tf_op jit(solution)/shard_map/ppermute | solution.py:28
  23.0 2.5 %collective-permute-start.5 = (bf16[2,48,480]{2,1,0:T(8,128)(2,1)S(1)}, bf16[2,48,480]{2,1,0:T(8,128)(2,1)S(1)}, u32[]{:S(2)}, u32[]{:S(2)}) collective-permute-start(bf16[2,48,480]{2,1,0:T(8,128)(2,1)S(1)} %fusion), channel_id=1, source_target_pairs={{0,2},{1,0},{2,4},{3,1},{4,6},{5,3},{6,8},{7,5},{8,10},{9,7},{10,1... | collective-permute-start | bytes 276488 | tf_op jit(solution)/shard_map/ppermute | solution.py:28
  25.5 4.5 %collective-permute-done.6.two_ref = bf16[2,48,480]{2,1,0:T(8,128)(2,1)S(1)} collective-permute-done((bf16[2,48,480]{2,1,0:T(8,128)(2,1)S(1)}, bf16[2,48,480]{2,1,0:T(8,128)(2,1)S(1)}, u32[]{:S(2)}, u32[]{:S(2)}) %collective-permute-start.6) | collective-permute-done | bytes 92192 | tf_op jit(solution)/shard_map/ppermute | solution.py:28
  29.9 0.8 %collective-permute-done.5.one_ref = bf16[2,48,480]{2,1,0:T(8,128)(2,1)S(1)} collective-permute-done((bf16[2,48,480]{2,1,0:T(8,128)(2,1)S(1)}, bf16[2,48,480]{2,1,0:T(8,128)(2,1)S(1)}, u32[]{:S(2)}, u32[]{:S(2)}) %collective-permute-start.5) | collective-permute-done | bytes 92192 | tf_op jit(solution)/shard_map/ppermute | solution.py:28
  30.7 0.2 window.1
  30.9 0.1 collective-permute-start.7
  31.0 1.4 %collective-permute-done.7 = f32[48,816]{1,0:T(8,128)S(1)} collective-permute-done((f32[48,816]{1,0:T(8,128)S(1)}, f32[48,816]{1,0:T(8,128)S(1)}, u32[]{:S(2)}, u32[]{:S(2)}) %collective-permute-start.7) | collective-permute-done | bytes 156704 | tf_op jit(solution)/shard_map/ppermute | solution.py:19
  32.4 3.1 %collective-permute-start.10 = (bf16[48,816]{1,0:T(8,128)(2,1)S(1)}, bf16[48,816]{1,0:T(8,128)(2,1)S(1)}, u32[]{:S(2)}, u32[]{:S(2)}) collective-permute-start(bf16[48,816]{1,0:T(8,128)(2,1)S(1)} %add_convert_fusion.own_ref), channel_id=1, source_target_pairs={{0,128},{64,192},{128,0},{192,64},{1,129},{65,193},{129,1},{193,65... | collective-permute-start | bytes 235016 | tf_op jit(solution)/shard_map/ppermute | solution.py:240
  35.5 1.1 %collective-permute-start.9 = (bf16[48,816]{1,0:T(8,128)(2,1)S(1)}, bf16[48,816]{1,0:T(8,128)(2,1)S(1)}, u32[]{:S(2)}, u32[]{:S(2)}) collective-permute-start(bf16[48,816]{1,0:T(8,128)(2,1)S(1)} %add_convert_fusion.own_ref), channel_id=1, source_target_pairs={{0,192},{64,128},{128,64},{192,0},{1,193},{65,129},{129,65},{193,1... | collective-permute-start | bytes 235016 | tf_op jit(solution)/shard_map/ppermute | solution.py:240
  36.7 0.0 collective-permute-start.8
  36.7 1.9 %collective-permute-done.10.two_ref = bf16[48,816]{1,0:T(8,128)(2,1)S(1)} collective-permute-done((bf16[48,816]{1,0:T(8,128)(2,1)S(1)}, bf16[48,816]{1,0:T(8,128)(2,1)S(1)}, u32[]{:S(2)}, u32[]{:S(2)}) %collective-permute-start.10) | collective-permute-done | bytes 78368 | tf_op jit(solution)/shard_map/ppermute | solution.py:240
  38.6 2.6 %collective-permute-done.9.three_ref = bf16[48,816]{1,0:T(8,128)(2,1)S(1)} collective-permute-done((bf16[48,816]{1,0:T(8,128)(2,1)S(1)}, bf16[48,816]{1,0:T(8,128)(2,1)S(1)}, u32[]{:S(2)}, u32[]{:S(2)}) %collective-permute-start.9) | collective-permute-done | bytes 78368 | tf_op jit(solution)/shard_map/ppermute | solution.py:240
  41.2 0.0 collective-permute-done.8.one_ref
  41.2 0.9 %spread.1 = f32[4,48,816]{2,1,0:T(8,128)} custom-call(bf16[48,816]{1,0:T(8,128)(2,1)S(1)} %add_convert_fusion.own_ref, bf16[48,816]{1,0:T(8,128)(2,1)S(1)} %collective-permute-done.8.one_ref, bf16[48,816]{1,0:T(8,128)(2,1)S(1)} %collective-permute-done.9.three_ref, bf16[48,816]{1,0:T(8,128)(2,1)S(1)} %collective-permute-done.10.two_ref), custom_call_target="tpu_custom_call" | custom-call | tf_op jit(solution)/shard_map/spread/pallas_call | solution.py:384
  (14 shorter events, 0.2 us)
Async XLA Ops:
  1.3 1.6 %collective-permute-start = (bf16[5,4,48,128]{3,2,1,0:T(8,128)(2,1)S(1)}, bf16[5,4,48,128]{3,2,1,0:T(8,128)(2,1)S(1)}, u32[]{:S(2)}, u32[]{:S(2)}) collective-permute-start(bf16[5,4,48,128]{3,2,1,0:T(8,128)(2,1)S(1)} %get-tuple-element.29), channel_id=1, source_target_pairs={{0,1},{1,0},{2,3},{3,2},{4,5},{5,4},{6,7},{7,6},{8,9},{9,8},{10,11... | collective-permute-start | bytes 737288 | tf_op jit(solution)/shard_map/ppermute | solution.py:19
  1.4 7.9 %copy-start = (bf16[1,1,2048,2048]{3,2,1,0:T(8,128)(2,1)S(1)}, bf16[1,1,2048,2048]{3,2,1,0:T(8,128)(2,1)}, u32[]{:S(2)}) copy-start(bf16[1,1,2048,2048]{3,2,1,0:T(8,128)(2,1)} %param.6) | copy-start | bytes 25165828
  2.9 9.8 %collective-permute-start.1 = (bf16[3,4,48,128]{3,2,1,0:T(8,128)(2,1)S(1)}, bf16[3,4,48,128]{3,2,1,0:T(8,128)(2,1)S(1)}, u32[]{:S(2)}, u32[]{:S(2)}) collective-permute-start(bf16[3,4,48,128]{3,2,1,0:T(8,128)(2,1)S(1)} %pad_maximum_fusion.1), channel_id=1, source_target_pairs={{0,4},{1,0},{2,6},{3,2},{4,8},{5,1},{6,10},{7,3},{8,12},{9,5},{10,... | collective-permute-start | bytes 442376 | tf_op jit(solution)/shard_map/ppermute | solution.py:28
  6.3 9.5 %collective-permute-start.2 = (bf16[4,4,48,128]{3,2,1,0:T(8,128)(2,1)S(1)}, bf16[4,4,48,128]{3,2,1,0:T(8,128)(2,1)S(1)}, u32[]{:S(2)}, u32[]{:S(2)}) collective-permute-start(bf16[4,4,48,128]{3,2,1,0:T(8,128)(2,1)S(1)} %pad_maximum_fusion), channel_id=1, source_target_pairs={{0,2},{1,0},{2,4},{3,1},{4,6},{5,3},{6,8},{7,5},{8,10},{9,7},{10,1... | collective-permute-start | bytes 589832 | tf_op jit(solution)/shard_map/ppermute | solution.py:28
  15.9 2.2 %collective-permute-start.3 = (bf16[3,4,48,128]{3,2,1,0:T(8,128)(2,1)S(1)}, bf16[3,4,48,128]{3,2,1,0:T(8,128)(2,1)S(1)}, u32[]{:S(2)}, u32[]{:S(2)}) collective-permute-start(bf16[3,4,48,128]{3,2,1,0:T(8,128)(2,1)S(1)} %pad_maximum_fusion.2), channel_id=1, source_target_pairs={{0,1},{1,0},{2,3},{3,2},{4,5},{5,4},{6,7},{7,6},{8,9},{9,8},{10,11... | collective-permute-start | bytes 442376 | tf_op jit(solution)/shard_map/ppermute | solution.py:19
  19.5 2.5 %collective-permute-start.4 = (bf16[4,48,480]{2,1,0:T(8,128)(2,1)S(1)}, bf16[4,48,480]{2,1,0:T(8,128)(2,1)S(1)}, u32[]{:S(2)}, u32[]{:S(2)}) collective-permute-start(bf16[4,48,480]{2,1,0:T(8,128)(2,1)S(1)} %get-tuple-element.45), channel_id=1, source_target_pairs={{0,1},{1,0},{2,3},{3,2},{4,5},{5,4},{6,7},{7,6},{8,9},{9,8},{10,11... | collective-permute-start | bytes 552968 | tf_op jit(solution)/shard_map/ppermute | solution.py:19
  22.1 7.8 %collective-permute-start.6 = (bf16[2,48,480]{2,1,0:T(8,128)(2,1)S(1)}, bf16[2,48,480]{2,1,0:T(8,128)(2,1)S(1)}, u32[]{:S(2)}, u32[]{:S(2)}) collective-permute-start(bf16[2,48,480]{2,1,0:T(8,128)(2,1)S(1)} %pad_maximum_fusion.3), channel_id=1, source_target_pairs={{0,4},{1,0},{2,6},{3,2},{4,8},{5,1},{6,10},{7,3},{8,12},{9,5},{10,... | collective-permute-start | bytes 276488 | tf_op jit(solution)/shard_map/ppermute | solution.py:28
  23.0 7.8 %collective-permute-start.5 = (bf16[2,48,480]{2,1,0:T(8,128)(2,1)S(1)}, bf16[2,48,480]{2,1,0:T(8,128)(2,1)S(1)}, u32[]{:S(2)}, u32[]{:S(2)}) collective-permute-start(bf16[2,48,480]{2,1,0:T(8,128)(2,1)S(1)} %fusion), channel_id=1, source_target_pairs={{0,2},{1,0},{2,4},{3,1},{4,6},{5,3},{6,8},{7,5},{8,10},{9,7},{10,1... | collective-permute-start | bytes 276488 | tf_op jit(solution)/shard_map/ppermute | solution.py:28
  30.9 1.5 %collective-permute-start.7 = (f32[48,816]{1,0:T(8,128)S(1)}, f32[48,816]{1,0:T(8,128)S(1)}, u32[]{:S(2)}, u32[]{:S(2)}) collective-permute-start(f32[48,816]{1,0:T(8,128)S(1)} %get-tuple-element.50), channel_id=1, source_target_pairs={{0,1},{1,0},{2,3},{3,2},{4,5},{5,4},{6,7},{7,6},{8,9},{9,8},{10,11... | collective-permute-start | bytes 470024 | tf_op jit(solution)/shard_map/ppermute | solution.py:19
  32.4 6.2 %collective-permute-start.10 = (bf16[48,816]{1,0:T(8,128)(2,1)S(1)}, bf16[48,816]{1,0:T(8,128)(2,1)S(1)}, u32[]{:S(2)}, u32[]{:S(2)}) collective-permute-start(bf16[48,816]{1,0:T(8,128)(2,1)S(1)} %add_convert_fusion.own_ref), channel_id=1, source_target_pairs={{0,128},{64,192},{128,0},{192,64},{1,129},{65,193},{129,1},{193,65... | collective-permute-start | bytes 235016 | tf_op jit(solution)/shard_map/ppermute | solution.py:240
  35.5 5.7 %collective-permute-start.9 = (bf16[48,816]{1,0:T(8,128)(2,1)S(1)}, bf16[48,816]{1,0:T(8,128)(2,1)S(1)}, u32[]{:S(2)}, u32[]{:S(2)}) collective-permute-start(bf16[48,816]{1,0:T(8,128)(2,1)S(1)} %add_convert_fusion.own_ref), channel_id=1, source_target_pairs={{0,192},{64,128},{128,64},{192,0},{1,193},{65,129},{129,65},{193,1... | collective-permute-start | bytes 235016 | tf_op jit(solution)/shard_map/ppermute | solution.py:240
  36.7 4.6 %collective-permute-start.8 = (bf16[48,816]{1,0:T(8,128)(2,1)S(1)}, bf16[48,816]{1,0:T(8,128)(2,1)S(1)}, u32[]{:S(2)}, u32[]{:S(2)}) collective-permute-start(bf16[48,816]{1,0:T(8,128)(2,1)S(1)} %add_convert_fusion.own_ref), channel_id=1, source_target_pairs={{0,64},{64,0},{128,192},{192,128},{1,65},{65,1},{129,193},{193,129... | collective-permute-start | bytes 235016 | tf_op jit(solution)/shard_map/ppermute | solution.py:240

commit v5 on v4

--- a/solution.py
+++ b/solution.py
@@ -119,13 +119,24 @@
     ).astype(jnp.bfloat16)
 
 
-def pair_kernel(hot_ref, mask_ref, two_ref, present_ref):
+def right_rows(core, k, vectors):
+    position = jnp.where(core == 0, H + k, H + 1 - k)
+    return pl.ds(pl.multiple_of(position * vectors, vectors), vectors)
+
+
+def pair_kernel(own_present_ref, hot_ref, mask_ref, two_ref, present_ref, right_ref):
     vectors = two_ref.shape[2]
     me, core, sign = signs()
+    right_ref[right_rows(core, H + 1, vectors)] = jnp.zeros(
+        (vectors, right_ref.shape[1]), jnp.bfloat16
+    )
+    for at in range(2):
+        right_ref[right_rows(core, at, vectors)] = own_present_ref[at * vectors : (at + 1) * vectors]
     for at, source in enumerate((two_ref.at[1], two_ref.at[0])):
         slot = slot_of(sign, -3 - at)
         for h, block in enumerate(expand(source[...], hot_ref[slot], mask_ref[slot])):
             present_ref[at * vectors : (at + 1) * vectors, h * PART : (h + 1) * PART] = block
+            right_ref[right_rows(core, -3 - at, vectors), h * PART : (h + 1) * PART] = block
 
 
 def near_kernel(matrix_ref, hot_ref, mask_ref, pair_ref, one_ref, present_ref, product_ref):
@@ -148,28 +159,21 @@
 
 
 def back_kernel(
-    own_present_ref, near_present_ref, near_product_ref, hot_ref, mask_ref, post_ref,
+    early_ref, near_present_ref, near_product_ref, hot_ref, mask_ref, post_ref,
     far_present_ref, right_ref, back_ref,
 ):
     vectors = post_ref.shape[2]
     width = right_ref.shape[1]
     me, core, sign = signs()
 
-    def right_rows(k):
-        position = jnp.where(core == 0, H + k, H + 1 - k)
-        return pl.ds(pl.multiple_of(position * vectors, vectors), vectors)
-
-    right_ref[right_rows(H + 1)] = jnp.zeros((vectors, width), jnp.bfloat16)
     for at in range(2):
-        right_ref[right_rows(at)] = own_present_ref[at * vectors : (at + 1) * vectors]
-    for at in range(4):
-        right_ref[right_rows(-1 - at)] = near_present_ref[at * vectors : (at + 1) * vectors]
+        right_ref[right_rows(core, -1 - at, vectors)] = near_present_ref[at * vectors : (at + 1) * vectors]
     for at, source in enumerate((post_ref.at[2], post_ref.at[1], post_ref.at[0])):
         slot = slot_of(sign, 2 + at)
         for h, block in enumerate(expand(source[...], hot_ref[slot], mask_ref[slot])):
             place = slice(h * PART, (h + 1) * PART)
             far_present_ref[at * vectors : (at + 1) * vectors, place] = block
-            right_ref[right_rows(2 + at), place] = block
+            right_ref[right_rows(core, 2 + at, vectors), place] = block
     gram = times_all(near_product_ref[...], right_ref[...]).astype(jnp.bfloat16)
     for at in range(4):
         back_ref[at] = gram[at * vectors : (at + 1) * vectors]
@@ -224,16 +228,24 @@
                 )
 
 
-def spread_kernel(own_ref, one_ref, three_ref, two_ref, out_hbm, wide, sems):
+def write_rows(refs, out_hbm, wide, sems):
     x = lax.axis_index("grp")
     copies = []
-    for d, ref in enumerate((own_ref, one_ref, two_ref, three_ref)):
-        wide[d] = ref[...].astype(jnp.float32)
-        copy = pltpu.make_async_copy(wide.at[d], out_hbm.at[x ^ d], sems.at[d])
+    for n, (bits, ref) in enumerate(refs):
+        wide[n] = ref[...].astype(jnp.float32)
+        copy = pltpu.make_async_copy(wide.at[n], out_hbm.at[x ^ bits], sems.at[n])
         copy.start()
         copies.append(copy)
     for copy in copies:
         copy.wait()
+
+
+def first_kernel(own_ref, two_ref, out_hbm, wide, sems):
+    write_rows(((0, own_ref), (2, two_ref)), out_hbm, wide, sems)
+
+
+def second_kernel(three_ref, one_ref, half_hbm, out_hbm, wide, sems):
+    write_rows(((3, three_ref), (1, one_ref)), out_hbm, wide, sems)
 
 
 def across(block, bits):
@@ -310,15 +322,18 @@
         name="times",
     )(own_present, loaded)
     two, own_product = lax.optimization_barrier((two, own_product))
-    pair = pl.pallas_call(
+    pair, early = pl.pallas_call(
         pair_kernel,
-        out_shape=pltpu.VMEM((2 * vectors, width), bf16),
-        in_specs=[VMEM] * 3,
-        out_specs=VMEM,
+        out_shape=(
+            pltpu.VMEM((2 * vectors, width), bf16),
+            pltpu.VMEM((WIDE * vectors, width), bf16),
+        ),
+        in_specs=[VMEM] * 4,
+        out_specs=(VMEM,) * 2,
         compiler_params=limit(8),
         cost_estimate=pl.CostEstimate(flops=10**9, bytes_accessed=2**23, transcendentals=0),
         name="pair",
-    )(hot, mask, two)
+    )(own_present, hot, mask, two)
     one, pair = lax.optimization_barrier((one, pair))
     post = partner_swap(jnp.concatenate([two[2:3], one[2:4]]))
 
@@ -343,8 +358,9 @@
         out_specs=(VMEM,) * 3,
         compiler_params=limit(12),
         cost_estimate=pl.CostEstimate(flops=10**9, bytes_accessed=2**20, transcendentals=0),
+        input_output_aliases={0: 1},
         name="back",
-    )(own_present, near_present, near_product, hot, mask, post)
+    )(early, near_present, near_product, hot, mask, post)
     reverse = partner_swap(back)
     home, ahead = pl.pallas_call(
         ahead_kernel,
@@ -381,18 +397,28 @@
     across_three = across(coarse, 3)
     across_one = across(coarse, 1)
     count = lax.axis_size("grp")
+    scratch = [pltpu.VMEM((2,) + row.shape, f32), pltpu.SemaphoreType.DMA((2,))]
+    half = pl.pallas_call(
+        first_kernel,
+        out_shape=pltpu.HBM((count,) + row.shape, f32),
+        in_specs=[VMEM] * 2,
+        out_specs=HBM,
+        scratch_shapes=scratch,
+        compiler_params=limit(6),
+        cost_estimate=pl.CostEstimate(flops=10**6, bytes_accessed=2**20, transcendentals=0),
+        name="first",
+    )(coarse, across_two)
+    across_three, half = lax.optimization_barrier((across_three, half))
     gathered = pl.pallas_call(
-        spread_kernel,
+        second_kernel,
         out_shape=pltpu.HBM((count,) + row.shape, f32),
-        in_specs=[VMEM] * 4,
+        in_specs=[VMEM, VMEM, HBM],
         out_specs=HBM,
-        scratch_shapes=[
-            pltpu.VMEM((count,) + row.shape, f32),
-            pltpu.SemaphoreType.DMA((count,)),
-        ],
+        scratch_shapes=scratch,
+        input_output_aliases={2: 0},
         compiler_params=limit(6),
-        name="spread",
-    )(coarse, across_one, across_three, across_two)
+        name="second",
+    )(across_three, across_one, in_hbm(half))
     return gathered[:, None]
 
 

time: 42.3 us -> 42.1 us (level)
  waiting for transfers between devices: 16.1 us -> 15.3 us
  Pallas kernels: 11.8 us -> 12.5 us
    ppermute x3, waiting for transfers between devices: 4.55 us -> 3.79 us  [across(): lax.ppermute(block, 'grp', [(i, i ^ bits) for i in range(lax.axis_size('g...]
    pallas_call x2 -> x3, Pallas kernels: 1.29 us -> 1.94 us  [the longest x1 0.76 us: on_device(): pl.pallas_call(second_kernel, out_shape=pltpu.HBM((count,) + row.shape, f...]
  transfers between devices with their start and end apart: 11 -> 11, of which waited for: 8 -> 8; matrix products, arithmetic and copies ran while one was open for 0% -> 0% of each run, Pallas kernels for 19% -> 21%
where the time goes in v5:
time: 42.1 us; the launch traced here: 42 us
  waiting for transfers between devices  15.3 us (36%)
  starting transfers between devices  13.8 us (33%)
  Pallas kernels  12.5 us (30%)
    ppermute x4, waiting for transfers between devices, stream(): return lax.ppermute(block, 'sub', route)  9.99 us
    ppermute x4, starting transfers between devices, stream(): return lax.ppermute(block, 'sub', route)  8.66 us
    ppermute x3, starting transfers between devices, across(): lax.ppermute(block, 'grp', [(i, i ^ bits) for i in range(lax.axis_size('g...  4.25 us
    ppermute x3, waiting for transfers between devices, across(): lax.ppermute(block, 'grp', [(i, i ^ bits) for i in range(lax.axis_size('g...  3.79 us
    pallas_call x1, Pallas kernels, on_device(): pl.pallas_call(near_kernel, out_shape=(pltpu.VMEM((4 * vectors, width), b...  2.08 us
    pallas_call x1, Pallas kernels, on_device(): pl.pallas_call(ahead_kernel, out_shape=(pltpu.VMEM((2, vectors, WIDE * ve...  1.94 us
    ppermute x4, waiting for transfers between devices, partner_swap(): lax.ppermute(block, 'sub', [(i, i ^ 1) for i in range(lax.axis_size('sub'...  1.52 us
    pallas_call x1, Pallas kernels, on_device(): pl.pallas_call(times_kernel, out_shape=pltpu.VMEM((2 * vectors, width), b...  1.46 us
  transfers between devices with their start and end apart: 11, of which 8 were waited for; matrix products, arithmetic and copies ran while one was open for 0% of the time, Pallas kernels for 21%

profile of v5, /device:TPU:24, one launch (start us, length us, event | category | flops | bytes accessed | tf_op | source)
XLA Modules:
  0.0 42.0 jit_solution(12111863182694918691)
XLA Ops:
  0.0 1.3 %pick.1 = (bf16[5,4,48,128]{3,2,1,0:T(8,128)(2,1)S(1)}, bf16[3,4,48,128]{3,2,1,0:T(8,128)(2,1)S(1)}) custom-call(s32[8]{0:T(128)} %bitcast.13, s32[8]{0:T(128)} %bitcast.14, bf16[8,4,48,128]{3,2,1,0:T(8,128)(2,1)} %bitcast.12), custom_call_target="tpu_custom_call" | custom-call | tf_op jit(solution)/shard_map/pick/pallas_call | solution.py:271
  1.3 0.1 collective-permute-start
  1.4 0.0 copy-start
  1.4 1.3 %hot.1 = (bf16[8,256,512]{2,1,0:T(8,128)(2,1)S(1)}, f32[8,8,512]{2,1,0:T(8,128)S(1)}) custom-call(s32[8,4,128]{2,1,0:T(4,128)} %bitcast.16), custom_call_target="tpu_custom_call" | custom-call | flops 1000000000 | bytes 16777216 | tf_op jit(solution)/shard_map/hot/pallas_call | solution.py:287
  2.7 0.1 collective-permute-done.swap_ref
  2.9 3.3 %collective-permute-start.1 = (bf16[3,4,48,128]{3,2,1,0:T(8,128)(2,1)S(1)}, bf16[3,4,48,128]{3,2,1,0:T(8,128)(2,1)S(1)}, u32[]{:S(2)}, u32[]{:S(2)}) collective-permute-start(bf16[3,4,48,128]{3,2,1,0:T(8,128)(2,1)S(1)} %pad_maximum_fusion.1), channel_id=1, source_target_pairs={{0,4},{1,0},{2,6},{3,2},{4,8},{5,1},{6,10},{7,3},{8,12},{9,5},{10,... | collective-permute-start | bytes 442376 | tf_op jit(solution)/shard_map/ppermute | solution.py:28
  6.3 2.0 %collective-permute-start.2 = (bf16[4,4,48,128]{3,2,1,0:T(8,128)(2,1)S(1)}, bf16[4,4,48,128]{3,2,1,0:T(8,128)(2,1)S(1)}, u32[]{:S(2)}, u32[]{:S(2)}) collective-permute-start(bf16[4,4,48,128]{3,2,1,0:T(8,128)(2,1)S(1)} %pad_maximum_fusion), channel_id=1, source_target_pairs={{0,2},{1,0},{2,4},{3,1},{4,6},{5,3},{6,8},{7,5},{8,10},{9,7},{10,1... | collective-permute-start | bytes 589832 | tf_op jit(solution)/shard_map/ppermute | solution.py:28
  8.3 0.9 %own.1.present_ref.own_present_ref = bf16[96,2048]{1,0:T(8,128)(2,1)S(1)} custom-call(bf16[48,2048]{1,0:T(8,128)(2,1)} %bitcast.15, bf16[5,4,48,128]{3,2,1,0:T(8,128)(2,1)S(1)} %collective-permute-done.swap_ref, bf16[8,256,512]{2,1,0:T(8,128)(2,1)S(1)} %get-tuple-element.36.hot_ref, f32[8,8,512]{2,1,0:T(8,128)S(1)} %get-tuple-element.37.mask_ref), custom_call_target="tpu_custom_call" | custom-call | flops 1000000000 | bytes 16777216 | tf_op jit(solution)/shard_map/own/pallas_call | solution.py:304
  9.2 0.0 copy-done
  9.2 1.5 %times.1.own_product_ref = bf16[96,2048]{1,0:T(8,128)(2,1)S(1)} custom-call(bf16[96,2048]{1,0:T(8,128)(2,1)S(1)} %own.1.present_ref.own_present_ref, bf16[2048,2048]{1,0:T(8,128)(2,1)S(1)} %bitcast.9), custom_call_target="tpu_custom_call" | custom-call | flops 1000000000 | bytes 8388608 | tf_op jit(solution)/shard_map/times/pallas_call | solution.py:315
  10.7 2.0 %collective-permute-done.1.two_ref = bf16[3,4,48,128]{3,2,1,0:T(8,128)(2,1)S(1)} collective-permute-done((bf16[3,4,48,128]{3,2,1,0:T(8,128)(2,1)S(1)}, bf16[3,4,48,128]{3,2,1,0:T(8,128)(2,1)S(1)}, u32[]{:S(2)}, u32[]{:S(2)}) %collective-permute-start.1) | collective-permute-done | bytes 147488 | tf_op jit(solution)/shard_map/ppermute | solution.py:28
  12.7 0.4 %pair.1 = (bf16[96,2048]{1,0:T(8,128)(2,1)S(1)}, bf16[480,2048]{1,0:T(8,128)(2,1)S(1)}) custom-call(bf16[96,2048]{1,0:T(8,128)(2,1)S(1)} %own.1.present_ref.own_present_ref, bf16[8,256,512]{2,1,0:T(8,128)(2,1)S(1)} %get-tuple-element.36.hot_ref, f32[8,8,512]{2,1,0:T(8,128)S(1)} %get-tuple-element.37.mask_ref, ...), custom_call_target="tpu_custom_call" | custom-call | flops 1000000000 | bytes 8388608 | tf_op jit(solution)/shard_map/pair/pallas_call | solution.py:325
  13.1 2.7 %collective-permute-done.2.one_ref = bf16[4,4,48,128]{3,2,1,0:T(8,128)(2,1)S(1)} collective-permute-done((bf16[4,4,48,128]{3,2,1,0:T(8,128)(2,1)S(1)}, bf16[4,4,48,128]{3,2,1,0:T(8,128)(2,1)S(1)}, u32[]{:S(2)}, u32[]{:S(2)}) %collective-permute-start.2) | collective-permute-done | bytes 196640 | tf_op jit(solution)/shard_map/ppermute | solution.py:28
  15.9 0.1 collective-permute-start.3
  16.0 2.1 %near.1 = (bf16[192,2048]{1,0:T(8,128)(2,1)S(1)}, bf16[192,2048]{1,0:T(8,128)(2,1)S(1)}) custom-call(bf16[2048,2048]{1,0:T(8,128)(2,1)S(1)} %bitcast.10, bf16[8,256,512]{2,1,0:T(8,128)(2,1)S(1)} %get-tuple-element.36.hot_ref, f32[8,8,512]{2,1,0:T(8,128)S(1)} %get-tuple-element.37.mask_ref, bf16[96,2048]{1,0:T(8,128)(2,1)S(1)} %get-tuple-element.42.pair_ref, ...), custom_call_target="tpu_custom_call" | custom-call | flops 2000000000 | bytes 1048576 | tf_op jit(solution)/shard_map/near/pallas_call | solution.py:340
  18.1 0.0 collective-permute-done.3.post_ref
  18.1 1.4 %back.1 = (bf16[144,2048]{1,0:T(8,128)(2,1)S(1)}, bf16[480,2048]{1,0:T(8,128)(2,1)S(1)}, bf16[4,48,480]{2,1,0:T(8,128)(2,1)S(1)}) custom-call(bf16[480,2048]{1,0:T(8,128)(2,1)S(1)} %get-tuple-element.40.early_ref, bf16[192,2048]{1,0:T(8,128)(2,1)S(1)} %get-tuple-element.44.near_present_ref, ...), custom_call_target="tpu_custom_call", output_to_operand_aliasing={{1}: (0, {})} | custom-call | flops 1000000000 | bytes 1048576 | tf_op jit(solution)/shard_map/back/pallas_call | solution.py:350
  19.4 0.6 %collective-permute-start.4 = (bf16[4,48,480]{2,1,0:T(8,128)(2,1)S(1)}, bf16[4,48,480]{2,1,0:T(8,128)(2,1)S(1)}, u32[]{:S(2)}, u32[]{:S(2)}) collective-permute-start(bf16[4,48,480]{2,1,0:T(8,128)(2,1)S(1)} %get-tuple-element.51), channel_id=1, source_target_pairs={{0,1},{1,0},{2,3},{3,2},{4,5},{5,4},{6,7},{7,6},{8,9},{9,8},{10,11... | collective-permute-start | bytes 552968 | tf_op jit(solution)/shard_map/ppermute | solution.py:19
  20.0 1.9 %ahead.1 = (f32[2,48,480]{2,1,0:T(8,128)S(1)}, f32[3,48,480]{2,1,0:T(8,128)S(1)}) custom-call(bf16[2048,2048]{1,0:T(8,128)(2,1)S(1)} %bitcast.11, bf16[96,2048]{1,0:T(8,128)(2,1)S(1)} %times.1.own_product_ref, bf16[144,2048]{1,0:T(8,128)(2,1)S(1)} %get-tuple-element.48.far_present_ref, bf16[480,2048]{1,0:T(8,128)(2,1)S(1)} %get-tuple-element.49.right_ref), custom_call_target="tpu_custom_call" | custom-call | flops 2000000000 | bytes 1048576 | tf_op jit(solution)/shard_map/ahead/pallas_call | solution.py:365
  22.0 0.0 collective-permute-done.4
  22.1 0.8 %collective-permute-start.6 = (bf16[2,48,480]{2,1,0:T(8,128)(2,1)S(1)}, bf16[2,48,480]{2,1,0:T(8,128)(2,1)S(1)}, u32[]{:S(2)}, u32[]{:S(2)}) collective-permute-start(bf16[2,48,480]{2,1,0:T(8,128)(2,1)S(1)} %pad_maximum_fusion.3), channel_id=1, source_target_pairs={{0,4},{1,0},{2,6},{3,2},{4,8},{5,1},{6,10},{7,3},{8,12},{9,5},{10,... | collective-permute-start | bytes 276488 | tf_op jit(solution)/shard_map/ppermute | solution.py:28
  22.9 2.5 %collective-permute-start.5 = (bf16[2,48,480]{2,1,0:T(8,128)(2,1)S(1)}, bf16[2,48,480]{2,1,0:T(8,128)(2,1)S(1)}, u32[]{:S(2)}, u32[]{:S(2)}) collective-permute-start(bf16[2,48,480]{2,1,0:T(8,128)(2,1)S(1)} %fusion), channel_id=1, source_target_pairs={{0,2},{1,0},{2,4},{3,1},{4,6},{5,3},{6,8},{7,5},{8,10},{9,7},{10,1... | collective-permute-start | bytes 276488 | tf_op jit(solution)/shard_map/ppermute | solution.py:28
  25.4 4.5 %collective-permute-done.6.two_ref = bf16[2,48,480]{2,1,0:T(8,128)(2,1)S(1)} collective-permute-done((bf16[2,48,480]{2,1,0:T(8,128)(2,1)S(1)}, bf16[2,48,480]{2,1,0:T(8,128)(2,1)S(1)}, u32[]{:S(2)}, u32[]{:S(2)}) %collective-permute-start.6) | collective-permute-done | bytes 92192 | tf_op jit(solution)/shard_map/ppermute | solution.py:28
  29.9 0.8 %collective-permute-done.5.one_ref = bf16[2,48,480]{2,1,0:T(8,128)(2,1)S(1)} collective-permute-done((bf16[2,48,480]{2,1,0:T(8,128)(2,1)S(1)}, bf16[2,48,480]{2,1,0:T(8,128)(2,1)S(1)}, u32[]{:S(2)}, u32[]{:S(2)}) %collective-permute-start.5) | collective-permute-done | bytes 92192 | tf_op jit(solution)/shard_map/ppermute | solution.py:28
  30.7 0.2 window.1
  30.9 0.1 collective-permute-start.7
  31.0 1.4 %collective-permute-done.7 = f32[48,816]{1,0:T(8,128)S(1)} collective-permute-done((f32[48,816]{1,0:T(8,128)S(1)}, f32[48,816]{1,0:T(8,128)S(1)}, u32[]{:S(2)}, u32[]{:S(2)}) %collective-permute-start.7) | collective-permute-done | bytes 156704 | tf_op jit(solution)/shard_map/ppermute | solution.py:19
  32.4 3.1 %collective-permute-start.9 = (bf16[48,816]{1,0:T(8,128)(2,1)S(1)}, bf16[48,816]{1,0:T(8,128)(2,1)S(1)}, u32[]{:S(2)}, u32[]{:S(2)}) collective-permute-start(bf16[48,816]{1,0:T(8,128)(2,1)S(1)} %add_convert_fusion.own_ref), channel_id=1, source_target_pairs={{0,128},{64,192},{128,0},{192,64},{1,129},{65,193},{129,1},{193,65... | collective-permute-start | bytes 235016 | tf_op jit(solution)/shard_map/ppermute | solution.py:252
  35.5 1.1 %collective-permute-start.8 = (bf16[48,816]{1,0:T(8,128)(2,1)S(1)}, bf16[48,816]{1,0:T(8,128)(2,1)S(1)}, u32[]{:S(2)}, u32[]{:S(2)}) collective-permute-start(bf16[48,816]{1,0:T(8,128)(2,1)S(1)} %add_convert_fusion.own_ref), channel_id=1, source_target_pairs={{0,192},{64,128},{128,64},{192,0},{1,193},{65,129},{129,65},{193,1... | collective-permute-start | bytes 235016 | tf_op jit(solution)/shard_map/ppermute | solution.py:252
  36.7 0.0 collective-permute-start.10
  36.7 1.9 %collective-permute-done.9.two_ref = bf16[48,816]{1,0:T(8,128)(2,1)S(1)} collective-permute-done((bf16[48,816]{1,0:T(8,128)(2,1)S(1)}, bf16[48,816]{1,0:T(8,128)(2,1)S(1)}, u32[]{:S(2)}, u32[]{:S(2)}) %collective-permute-start.9) | collective-permute-done | bytes 78368 | tf_op jit(solution)/shard_map/ppermute | solution.py:252
  38.6 0.8 %first.1.half_hbm = f32[4,48,816]{2,1,0:T(8,128)} custom-call(bf16[48,816]{1,0:T(8,128)(2,1)S(1)} %add_convert_fusion.own_ref, bf16[48,816]{1,0:T(8,128)(2,1)S(1)} %collective-permute-done.9.two_ref), custom_call_target="tpu_custom_call" | custom-call | flops 1000000 | bytes 1048576 | tf_op jit(solution)/shard_map/first/pallas_call | solution.py:401
  39.3 1.9 %collective-permute-done.8.three_ref = bf16[48,816]{1,0:T(8,128)(2,1)S(1)} collective-permute-done((bf16[48,816]{1,0:T(8,128)(2,1)S(1)}, bf16[48,816]{1,0:T(8,128)(2,1)S(1)}, u32[]{:S(2)}, u32[]{:S(2)}) %collective-permute-start.8) | collective-permute-done | bytes 78368 | tf_op jit(solution)/shard_map/ppermute | solution.py:252
  41.2 0.0 collective-permute-done.10.one_ref
  41.2 0.8 %second.1 = f32[4,48,816]{2,1,0:T(8,128)} custom-call(bf16[48,816]{1,0:T(8,128)(2,1)S(1)} %collective-permute-done.8.three_ref, bf16[48,816]{1,0:T(8,128)(2,1)S(1)} %collective-permute-done.10.one_ref, f32[4,48,816]{2,1,0:T(8,128)} %first.1.half_hbm), custom_call_target="tpu_custom_call", output_to_operand_aliasing={{}: (2, {})} | custom-call | tf_op jit(solution)/shard_map/second/pallas_call | solution.py:412
  (14 shorter events, 0.2 us)
Async XLA Ops:
  1.3 1.6 %collective-permute-start = (bf16[5,4,48,128]{3,2,1,0:T(8,128)(2,1)S(1)}, bf16[5,4,48,128]{3,2,1,0:T(8,128)(2,1)S(1)}, u32[]{:S(2)}, u32[]{:S(2)}) collective-permute-start(bf16[5,4,48,128]{3,2,1,0:T(8,128)(2,1)S(1)} %get-tuple-element.33), channel_id=1, source_target_pairs={{0,1},{1,0},{2,3},{3,2},{4,5},{5,4},{6,7},{7,6},{8,9},{9,8},{10,11... | collective-permute-start | bytes 737288 | tf_op jit(solution)/shard_map/ppermute | solution.py:19
  1.4 7.9 %copy-start = (bf16[1,1,2048,2048]{3,2,1,0:T(8,128)(2,1)S(1)}, bf16[1,1,2048,2048]{3,2,1,0:T(8,128)(2,1)}, u32[]{:S(2)}) copy-start(bf16[1,1,2048,2048]{3,2,1,0:T(8,128)(2,1)} %param.6) | copy-start | bytes 25165828
  2.9 9.8 %collective-permute-start.1 = (bf16[3,4,48,128]{3,2,1,0:T(8,128)(2,1)S(1)}, bf16[3,4,48,128]{3,2,1,0:T(8,128)(2,1)S(1)}, u32[]{:S(2)}, u32[]{:S(2)}) collective-permute-start(bf16[3,4,48,128]{3,2,1,0:T(8,128)(2,1)S(1)} %pad_maximum_fusion.1), channel_id=1, source_target_pairs={{0,4},{1,0},{2,6},{3,2},{4,8},{5,1},{6,10},{7,3},{8,12},{9,5},{10,... | collective-permute-start | bytes 442376 | tf_op jit(solution)/shard_map/ppermute | solution.py:28
  6.3 9.5 %collective-permute-start.2 = (bf16[4,4,48,128]{3,2,1,0:T(8,128)(2,1)S(1)}, bf16[4,4,48,128]{3,2,1,0:T(8,128)(2,1)S(1)}, u32[]{:S(2)}, u32[]{:S(2)}) collective-permute-start(bf16[4,4,48,128]{3,2,1,0:T(8,128)(2,1)S(1)} %pad_maximum_fusion), channel_id=1, source_target_pairs={{0,2},{1,0},{2,4},{3,1},{4,6},{5,3},{6,8},{7,5},{8,10},{9,7},{10,1... | collective-permute-start | bytes 589832 | tf_op jit(solution)/shard_map/ppermute | solution.py:28
  15.9 2.2 %collective-permute-start.3 = (bf16[3,4,48,128]{3,2,1,0:T(8,128)(2,1)S(1)}, bf16[3,4,48,128]{3,2,1,0:T(8,128)(2,1)S(1)}, u32[]{:S(2)}, u32[]{:S(2)}) collective-permute-start(bf16[3,4,48,128]{3,2,1,0:T(8,128)(2,1)S(1)} %pad_maximum_fusion.2), channel_id=1, source_target_pairs={{0,1},{1,0},{2,3},{3,2},{4,5},{5,4},{6,7},{7,6},{8,9},{9,8},{10,11... | collective-permute-start | bytes 442376 | tf_op jit(solution)/shard_map/ppermute | solution.py:19
  19.4 2.5 %collective-permute-start.4 = (bf16[4,48,480]{2,1,0:T(8,128)(2,1)S(1)}, bf16[4,48,480]{2,1,0:T(8,128)(2,1)S(1)}, u32[]{:S(2)}, u32[]{:S(2)}) collective-permute-start(bf16[4,48,480]{2,1,0:T(8,128)(2,1)S(1)} %get-tuple-element.51), channel_id=1, source_target_pairs={{0,1},{1,0},{2,3},{3,2},{4,5},{5,4},{6,7},{7,6},{8,9},{9,8},{10,11... | collective-permute-start | bytes 552968 | tf_op jit(solution)/shard_map/ppermute | solution.py:19
  22.1 7.8 %collective-permute-start.6 = (bf16[2,48,480]{2,1,0:T(8,128)(2,1)S(1)}, bf16[2,48,480]{2,1,0:T(8,128)(2,1)S(1)}, u32[]{:S(2)}, u32[]{:S(2)}) collective-permute-start(bf16[2,48,480]{2,1,0:T(8,128)(2,1)S(1)} %pad_maximum_fusion.3), channel_id=1, source_target_pairs={{0,4},{1,0},{2,6},{3,2},{4,8},{5,1},{6,10},{7,3},{8,12},{9,5},{10,... | collective-permute-start | bytes 276488 | tf_op jit(solution)/shard_map/ppermute | solution.py:28
  22.9 7.8 %collective-permute-start.5 = (bf16[2,48,480]{2,1,0:T(8,128)(2,1)S(1)}, bf16[2,48,480]{2,1,0:T(8,128)(2,1)S(1)}, u32[]{:S(2)}, u32[]{:S(2)}) collective-permute-start(bf16[2,48,480]{2,1,0:T(8,128)(2,1)S(1)} %fusion), channel_id=1, source_target_pairs={{0,2},{1,0},{2,4},{3,1},{4,6},{5,3},{6,8},{7,5},{8,10},{9,7},{10,1... | collective-permute-start | bytes 276488 | tf_op jit(solution)/shard_map/ppermute | solution.py:28
  30.9 1.5 %collective-permute-start.7 = (f32[48,816]{1,0:T(8,128)S(1)}, f32[48,816]{1,0:T(8,128)S(1)}, u32[]{:S(2)}, u32[]{:S(2)}) collective-permute-start(f32[48,816]{1,0:T(8,128)S(1)} %get-tuple-element.56), channel_id=1, source_target_pairs={{0,1},{1,0},{2,3},{3,2},{4,5},{5,4},{6,7},{7,6},{8,9},{9,8},{10,11... | collective-permute-start | bytes 470024 | tf_op jit(solution)/shard_map/ppermute | solution.py:19
  32.4 6.2 %collective-permute-start.9 = (bf16[48,816]{1,0:T(8,128)(2,1)S(1)}, bf16[48,816]{1,0:T(8,128)(2,1)S(1)}, u32[]{:S(2)}, u32[]{:S(2)}) collective-permute-start(bf16[48,816]{1,0:T(8,128)(2,1)S(1)} %add_convert_fusion.own_ref), channel_id=1, source_target_pairs={{0,128},{64,192},{128,0},{192,64},{1,129},{65,193},{129,1},{193,65... | collective-permute-start | bytes 235016 | tf_op jit(solution)/shard_map/ppermute | solution.py:252
  35.5 5.7 %collective-permute-start.8 = (bf16[48,816]{1,0:T(8,128)(2,1)S(1)}, bf16[48,816]{1,0:T(8,128)(2,1)S(1)}, u32[]{:S(2)}, u32[]{:S(2)}) collective-permute-start(bf16[48,816]{1,0:T(8,128)(2,1)S(1)} %add_convert_fusion.own_ref), channel_id=1, source_target_pairs={{0,192},{64,128},{128,64},{192,0},{1,193},{65,129},{129,65},{193,1... | collective-permute-start | bytes 235016 | tf_op jit(solution)/shard_map/ppermute | solution.py:252
  36.7 4.6 %collective-permute-start.10 = (bf16[48,816]{1,0:T(8,128)(2,1)S(1)}, bf16[48,816]{1,0:T(8,128)(2,1)S(1)}, u32[]{:S(2)}, u32[]{:S(2)}) collective-permute-start(bf16[48,816]{1,0:T(8,128)(2,1)S(1)} %add_convert_fusion.own_ref), channel_id=1, source_target_pairs={{0,64},{64,0},{128,192},{192,128},{1,65},{65,1},{129,193},{193,129... | collective-permute-start | bytes 235016 | tf_op jit(solution)/shard_map/ppermute | solution.py:252
